TPU v7x, 32 devices: a whole 2x2x4 slice. The times are simulated.
32 devices in a mesh: lat: 4 (over z), lon: 4 (over y, core), tm: 2 (over x).
Axes of the slice: x: 2, y: 2, z: 4, core: 2. Of those that a mesh axis runs over, the one named last changes fastest.
Arguments:
- class_ids: int32 [1, 32, 512], P(None, 'lat', 'lon'), may hold values from 0 to 7
- coef_table: float32 [8], replicated, may hold values from 0.2 to 2
- land_mask: int32 [1, 32, 512], P(None, 'lat', 'lon'), may hold values 0 or 1
- cross_cov: float32 [3, 3], replicated, may hold values from -0.4 to 2, as said below
- time_metric: float32 [2, 2], replicated, may hold values from -1.2 to 2.2, as said below
- obs_values: float32 [2048, 3, 128], P(('lat', 'lon', 'tm')), may hold values from -6 to 6
- obs_weight: float32 [2048, 128], P(('lat', 'lon', 'tm')), may hold values from 0.3 to 3
- obs_cells: int32 [2048, 128], P(('lat', 'lon', 'tm')), may hold values from 0 to 1023
- obs_count: int32 [2048], P(('lat', 'lon', 'tm')), may hold values from 1 to 128
- block_owner: int32 [2048, 1], P(('lat', 'lon', 'tm')), may hold values from 0 to 15; in each aligned block of 64 rows (0 to 63, 64 to 127, ...) at most 8 rows name the same one
Outputs:
- solution: float32 [2, 3, 1, 32, 512], P('tm', None, None, 'lat', 'lon')
- residual: float32 [2, 3, 1, 32, 512], P('tm', None, None, 'lat', 'lon')
Inputs may be any that keep to these rules, and one draw needn't show every extreme that they name: `block_owner`: the blocks of one device name each owner at most 8 times, a bound that some block reaches. `obs_count`: records at or after a block's count are padding. `obs_cells`: a cell of the owner's tile flattened over months, levels, rows and columns in this order. `time_metric`: symmetric positive definite. `cross_cov`: symmetric positive definite.
All inputs are finite; a program needn't handle non-finite values. No bound on the sum of `land_mask` on one device may be relied on, other than what follows from the above.
Results may differ from a plain program's by a relative error of at most 0.0003.
Values sent between devices are 32-bit elements; how exact they have to be, the bound alone decides.
No kernel may reach another device: no remote copies, remote signals or barrier semaphores. Data moves between devices by JAX's collectives and lax.ppermute only.
A program may use at most 64 MiB of HBM per device.

v0:
```python
import jax
import jax.numpy as jnp
from jax import lax
from jax.sharding import PartitionSpec as P

NV = 3
MD = 1
LEV = 1
CLAT = 8
CLON = 128
ITERS = 2


HIGHEST = lax.Precision.HIGHEST


def extended(x, sides, width, wrap):
    for axis, dim in sides:
        count, length = (lax.axis_size(axis), x.shape[dim])
        up = [(i, (i + 1) % count) for i in range(count if wrap else count - 1)]
        down = [(j, i) for i, j in up]
        last = lax.slice_in_dim(x, length - width, length, axis=dim)
        first = lax.slice_in_dim(x, 0, width, axis=dim)
        before = lax.ppermute(last, axis, up)
        after = lax.ppermute(first, axis, down)
        x = jnp.concatenate([before, x, after], axis=dim)
    return x


def coefficients(class_ids, coef_table):
    classes = jnp.arange(coef_table.shape[0], dtype=jnp.int32)
    chosen = jnp.where(
        class_ids[None] == classes[:, None, None, None],
        coef_table[:, None, None, None],
        jnp.float32(0.0),
    )
    return jnp.sum(chosen, axis=0)


def vertical_terms(masked):
    diff_lev = masked[:, :, 1:] - masked[:, :, :-1]
    zero_layer = jnp.zeros_like(masked)
    return jnp.concatenate([diff_lev, zero_layer], axis=2) - jnp.concatenate(
        [zero_layer, diff_lev], axis=2
    )


def squares(current):
    return lax.psum(jnp.sum(current * current), ("lat", "lon", "tm"))


def group_size(block_count, slot_count):
    best = 1
    for candidate in range(1, block_count + 1):
        if block_count % candidate == 0 and candidate * slot_count <= 4096:
            best = candidate
    return best


def cell_statistics(stat_rows, recv_cells, row_total, col_total):
    block_count, stat_count, slot_count = stat_rows.shape
    per_group = group_size(block_count, slot_count)
    group_count = block_count // per_group
    width = per_group * slot_count
    grouped_stats = (
        stat_rows.reshape(group_count, per_group, stat_count, slot_count)
        .transpose(0, 2, 1, 3)
        .reshape(group_count, stat_count, width)
    )
    grouped_cells = recv_cells.reshape(group_count, width)
    row_ids = jnp.arange(row_total, dtype=jnp.int32)
    col_ids = jnp.arange(col_total, dtype=jnp.int32)

    def accumulate(total, inputs):
        stats_part, cells_part = inputs
        row_part = cells_part // col_total
        col_part = cells_part % col_total
        row_hot = jnp.where(
            row_part[None, :] == row_ids[:, None], jnp.float32(1.0), jnp.float32(0.0)
        )
        weighted = (stats_part[:, None, :] * row_hot[None, :, :]).reshape(
            stat_count * row_total, width
        )
        col_hot = jnp.where(
            col_part[:, None] == col_ids[None, :], jnp.float32(1.0), jnp.float32(0.0)
        )
        return (
            total
            + jnp.dot(weighted, col_hot, precision=HIGHEST, preferred_element_type=jnp.float32),
            None,
        )

    start = jnp.zeros((stat_count * row_total, col_total), jnp.float32)
    result, unused = lax.scan(accumulate, start, (grouped_stats, grouped_cells))
    return result.reshape(stat_count, row_total, col_total)


def per_device(
    class_ids,
    coef_table,
    land_mask,
    cross_cov,
    time_metric,
    obs_values,
    obs_weight,
    obs_cells,
    obs_count,
    block_owner,
):
    diffusivity = coefficients(class_ids, coef_table)
    padded_coef = extended(diffusivity, (("lat", 1),), 1, False)
    face_lat = 0.5 * (padded_coef[:, :-1] + padded_coef[:, 1:])
    wrapped_coef = extended(diffusivity, (("lon", 2),), 1, True)
    face_lon = 0.5 * (wrapped_coef[..., :-1] + wrapped_coef[..., 1:])
    sea_mask = land_mask.astype(jnp.float32)[None, None]
    owner_total = lax.axis_size("lat") * lax.axis_size("lon")
    block_total = block_owner.shape[0]
    capacity = max(2, 2 * block_total // owner_total)
    owner_ids = block_owner[:, 0]
    block_index = jnp.arange(block_total, dtype=jnp.int32)
    same_owner = owner_ids[:, None] == owner_ids[None, :]
    earlier_mask = block_index[:, None] < block_index[None, :]
    slot_rank = jnp.sum(jnp.where(same_owner & earlier_mask, 1, 0), axis=0).astype(jnp.int32)
    destination = owner_ids * capacity + slot_rank
    slot_ids = jnp.arange(owner_total * capacity, dtype=jnp.int32)
    slot_hits = destination[None, :] == slot_ids[:, None]
    source_block = jnp.sum(jnp.where(slot_hits, block_index[None, :], 0), axis=1)
    filled = jnp.any(slot_hits, axis=1)
    send_values = jnp.take(obs_values, source_block, axis=0)
    send_weight = jnp.take(obs_weight, source_block, axis=0)
    send_cells = jnp.take(obs_cells, source_block, axis=0)
    send_count = jnp.where(filled, jnp.take(obs_count, source_block, axis=0), 0)
    recv_values, recv_weight, recv_cells, recv_count = (
        lax.all_to_all(send_values, ("lat", "lon"), split_axis=0, concat_axis=0, tiled=True),
        lax.all_to_all(send_weight, ("lat", "lon"), split_axis=0, concat_axis=0, tiled=True),
        lax.all_to_all(send_cells, ("lat", "lon"), split_axis=0, concat_axis=0, tiled=True),
        lax.all_to_all(send_count, ("lat", "lon"), split_axis=0, concat_axis=0, tiled=True),
    )
    slot_count = recv_weight.shape[1]
    live_mask = jnp.arange(slot_count, dtype=jnp.int32)[None, :] < recv_count[:, None]
    live_weight = jnp.where(live_mask, recv_weight, jnp.float32(0.0))
    stat_rows = jnp.concatenate(
        [live_weight[:, None, :], recv_values * live_weight[:, None, :]], axis=1
    )
    row_total = MD * LEV * CLAT
    per_cell = cell_statistics(stat_rows, recv_cells, row_total, CLON)
    obs_diag = per_cell[0].reshape(MD, 1, LEV, CLAT, CLON)
    right_side = per_cell[1:].reshape(NV, MD, LEV, CLAT, CLON).transpose(1, 0, 2, 3, 4) * sea_mask
    solution = jnp.zeros_like(right_side)
    residual = right_side
    direction = right_side
    norm_now = squares(residual)
    for iteration in range(ITERS):
        masked = direction * sea_mask
        padded_lat = extended(masked, (("lat", 3),), 1, False)
        flux_lat = face_lat * (padded_lat[:, :, :, 1:] - padded_lat[:, :, :, :-1])
        wrapped = extended(masked, (("lon", 4),), 1, True)
        flux_lon = face_lon * (wrapped[..., 1:] - wrapped[..., :-1])
        spatial = (
            flux_lat[:, :, :, 1:]
            - flux_lat[:, :, :, :-1]
            + flux_lon[..., 1:]
            - flux_lon[..., :-1]
            + vertical_terms(masked)
        )
        mixed_vars = jnp.einsum("vw,mwlij->mvlij", cross_cov, masked, precision=HIGHEST)
        local_cols = lax.dynamic_slice_in_dim(time_metric, lax.axis_index("tm") * MD, MD, 1)
        time_term = lax.psum_scatter(
            jnp.tensordot(local_cols, masked, axes=(1, 0), precision=HIGHEST),
            "tm",
            scatter_dimension=0,
            tiled=True,
        )
        combined = mixed_vars + time_term - spatial + obs_diag * masked
        image_field = sea_mask * combined + (1.0 - sea_mask) * direction
        step_size = norm_now / lax.psum(jnp.sum(direction * image_field), ("lat", "lon", "tm"))
        solution = solution + step_size * direction
        residual = residual - step_size * image_field
        norm_next = squares(residual)
        direction = residual + norm_next / norm_now * direction
        norm_now = norm_next
    return (solution, residual)


def solution(mesh):
    in_specs = (
        P(None, "lat", "lon"),
        P(),
        P(None, "lat", "lon"),
        P(),
        P(),
        P(("lat", "lon", "tm"), None, None),
        P(("lat", "lon", "tm"), None),
        P(("lat", "lon", "tm"), None),
        P(("lat", "lon", "tm")),
        P(("lat", "lon", "tm"), None),
    )
    out_specs = (P("tm", None, None, "lat", "lon"), P("tm", None, None, "lat", "lon"))
    return jax.shard_map(
        per_device, mesh=mesh, in_specs=in_specs, out_specs=out_specs, check_vma=False
    )
```

profile of v0, /device:TPU:0, one launch (start us, length us, event | category | flops | bytes accessed | tf_op | source)
XLA Modules:
  0.0 244.3 jit_solution(1620441244721728166)
XLA Ops:
  11.0 7.4 %all-to-all-start = ((s32[16,8,1]{1,2,0:T(1,128)}), s32[16,8,1]{1,2,0:T(1,128)S(1)}, u32[]{:S(2)}, u32[]{:S(2)}) async-start(s32[16,8,1]{1,2,0:T(1,128)} %bitcast.3), calls=%async_computation | async-start | bytes 16384 | tf_op jit(solution)/shard_map/all_to_all | solution.py:137
  18.5 3.8 %collective-permute-start = (f32[1,1,128]{2,1,0:T(1,128)S(1)}, f32[1,1,128]{2,1,0:T(1,128)S(1)}, u32[]{:S(2)}, u32[]{:S(2)}) collective-permute-start(f32[1,1,128]{2,1,0:T(1,128)S(1)} %get-tuple-element.141), channel_id=1, source_target_pairs={{0,8},{8,16},{16,24},{1,9},{9,17},{17,25},{2,10},{10,18},{18,26},{... | collective-permute-start | bytes 1544 | tf_op jit(solution)/shard_map/ppermute | solution.py:24
  23.8 1.7 collective-permute-start.5
  30.4 6.7 %all-to-all-start.3 = ((s32[16,8,128]{2,1,0:T(8,128)}), s32[16,8,128]{2,1,0:T(8,128)S(1)}, u32[]{:S(2)}, u32[]{:S(2)}) async-start(s32[16,8,128]{2,1,0:T(8,128)} %bitcast_select_fusion), calls=%async_computation.3 | async-start | bytes 131072 | tf_op jit(solution)/shard_map/all_to_all | solution.py:136
  37.1 6.9 %all-to-all-done.3 = s32[16,8,128]{2,1,0:T(8,128)S(1)} async-done(((s32[16,8,128]{2,1,0:T(8,128)}), s32[16,8,128]{2,1,0:T(8,128)S(1)}, u32[]{:S(2)}, u32[]{:S(2)}) %all-to-all-start.3) | async-done | bytes 65568 | tf_op jit(solution)/shard_map/all_to_all | solution.py:136
  44.0 3.5 %all-to-all-start.1 = ((f32[16,8,128]{2,1,0:T(8,128)}), f32[16,8,128]{2,1,0:T(8,128)S(1)}, u32[]{:S(2)}, u32[]{:S(2)}) async-start(f32[16,8,128]{2,1,0:T(8,128)} %bitcast_select_fusion.2), calls=%async_computation.1 | async-start | bytes 131072 | tf_op jit(solution)/shard_map/all_to_all | solution.py:135
  49.0 5.3 %all-to-all-done.1 = f32[16,8,128]{2,1,0:T(8,128)S(1)} async-done(((f32[16,8,128]{2,1,0:T(8,128)}), f32[16,8,128]{2,1,0:T(8,128)S(1)}, u32[]{:S(2)}, u32[]{:S(2)}) %all-to-all-start.1) | async-done | bytes 65568 | tf_op jit(solution)/shard_map/all_to_all | solution.py:135
  54.4 3.5 %all-to-all-start.2 = ((f32[128,3,128]{2,1,0:T(4,128)}), f32[128,3,128]{2,1,0:T(4,128)S(1)}, u32[]{:S(2)}, u32[]{:S(2)}) async-start(f32[128,3,128]{2,1,0:T(4,128)} %copy.64), calls=%async_computation.2 | async-start | bytes 524288 | tf_op jit(solution)/shard_map/all_to_all | solution.py:134
  58.3 9.7 %all-to-all-done.2 = f32[128,3,128]{2,1,0:T(4,128)S(1)} async-done(((f32[128,3,128]{2,1,0:T(4,128)}), f32[128,3,128]{2,1,0:T(4,128)S(1)}, u32[]{:S(2)}, u32[]{:S(2)}) %all-to-all-start.2) | async-done | bytes 196640 | tf_op jit(solution)/shard_map/all_to_all | solution.py:134
  68.1 7.0 %while.13 = (s32[]{:T(128)}, f32[32,128]{1,0:T(8,128)S(1)}, f32[4,4,4096]{2,1,0:T(4,128)S(1)}, s32[4,4096]{1,0:T(4,128)S(1)}, s32[]{:T(128)}, /*index=5*/s32[]{:T(128)}) while((s32[]{:T(128)}, f32[32,128]{1,0:T(8,128)S(1)}, f32[4,4,4096]{2,1,0:T(4,128)S(1)}, s32[4,4096]{1,0:T(4,128)S(1)}, s32[]{:T(128)}, /*index=5*/s32[]{:T(128)}) %tuple.55), condition=%wide.region_4.5_spmd.clone, body=%wide.region_3.4_spmd.clone.sunk | while | flops 202686464 | bytes 606295 | solution.py:94
  68.3 1.6 fusion.63
  70.1 1.6 fusion.63
  71.8 1.6 fusion.63
  73.6 1.6 fusion.63
  77.1 4.5 %collective-permute-start.3 = (f32[1,3,1,1,128]{4,1,3,2,0:T(4,128)S(1)}, f32[1,3,1,1,128]{4,1,3,2,0:T(4,128)S(1)}, u32[]{:S(2)}, u32[]{:S(2)}) collective-permute-start(f32[1,3,1,1,128]{4,1,3,2,0:T(4,128)S(1)} %get-tuple-element.136), channel_id=1, source_target_pairs={{0,8},{8,16},{16,24},{1,9},{9,17},{17,25},{2,10},{10,18},{18,26},{... | collective-permute-start | bytes 4616 | tf_op jit(solution)/shard_map/ppermute | solution.py:24
  83.2 1.8 collective-permute-done.7
  85.1 6.3 %reduce-scatter.7.cloned.1.call-done = f32[1,3,1,8,128]{4,3,2,1,0:T(8,128)} async-done(((f32[2,3,1,8,128]{4,3,2,1,0:T(8,128)}), f32[1,3,1,8,128]{4,3,2,1,0:T(8,128)}) %reduce-scatter.7.cloned.1.call-update) | async-done | bytes 12304
  92.9 39.6 %all-reduce.2 = (f32[]{:T(128)}, f32[]{:T(128)}) all-reduce(f32[]{:T(128)} %get-tuple-element.126, f32[]{:T(128)} %get-tuple-element.144), channel_id=1, replica_groups=mesh['lat'=4,'lon'=4,'tm'=2] {'lat','lon','tm'}, use_global_device_ids=true, to_apply=%region_6.7 | all-reduce | flops 2 | bytes 16 | tf_op jit(solution)/shard_map/psum | solution.py:49
  134.4 41.4 %psum.30 = f32[]{:T(128)} all-reduce(f32[]{:T(128)} %multiply_reduce_fusion.1), channel_id=1, replica_groups=mesh['lat'=4,'lon'=4,'tm'=2] {'lat','lon','tm'}, use_global_device_ids=true, to_apply=%region_12.13 | all-reduce | flops 1 | bytes 8 | tf_op jit(solution)/shard_map/psum | solution.py:49
  178.6 4.5 %collective-permute-start.9 = (f32[1,3,1,1,128]{4,1,3,2,0:T(4,128)S(1)}, f32[1,3,1,1,128]{4,1,3,2,0:T(4,128)S(1)}, u32[]{:S(2)}, u32[]{:S(2)}) collective-permute-start(f32[1,3,1,1,128]{4,1,3,2,0:T(4,128)S(1)} %get-tuple-element.130), channel_id=1, source_target_pairs={{0,8},{8,16},{16,24},{1,9},{9,17},{17,25},{2,10},{10,18},{18,26},{... | collective-permute-start | bytes 4616 | tf_op jit(solution)/shard_map/ppermute | solution.py:24
  184.6 2.6 %collective-permute-done.11 = f32[1,3,1,8,1]{4,1,3,2,0:T(4,128)S(1)} collective-permute-done((f32[1,3,1,8,1]{4,1,3,2,0:T(4,128)S(1)}, f32[1,3,1,8,1]{4,1,3,2,0:T(4,128)S(1)}, u32[]{:S(2)}, u32[]{:S(2)}) %collective-permute-start.11) | collective-permute-done | bytes 128 | tf_op jit(solution)/shard_map/ppermute | solution.py:24
  187.3 6.6 %reduce-scatter.9.cloned.1.call-done = f32[1,3,1,8,128]{4,3,2,1,0:T(8,128)} async-done(((f32[2,3,1,8,128]{4,3,2,1,0:T(8,128)}), f32[1,3,1,8,128]{4,3,2,1,0:T(8,128)}) %reduce-scatter.9.cloned.1.call-update) | async-done | bytes 12304
  193.8 1.5 multiply_reduce_fusion
  195.3 39.5 %psum.31 = f32[]{:T(128)} all-reduce(f32[]{:T(128)} %get-tuple-element.146), channel_id=1, replica_groups=mesh['lat'=4,'lon'=4,'tm'=2] {'lat','lon','tm'}, use_global_device_ids=true, to_apply=%region_15.16 | all-reduce | flops 1 | bytes 8 | tf_op jit(solution)/shard_map/psum | solution.py:176
  (118 shorter events, 22.4 us)
Async XLA Ops:
  7.2 19.1 %copy-start = (f32[64,3,128]{2,0,1:T(8,128)S(1)}, f32[64,3,128]{2,0,1:T(8,128)}, u32[]{:S(2)}) copy-start(f32[64,3,128]{2,0,1:T(8,128)} %param.17) | copy-start | bytes 294916
  7.2 1.8 copy-start.1
  9.0 9.5 %copy-start.5 = (s32[1,8,128]{2,1,0:T(8,128)S(1)}, s32[1,8,128]{2,1,0:T(8,128)}, u32[]{:S(2)}) copy-start(s32[1,8,128]{2,1,0:T(8,128)} %param.12) | copy-start | bytes 12292
  9.0 9.5 %copy-start.7 = (f32[8]{0:T(128)S(1)}, f32[8]{0:T(128)}, u32[]{:S(2)}) copy-start(f32[8]{0:T(128)} %param.13) | copy-start | bytes 100
  9.0 16.6 %copy-start.2 = (f32[64,128]{1,0:T(8,128)S(1)}, f32[64,128]{1,0:T(8,128)}, u32[]{:S(2)}) copy-start(f32[64,128]{1,0:T(8,128)} %param.18) | copy-start | bytes 98308
  11.0 19.3 %all-to-all-start = ((s32[16,8,1]{1,2,0:T(1,128)}), s32[16,8,1]{1,2,0:T(1,128)S(1)}, u32[]{:S(2)}, u32[]{:S(2)}) async-start(s32[16,8,1]{1,2,0:T(1,128)} %bitcast.3), calls=%async_computation | async-start | bytes 16384 | tf_op jit(solution)/shard_map/all_to_all | solution.py:137
  18.5 29.1 %collective-permute-start = (f32[1,1,128]{2,1,0:T(1,128)S(1)}, f32[1,1,128]{2,1,0:T(1,128)S(1)}, u32[]{:S(2)}, u32[]{:S(2)}) collective-permute-start(f32[1,1,128]{2,1,0:T(1,128)S(1)} %get-tuple-element.141), channel_id=1, source_target_pairs={{0,8},{8,16},{16,24},{1,9},{9,17},{17,25},{2,10},{10,18},{18,26},{... | collective-permute-start | bytes 1544 | tf_op jit(solution)/shard_map/ppermute | solution.py:24
  22.4 25.2 %collective-permute-start.1 = (f32[1,1,128]{2,1,0:T(1,128)S(1)}, f32[1,1,128]{2,1,0:T(1,128)S(1)}, u32[]{:S(2)}, u32[]{:S(2)}) collective-permute-start(f32[1,1,128]{2,1,0:T(1,128)S(1)} %get-tuple-element.140), channel_id=1, source_target_pairs={{8,0},{16,8},{24,16},{9,1},{17,9},{25,17},{10,2},{18,10},{26,18},{... | collective-permute-start | bytes 1544 | tf_op jit(solution)/shard_map/ppermute | solution.py:25
  23.8 23.8 %collective-permute-start.4 = (f32[1,8,1]{2,1,0:T(8,128)S(1)}, f32[1,8,1]{2,1,0:T(8,128)S(1)}, u32[]{:S(2)}, u32[]{:S(2)}) collective-permute-start(f32[1,8,1]{2,1,0:T(8,128)S(1)} %get-tuple-element.143), channel_id=1, source_target_pairs={{0,2},{2,4},{4,6},{6,0},{1,3},{3,5},{5,7},{7,1},{8,10},{10,12},{12... | collective-permute-start | bytes 104 | tf_op jit(solution)/shard_map/ppermute | solution.py:24
  23.8 23.8 %collective-permute-start.5 = (f32[1,8,1]{2,1,0:T(8,128)S(1)}, f32[1,8,1]{2,1,0:T(8,128)S(1)}, u32[]{:S(2)}, u32[]{:S(2)}) collective-permute-start(f32[1,8,1]{2,1,0:T(8,128)S(1)} %get-tuple-element.142), channel_id=1, source_target_pairs={{2,0},{4,2},{6,4},{0,6},{3,1},{5,3},{7,5},{1,7},{10,8},{12,10},{14... | collective-permute-start | bytes 104 | tf_op jit(solution)/shard_map/ppermute | solution.py:25
  30.4 13.6 %all-to-all-start.3 = ((s32[16,8,128]{2,1,0:T(8,128)}), s32[16,8,128]{2,1,0:T(8,128)S(1)}, u32[]{:S(2)}, u32[]{:S(2)}) async-start(s32[16,8,128]{2,1,0:T(8,128)} %bitcast_select_fusion), calls=%async_computation.3 | async-start | bytes 131072 | tf_op jit(solution)/shard_map/all_to_all | solution.py:136
  44.0 10.4 %all-to-all-start.1 = ((f32[16,8,128]{2,1,0:T(8,128)}), f32[16,8,128]{2,1,0:T(8,128)S(1)}, u32[]{:S(2)}, u32[]{:S(2)}) async-start(f32[16,8,128]{2,1,0:T(8,128)} %bitcast_select_fusion.2), calls=%async_computation.1 | async-start | bytes 131072 | tf_op jit(solution)/shard_map/all_to_all | solution.py:135
  54.4 13.5 %all-to-all-start.2 = ((f32[128,3,128]{2,1,0:T(4,128)}), f32[128,3,128]{2,1,0:T(4,128)S(1)}, u32[]{:S(2)}, u32[]{:S(2)}) async-start(f32[128,3,128]{2,1,0:T(4,128)} %copy.64), calls=%async_computation.2 | async-start | bytes 524288 | tf_op jit(solution)/shard_map/all_to_all | solution.py:134
  57.9 33.5 %reduce-scatter.7.cloned.1.call-start = ((), (), s32[]{:S(2)}) async-start(), calls=%async_computation.6 | async-start | bytes 36864
  75.1 16.3 %copy-start.8 = (f32[3,3]{1,0:T(4,128)S(1)}, f32[3,3]{1,0:T(4,128)}, u32[]{:S(2)}) copy-start(f32[3,3]{1,0:T(4,128)} %param.15) | copy-start | bytes 112
  75.8 9.2 %collective-permute-start.2 = (f32[1,3,1,1,128]{4,1,3,2,0:T(4,128)S(1)}, f32[1,3,1,1,128]{4,1,3,2,0:T(4,128)S(1)}, u32[]{:S(2)}, u32[]{:S(2)}) collective-permute-start(f32[1,3,1,1,128]{4,1,3,2,0:T(4,128)S(1)} %get-tuple-element.137), channel_id=1, source_target_pairs={{8,0},{16,8},{24,16},{9,1},{17,9},{25,17},{10,2},{18,10},{26,18},{... | collective-permute-start | bytes 4616 | tf_op jit(solution)/shard_map/ppermute | solution.py:25
  77.1 8.0 %collective-permute-start.3 = (f32[1,3,1,1,128]{4,1,3,2,0:T(4,128)S(1)}, f32[1,3,1,1,128]{4,1,3,2,0:T(4,128)S(1)}, u32[]{:S(2)}, u32[]{:S(2)}) collective-permute-start(f32[1,3,1,1,128]{4,1,3,2,0:T(4,128)S(1)} %get-tuple-element.136), channel_id=1, source_target_pairs={{0,8},{8,16},{16,24},{1,9},{9,17},{17,25},{2,10},{10,18},{18,26},{... | collective-permute-start | bytes 4616 | tf_op jit(solution)/shard_map/ppermute | solution.py:24
  81.7 1.5 collective-permute-start.6
  81.8 3.2 %collective-permute-start.7 = (f32[1,3,1,8,1]{4,1,3,2,0:T(4,128)S(1)}, f32[1,3,1,8,1]{4,1,3,2,0:T(4,128)S(1)}, u32[]{:S(2)}, u32[]{:S(2)}) collective-permute-start(f32[1,3,1,8,1]{4,1,3,2,0:T(4,128)S(1)} %get-tuple-element.138), channel_id=1, source_target_pairs={{0,2},{2,4},{4,6},{6,0},{1,3},{3,5},{5,7},{7,1},{8,10},{10,12},{12... | collective-permute-start | bytes 296 | tf_op jit(solution)/shard_map/ppermute | solution.py:24
  83.0 110.9 %reduce-scatter.9.cloned.1.call-start = ((), (), s32[]{:S(2)}) async-start(), calls=%async_computation.7 | async-start | bytes 36864
  177.3 10.0 %collective-permute-start.8 = (f32[1,3,1,1,128]{4,1,3,2,0:T(4,128)S(1)}, f32[1,3,1,1,128]{4,1,3,2,0:T(4,128)S(1)}, u32[]{:S(2)}, u32[]{:S(2)}) collective-permute-start(f32[1,3,1,1,128]{4,1,3,2,0:T(4,128)S(1)} %get-tuple-element.131), channel_id=1, source_target_pairs={{8,0},{16,8},{24,16},{9,1},{17,9},{25,17},{10,2},{18,10},{26,18},{... | collective-permute-start | bytes 4616 | tf_op jit(solution)/shard_map/ppermute | solution.py:25
  178.6 8.7 %collective-permute-start.9 = (f32[1,3,1,1,128]{4,1,3,2,0:T(4,128)S(1)}, f32[1,3,1,1,128]{4,1,3,2,0:T(4,128)S(1)}, u32[]{:S(2)}, u32[]{:S(2)}) collective-permute-start(f32[1,3,1,1,128]{4,1,3,2,0:T(4,128)S(1)} %get-tuple-element.130), channel_id=1, source_target_pairs={{0,8},{8,16},{16,24},{1,9},{9,17},{17,25},{2,10},{10,18},{18,26},{... | collective-permute-start | bytes 4616 | tf_op jit(solution)/shard_map/ppermute | solution.py:24
  183.1 1.5 collective-permute-start.10
  183.2 4.0 %collective-permute-start.11 = (f32[1,3,1,8,1]{4,1,3,2,0:T(4,128)S(1)}, f32[1,3,1,8,1]{4,1,3,2,0:T(4,128)S(1)}, u32[]{:S(2)}, u32[]{:S(2)}) collective-permute-start(f32[1,3,1,8,1]{4,1,3,2,0:T(4,128)S(1)} %get-tuple-element.132), channel_id=1, source_target_pairs={{0,2},{2,4},{4,6},{6,0},{1,3},{3,5},{5,7},{7,1},{8,10},{10,12},{12... | collective-permute-start | bytes 296 | tf_op jit(solution)/shard_map/ppermute | solution.py:24
  (3 other events, 2.6 us)
Sparse Core Ops, SparseCore 0:
  83.1 8.2 reduce-scatter.6
  184.5 9.2 reduce-scatter.8
where the time goes:
time: 246 us; the launch traced here: 244 us
  blocking collectives  120 us (49%)
  starting transfers between devices  40.9 us (17%)
  waiting for transfers between devices  39.5 us (16%)
  between operations  18.5 us (8%)
  matrix products  9.24 us (4%)
  other arithmetic  8.4 us (3%)
  local copies, waits for them, and re-layouts  6.98 us (3%)
    psum x2, blocking collectives, squares(): return lax.psum(jnp.sum(current * current), ('lat', 'lon', 'tm'))  81 us
    psum x1, blocking collectives, per_device(): lax.psum(jnp.sum(direction * image_field), ('lat', 'lon', 'tm'))  39.5 us
    ppermute x6, starting transfers between devices, extended(): before = lax.ppermute(last, axis, up)  13.9 us
    unnamed x4, waiting for transfers between devices  12.9 us
    all_to_all x1, waiting for transfers between devices, per_device(): lax.all_to_all(send_values, ('lat', 'lon'), split_axis=0, concat_axis=0,...  9.66 us
    all_to_all x1, starting transfers between devices, per_device(): lax.all_to_all(send_count, ('lat', 'lon'), split_axis=0, concat_axis=0, t...  7.39 us
    all_to_all x1, waiting for transfers between devices, per_device(): lax.all_to_all(send_cells, ('lat', 'lon'), split_axis=0, concat_axis=0, t...  6.88 us
    all_to_all x1, starting transfers between devices, per_device(): lax.all_to_all(send_cells, ('lat', 'lon'), split_axis=0, concat_axis=0, t...  6.74 us
  transfers between devices with their start and end apart: 18, of which 9 were waited for; matrix products, arithmetic and copies ran while one was open for 3% of the time, Pallas kernels for 0%

commit v1 on v0

v1 whole, which is shorter than its diff:
```python
import functools

import jax
import jax.numpy as jnp
from jax import lax
from jax.experimental import pallas as pl
from jax.experimental.pallas import tpu as pltpu
from jax.sharding import PartitionSpec as P

ITERS = 2
GROUP = 8
SPACE = ("lat", "lon")
ALL = ("lat", "lon", "tm")


def tile_kernel(owner_ref, count_ref, table_ref, values_ref, weight_ref, cells_ref, class_ref, land_ref, tiles_ref, plane_ref):
    block_total, variables, slots = values_ref.shape
    owners, stats, rows, cols = tiles_ref.shape

    diffusivity = jnp.zeros((rows, cols), jnp.float32)
    for index in range(table_ref.shape[0]):
        diffusivity = jnp.where(class_ref[0] == index, table_ref[index], diffusivity)
    sea = land_ref[0].astype(jnp.float32)
    plane_ref[...] = jnp.where(lax.axis_index("tm") == 0, diffusivity, sea)

    tiles_ref[...] = jnp.zeros_like(tiles_ref)
    lane = lax.broadcasted_iota(jnp.int32, (1, slots), 1)
    row_ids = lax.broadcasted_iota(jnp.int32, (rows, slots), 0)
    col_ids = lax.broadcasted_iota(jnp.int32, (cols, slots), 0)

    def block_sum(block):
        live = jnp.where(lane < count_ref[block], weight_ref[pl.ds(block, 1), :], 0.0)
        cells = cells_ref[pl.ds(block, 1), :]
        row_hit = row_ids == cells // cols
        terms = [live] + [live * values_ref[block, pl.ds(v, 1), :] for v in range(variables)]
        spread = jnp.concatenate([jnp.where(row_hit, term, 0.0) for term in terms], axis=0)
        high = spread.astype(jnp.bfloat16)
        low = (spread - high.astype(jnp.float32)).astype(jnp.bfloat16)
        col_hot = jnp.where(col_ids == cells % cols, 1.0, 0.0).astype(jnp.bfloat16)
        both = lax.dot_general(
            jnp.concatenate([high, low], axis=0),
            col_hot,
            (((1,), (1,)), ((), ())),
            preferred_element_type=jnp.float32,
        )
        return (both[: stats * rows] + both[stats * rows :]).reshape(stats, rows, cols)

    def step(group, carry):
        sums = [block_sum(group * GROUP + k) for k in range(GROUP)]
        for k in range(GROUP):
            owner = owner_ref[group * GROUP + k]
            tiles_ref[owner] += sums[k]
        return carry

    lax.fori_loop(0, block_total // GROUP, step, 0)


def total(x):
    return jnp.sum(jnp.sum(x, axis=1, keepdims=True), axis=0, keepdims=True)


def descent_kernel(counts, cov_ref, metric_ref, gathered_ref, solution_ref, residual_ref, right, image, direction, diag, coef):
    n_lat, n_lon, n_tm = counts
    rows, cols = gathered_ref.shape[2:]
    height, width = n_lat * rows, n_lon * cols
    variables = right.shape[1]

    def source(i, j, t):
        return (i * n_lon + j) * n_tm + t

    for i in range(n_lat):
        for j in range(n_lon):
            at = (slice(i * rows, (i + 1) * rows), slice(j * cols, (j + 1) * cols))
            coef[(0, *at)] = gathered_ref[source(i, j, 0), variables + 1]
            sea = gathered_ref[source(i, j, 1), variables + 1]
            coef[(1, *at)] = sea
            for t in range(n_tm):
                diag[(t, *at)] = gathered_ref[source(i, j, t), 0]
                for v in range(variables):
                    right[(t, v, *at)] = gathered_ref[source(i, j, t), v + 1] * sea

    def moved(x, dim, forward):
        return pltpu.roll(x, 1 if forward else x.shape[dim] - 1, dim)

    diffusivity, sea = coef[0], coef[1]
    row_ids = lax.broadcasted_iota(jnp.int32, (height, width), 0)
    north_open, south_open = row_ids > 0, row_ids < height - 1
    north = 0.5 * (jnp.where(north_open, moved(diffusivity, 0, True), 0.0) + diffusivity)
    south = 0.5 * (diffusivity + jnp.where(south_open, moved(diffusivity, 0, False), 0.0))
    west = 0.5 * (moved(diffusivity, 1, True) + diffusivity)
    east = 0.5 * (diffusivity + moved(diffusivity, 1, False))
    coef[2] = jnp.where(north_open, north, 0.0)
    coef[3] = jnp.where(south_open, south, 0.0)
    coef[4] = west
    coef[5] = east
    coef[6] = north + south + west + east

    def apply(field):
        along = jnp.zeros((height, width), jnp.float32)
        sea = coef[1]
        for t in range(n_tm):
            masked = [[field[s, v] * sea for v in range(variables)] for s in range(n_tm)]
            centre = diag[t] + coef[6]
            for v in range(variables):
                here = masked[t][v]
                mixed = centre * here
                for w in range(variables):
                    mixed = mixed + cov_ref[v, w] * masked[t][w]
                for s in range(n_tm):
                    mixed = mixed + metric_ref[t, s] * masked[s][v]
                spread = (
                    coef[2] * moved(here, 0, True)
                    + coef[3] * moved(here, 0, False)
                    + coef[4] * moved(here, 1, True)
                    + coef[5] * moved(here, 1, False)
                )
                full = field[t, v]
                result = sea * (mixed - spread) + (1.0 - sea) * full
                image[t, v] = result
                along = along + full * result
        return total(along)

    fields = [(t, v) for t in range(n_tm) for v in range(variables)]
    lat, lon, tm = lax.axis_index("lat"), lax.axis_index("lon"), lax.axis_index("tm")
    own = (pl.ds(pl.multiple_of(lat * rows, rows), rows), pl.ds(pl.multiple_of(lon * cols, cols), cols))

    squares = jnp.zeros((height, width), jnp.float32)
    for t, v in fields:
        squares = squares + right[t, v] * right[t, v]
    norm_now = total(squares)
    for v in range(variables):
        solution_ref[0, v, 0] = jnp.zeros((rows, cols), jnp.float32)
    current = right
    for iteration in range(ITERS):
        step_size = norm_now / apply(current)
        for v in range(variables):
            solution_ref[0, v, 0] += step_size * current[(tm, v, *own)]
        if iteration == ITERS - 1:
            for v in range(variables):
                residual_ref[0, v, 0] = right[(tm, v, *own)] - step_size * image[(tm, v, *own)]
            break
        squares = jnp.zeros((height, width), jnp.float32)
        for t, v in fields:
            after = right[t, v] - step_size * image[t, v]
            image[t, v] = after
            squares = squares + after * after
        norm_next = total(squares)
        share = norm_next / norm_now
        for t, v in fields:
            direction[t, v] = image[t, v] + share * current[t, v]
            right[t, v] = image[t, v]
        norm_now = norm_next
        current = direction


def whole(shape_of):
    return pl.BlockSpec(memory_space=shape_of)


def per_device(class_ids, coef_table, land_mask, cross_cov, time_metric, obs_values, obs_weight, obs_cells, obs_count, block_owner):
    counts = tuple(lax.axis_size(axis) for axis in ALL)
    n_lat, n_lon, n_tm = counts
    rows, cols = class_ids.shape[1:]
    variables = obs_values.shape[1]
    owners = n_lat * n_lon
    vmem, smem = whole(pltpu.VMEM), whole(pltpu.SMEM)
    tiles, plane = pl.pallas_call(
        tile_kernel,
        out_shape=(
            jax.ShapeDtypeStruct((owners, variables + 1, rows, cols), jnp.float32),
            jax.ShapeDtypeStruct((rows, cols), jnp.float32),
        ),
        in_specs=[smem, smem, smem] + [vmem] * 5,
        out_specs=(vmem, vmem),
        compiler_params=pltpu.CompilerParams(vmem_limit_bytes=32 * 1024 * 1024),
    )(block_owner[:, 0], obs_count, coef_table, obs_values, obs_weight, obs_cells, class_ids, land_mask)
    parts = lax.all_to_all(tiles, SPACE, split_axis=0, concat_axis=0, tiled=True)
    mine = jnp.concatenate([jnp.sum(parts, axis=0), plane[None]], axis=0)
    spread = jnp.broadcast_to(mine[None], (owners * n_tm, *mine.shape))
    gathered = lax.all_to_all(spread, ALL, split_axis=0, concat_axis=0, tiled=True)
    height, width = n_lat * rows, n_lon * cols
    field = (n_tm, variables, height, width)
    out = jax.ShapeDtypeStruct((1, variables, 1, rows, cols), jnp.float32)
    return pl.pallas_call(
        functools.partial(descent_kernel, counts),
        out_shape=(out, out),
        in_specs=[smem, smem, vmem],
        out_specs=(vmem, vmem),
        scratch_shapes=[
            pltpu.VMEM(field, jnp.float32),
            pltpu.VMEM(field, jnp.float32),
            pltpu.VMEM(field, jnp.float32),
            pltpu.VMEM((n_tm, height, width), jnp.float32),
            pltpu.VMEM((7, height, width), jnp.float32),
        ],
        compiler_params=pltpu.CompilerParams(vmem_limit_bytes=48 * 1024 * 1024),
    )(cross_cov, time_metric, gathered)


def solution(mesh):
    in_specs = (
        P(None, "lat", "lon"),
        P(),
        P(None, "lat", "lon"),
        P(),
        P(),
        P(ALL, None, None),
        P(ALL, None),
        P(ALL, None),
        P(ALL),
        P(ALL, None),
    )
    out_specs = (P("tm", None, None, "lat", "lon"), P("tm", None, None, "lat", "lon"))
    return jax.shard_map(per_device, mesh=mesh, in_specs=in_specs, out_specs=out_specs, check_vma=False)
```

time: 246 us -> 46.4 us (0.19)
  blocking collectives: 120 us -> 37.7 us
  starting transfers between devices: 40.9 us -> 0 us
  waiting for transfers between devices: 39.5 us -> 0 us
  between operations: 18.5 us -> 0.76 us
  matrix products: 9.24 us -> 0 us
  other arithmetic: 8.4 us -> 0.03 us
  Pallas kernels: 0 us -> 5.63 us
  local copies, waits for them, and re-layouts: 6.98 us -> 1.68 us
    psum x3 -> x0, blocking collectives: 120 us -> none  [the longest x2 81 us: squares(): return lax.psum(jnp.sum(current * current), ('lat', 'lon', 'tm'))]
    all_to_all x0 -> x2, blocking collectives: none -> 37.7 us  [the longest x1 20.5 us: per_device(): lax.all_to_all(spread, ALL, split_axis=0, concat_axis=0, tiled=True)]
    all_to_all x4 -> x0, waiting for transfers between devices: 21.9 us -> none  [the longest x1 9.66 us: per_device(): lax.all_to_all(send_values, ('lat', 'lon'), split_axis=0, concat_axis=0,...]
    all_to_all x4 -> x0, starting transfers between devices: 21.1 us -> none  [the longest x1 7.39 us: per_device(): lax.all_to_all(send_count, ('lat', 'lon'), split_axis=0, concat_axis=0, t...]
    ppermute x12 -> x0, starting transfers between devices: 19.6 us -> none  [the longest x6 13.9 us: extended(): before = lax.ppermute(last, axis, up)]
    unnamed x4 -> x0, waiting for transfers between devices: 12.9 us -> none
    dot_general x6 -> x0, matrix products: 9.24 us -> none  [the longest x4 6.26 us: accumulate(): jnp.dot(weighted, col_hot, precision=HIGHEST, preferred_element_type=jnp....]
    pallas_call x0 -> x2, Pallas kernels: none -> 5.63 us  [the longest x1 2.96 us: per_device(): pl.pallas_call(tile_kernel, out_shape=(jax.ShapeDtypeStruct((owners, vari...]
  transfers between devices with their start and end apart: 18 -> 0, of which waited for: 9 -> 0; matrix products, arithmetic and copies ran while one was open for 3% -> 0% of each run, Pallas kernels for 0% -> 0%
where the time goes in v1:
time: 46.4 us; the launch traced here: 45.8 us
  blocking collectives  37.7 us (81%)
  Pallas kernels  5.63 us (12%)
  local copies, waits for them, and re-layouts  1.68 us (4%)
  between operations  0.76 us (2%)
    all_to_all x1, blocking collectives, per_device(): lax.all_to_all(spread, ALL, split_axis=0, concat_axis=0, tiled=True)  20.5 us
    all_to_all x1, blocking collectives, per_device(): lax.all_to_all(tiles, SPACE, split_axis=0, concat_axis=0, tiled=True)  17.2 us
    pallas_call x1, Pallas kernels, per_device(): pl.pallas_call(tile_kernel, out_shape=(jax.ShapeDtypeStruct((owners, vari...  2.96 us
    pallas_call x1, Pallas kernels, per_device(): pl.pallas_call(functools.partial(descent_kernel, counts), out_shape=(out,...  2.67 us
    unnamed x19, local copies, waits for them, and re-layouts  1.64 us

profile of v1, /device:TPU:0, one launch (start us, length us, event | category | flops | bytes accessed | tf_op | source)
XLA Modules:
  0.0 45.8 jit_solution(17745587144602802451)
XLA Ops:
  0.6 0.0 copy-start.1
  0.6 0.0 copy-start
  0.7 0.0 copy-start.2
  0.7 0.0 copy-start.3
  0.7 1.0 %copy.12.values_ref = f32[64,3,128]{2,1,0:T(4,128)S(1)} copy(f32[64,3,128]{2,0,1:T(8,128)} %param.15) | data formatting | bytes 196608 | tf_op args[5]
  1.7 0.0 copy-start.6
  1.7 0.0 copy-start.7
  1.7 0.0 copy-start.8
  1.7 0.0 copy-done.1
  1.7 0.0 copy-done
  1.7 0.0 copy-done.2
  1.7 0.0 copy-done.3
  1.7 0.6 %copy-done.6 = s32[64,1]{0,1:T(1,128)S(1)} copy-done((s32[64,1]{0,1:T(1,128)S(1)}, s32[64,1]{0,1:T(1,128)}, u32[]{:S(2)}) %copy-start.6) | copy-done | bytes 280
  2.3 0.0 copy-done.7
  2.3 0.0 copy-done.8
  2.3 3.0 %shard_map.113 = (f32[16,4,8,128]{3,2,1,0:T(8,128)S(1)}, f32[8,128]{1,0:T(8,128)S(1)}) custom-call(s32[64]{0:T(128)S(1)} %bitcast.3, s32[64]{0:T(128)S(1)} %copy-done.7, f32[8]{0:T(128)S(1)} %copy-done.8, f32[64,3,128]{2,1,0:T(4,128)S(1)} %copy.12.values_ref, f32[64,128]{1,0:T(8,128)S(1)} %copy-done, s32[64,128]{1,0:T(8,128)S(1)} %copy-done.1, ...), custom_call_target="tpu_custom_call" | custom-call | tf_op jit(solution)/shard_map/pallas_call | solution.py:167
  5.3 17.2 %all_to_all.10 = f32[16,4,8,128]{3,2,1,0:T(8,128)S(1)} all-to-all(f32[16,4,8,128]{3,2,1,0:T(8,128)S(1)} %get-tuple-element.4), channel_id=1, replica_groups=mesh['lat'=4,'lon'=4,'tm'=2] {'lat','lon'}, dimensions={0} | all-to-all | bytes 524288 | tf_op jit(solution)/shard_map/all_to_all | solution.py:177
  22.6 0.0 copy-start.4
  22.6 0.0 copy-start.5
  22.7 20.5 %all_to_all.11.gathered_ref = f32[32,5,8,128]{3,2,1,0:T(8,128)S(1)} all-to-all(f32[32,5,8,128]{3,2,1,0:T(8,128)S(1)} %broadcast_in_dim.10), channel_id=1, replica_groups=mesh['lat'=4,'lon'=4,'tm'=2] {'lat','lon','tm'}, dimensions={0} | all-to-all | bytes 1310720 | tf_op jit(solution)/shard_map/all_to_all | solution.py:180
  43.2 0.0 copy-done.4
  43.2 0.0 copy-done.5
  43.2 2.7 %shard_map.114 = (f32[1,3,1,8,128]{4,3,2,1,0:T(8,128)}, f32[1,3,1,8,128]{4,3,2,1,0:T(8,128)}) custom-call(f32[3,3]{1,0:T(4,128)S(1)} %copy-done.4, f32[2,2]{1,0:T(2,128)S(1)} %copy-done.5, f32[32,5,8,128]{3,2,1,0:T(8,128)S(1)} %all_to_all.11.gathered_ref), custom_call_target="tpu_custom_call" | custom-call | tf_op jit(solution)/shard_map/pallas_call | solution.py:184
  (3 shorter events, 0.1 us)
Async XLA Ops:
  0.6 1.1 %copy-start.1 = (s32[64,128]{1,0:T(8,128)S(1)}, s32[64,128]{1,0:T(8,128)}, u32[]{:S(2)}) copy-start(s32[64,128]{1,0:T(8,128)} %cells_ref.1) | copy-start | bytes 98308
  0.6 1.1 %copy-start = (f32[64,128]{1,0:T(8,128)S(1)}, f32[64,128]{1,0:T(8,128)}, u32[]{:S(2)}) copy-start(f32[64,128]{1,0:T(8,128)} %weight_ref.1) | copy-start | bytes 98308
  0.7 1.1 %copy-start.2 = (s32[1,8,128]{2,1,0:T(8,128)S(1)}, s32[1,8,128]{2,1,0:T(8,128)}, u32[]{:S(2)}) copy-start(s32[1,8,128]{2,1,0:T(8,128)} %class_ref.1) | copy-start | bytes 12292
  0.7 1.1 %copy-start.3 = (s32[1,8,128]{2,1,0:T(8,128)S(1)}, s32[1,8,128]{2,1,0:T(8,128)}, u32[]{:S(2)}) copy-start(s32[1,8,128]{2,1,0:T(8,128)} %land_ref.1) | copy-start | bytes 12292
  1.7 0.7 %copy-start.6 = (s32[64,1]{0,1:T(1,128)S(1)}, s32[64,1]{0,1:T(1,128)}, u32[]{:S(2)}) copy-start(s32[64,1]{0,1:T(1,128)} %param.19) | copy-start | bytes 772
  1.7 0.7 %copy-start.7 = (s32[64]{0:T(128)S(1)}, s32[64]{0:T(128)}, u32[]{:S(2)}) copy-start(s32[64]{0:T(128)} %count_ref.1) | copy-start | bytes 772
  1.7 0.7 %copy-start.8 = (f32[8]{0:T(128)S(1)}, f32[8]{0:T(128)}, u32[]{:S(2)}) copy-start(f32[8]{0:T(128)} %table_ref.1) | copy-start | bytes 100
  22.6 20.5 %copy-start.4 = (f32[3,3]{1,0:T(4,128)S(1)}, f32[3,3]{1,0:T(4,128)}, u32[]{:S(2)}) copy-start(f32[3,3]{1,0:T(4,128)} %cov_ref.1) | copy-start | bytes 112
  22.6 20.5 %copy-start.5 = (f32[2,2]{1,0:T(2,128)S(1)}, f32[2,2]{1,0:T(2,128)}, u32[]{:S(2)}) copy-start(f32[2,2]{1,0:T(2,128)} %metric_ref.1) | copy-start | bytes 52

commit v2 on v1

v2 whole, which is shorter than its diff:
```python
import functools

import jax
import jax.numpy as jnp
from jax import lax
from jax.experimental import pallas as pl
from jax.experimental.pallas import tpu as pltpu
from jax.sharding import PartitionSpec as P

ITERS = 2
GROUP = 8
INPUTS = 8
ALL = ("lat", "lon", "tm")


def tile_kernel(*refs):
    arguments, (keep_ref, send_ref, planes_ref, tiles) = refs[:INPUTS], refs[INPUTS : INPUTS + 4]
    local, arrived = refs[INPUTS + 4 : -1], refs[-1]
    owner_ref, count_ref, table_ref, values_ref, weight_ref, cells_ref, class_ref, land_ref = local
    copies = [pltpu.make_async_copy(a, b, arrived.at[k]) for k, (a, b) in enumerate(zip(arguments, local))]
    for copy in copies:
        copy.start()
    tiles[...] = jnp.zeros_like(tiles)
    planes_ref[...] = jnp.zeros_like(planes_ref)
    variables, block_total, slots = values_ref.shape
    n_lon, n_lat, stats, rows, cols = tiles.shape
    lat, lon, tm = lax.axis_index("lat"), lax.axis_index("lon"), lax.axis_index("tm")
    for copy in copies:
        copy.wait()

    diffusivity = jnp.zeros((rows, cols), jnp.float32)
    for index in range(table_ref.shape[0]):
        diffusivity = jnp.where(class_ref[0] == index, table_ref[index], diffusivity)
    sea = land_ref[0].astype(jnp.float32)
    planes_ref[0, lat] = jnp.where(tm == 0, diffusivity, sea)

    lane = lax.broadcasted_iota(jnp.int32, (1, slots), 1)
    row_ids = lax.broadcasted_iota(jnp.int32, (rows, slots), 0)
    col_ids = lax.broadcasted_iota(jnp.int32, (cols, slots), 0)

    def block_sum(block):
        live = jnp.where(lane < count_ref[block], weight_ref[pl.ds(block, 1), :], 0.0)
        cells = cells_ref[pl.ds(block, 1), :]
        row_hit = row_ids == cells // cols
        terms = [live] + [live * values_ref[v, pl.ds(block, 1), :] for v in range(variables)]
        spread = jnp.concatenate([jnp.where(row_hit, term, 0.0) for term in terms], axis=0)
        high = spread.astype(jnp.bfloat16)
        low = (spread - high.astype(jnp.float32)).astype(jnp.bfloat16)
        col_hot = jnp.where(col_ids == cells % cols, 1.0, 0.0).astype(jnp.bfloat16)
        both = lax.dot_general(
            jnp.concatenate([high, low], axis=0),
            col_hot,
            (((1,), (1,)), ((), ())),
            preferred_element_type=jnp.float32,
        )
        return (both[: stats * rows] + both[stats * rows :]).reshape(stats, rows, cols)

    def step(group, carry):
        sums = [block_sum(group * GROUP + k) for k in range(GROUP)]
        for k in range(GROUP):
            owner = owner_ref[group * GROUP + k]
            tiles[jnp.bitwise_xor(owner % n_lon, lon), owner // n_lon] += sums[k]
        return carry

    lax.fori_loop(0, block_total // GROUP, step, 0)
    for m in range(n_lon // 2):
        for i in range(n_lat):
            for s in range(stats):
                keep_ref[m, s, i] = tiles[2 * m, i, s]
                send_ref[m, s, i] = tiles[2 * m + 1, i, s]


def total(x):
    return jnp.sum(jnp.sum(x, axis=1, keepdims=True), axis=0, keepdims=True)


def descent_kernel(offsets, cov_ref, metric_ref, near_ref, far_ref, solution_ref, residual_ref, right, image, direction, diag, coef, shared):
    n_lat, rows, cols = near_ref.shape[2:]
    n_tm, variables, height, width = right.shape
    lat, lon, tm = lax.axis_index("lat"), lax.axis_index("lon"), lax.axis_index("tm")

    def place(part_ref, part, lon_offset, tm_offset):
        t = jnp.bitwise_xor(tm, tm_offset)
        across = pl.ds(pl.multiple_of(jnp.bitwise_xor(lon, lon_offset) * cols, cols), cols)
        for i in range(n_lat):
            down = slice(i * rows, (i + 1) * rows)
            diag[t, down, across] = part_ref[part, 0, i]
            for v in range(variables):
                right[t, v, down, across] = part_ref[part, v + 1, i]
            shared[t, down, across] = part_ref[part, variables + 1, i]

    for part, (lon_offset, tm_offset) in enumerate(offsets):
        place(near_ref, part, lon_offset, tm_offset)
        place(far_ref, part, lon_offset + 1, tm_offset)

    def moved(x, dim, forward):
        return pltpu.roll(x, 1 if forward else x.shape[dim] - 1, dim)

    diffusivity, sea = shared[0], shared[1]
    row_ids = lax.broadcasted_iota(jnp.int32, (height, width), 0)
    north_open, south_open = row_ids > 0, row_ids < height - 1
    north = 0.5 * (jnp.where(north_open, moved(diffusivity, 0, True), 0.0) + diffusivity)
    south = 0.5 * (diffusivity + jnp.where(south_open, moved(diffusivity, 0, False), 0.0))
    west = 0.5 * (moved(diffusivity, 1, True) + diffusivity)
    east = 0.5 * (diffusivity + moved(diffusivity, 1, False))
    coef[0] = jnp.where(north_open, north, 0.0)
    coef[1] = jnp.where(south_open, south, 0.0)
    coef[2] = west
    coef[3] = east
    coef[4] = north + south + west + east

    def apply(field):
        along = jnp.zeros((height, width), jnp.float32)
        sea = shared[1]
        for t in range(n_tm):
            masked = [[field[s, v] * sea for v in range(variables)] for s in range(n_tm)]
            centre = diag[t] + coef[4]
            for v in range(variables):
                here = masked[t][v]
                mixed = centre * here
                for w in range(variables):
                    mixed = mixed + cov_ref[v, w] * masked[t][w]
                for s in range(n_tm):
                    mixed = mixed + metric_ref[t, s] * masked[s][v]
                spread = (
                    coef[0] * moved(here, 0, True)
                    + coef[1] * moved(here, 0, False)
                    + coef[2] * moved(here, 1, True)
                    + coef[3] * moved(here, 1, False)
                )
                full = field[t, v]
                result = sea * (mixed - spread) + (1.0 - sea) * full
                image[t, v] = result
                along = along + full * result
        return total(along)

    fields = [(t, v) for t in range(n_tm) for v in range(variables)]
    own = (pl.ds(pl.multiple_of(lat * rows, rows), rows), pl.ds(pl.multiple_of(lon * cols, cols), cols))

    squares = jnp.zeros((height, width), jnp.float32)
    for t, v in fields:
        start = sea * right[t, v]
        right[t, v] = start
        squares = squares + start * start
    norm_now = total(squares)
    for v in range(variables):
        solution_ref[0, v, 0] = jnp.zeros((rows, cols), jnp.float32)
    current = right
    for iteration in range(ITERS):
        step_size = norm_now / apply(current)
        for v in range(variables):
            solution_ref[0, v, 0] += step_size * current[(tm, v, *own)]
        if iteration == ITERS - 1:
            for v in range(variables):
                residual_ref[0, v, 0] = right[(tm, v, *own)] - step_size * image[(tm, v, *own)]
            break
        squares = jnp.zeros((height, width), jnp.float32)
        for t, v in fields:
            after = right[t, v] - step_size * image[t, v]
            image[t, v] = after
            squares = squares + after * after
        norm_next = total(squares)
        share = norm_next / norm_now
        for t, v in fields:
            direction[t, v] = image[t, v] + share * current[t, v]
            right[t, v] = image[t, v]
        norm_now = norm_next
        current = direction


def bits(count):
    return [1 << k for k in range(count.bit_length() - 1)]


def swapped(x, axis, bit):
    return lax.ppermute(x, axis, [(i, i ^ bit) for i in range(lax.axis_size(axis))])


def per_device(class_ids, coef_table, land_mask, cross_cov, time_metric, obs_values, obs_weight, obs_cells, obs_count, block_owner):
    n_lat, n_lon, n_tm = (lax.axis_size(axis) for axis in ("lat", "lon", "tm"))
    rows, cols = class_ids.shape[1:]
    variables = obs_values.shape[1]
    stats = variables + 1
    vmem, smem = pl.BlockSpec(memory_space=pltpu.VMEM), pl.BlockSpec(memory_space=pltpu.SMEM)
    half = jax.ShapeDtypeStruct((n_lon // 2, stats, n_lat, rows, cols), jnp.float32)
    values = obs_values.transpose(1, 0, 2)
    arguments = (block_owner[:, 0], obs_count, coef_table, values, obs_weight, obs_cells, class_ids, land_mask)
    places = [pltpu.SMEM] * 3 + [pltpu.VMEM] * 5
    keep, send, planes = pl.pallas_call(
        tile_kernel,
        out_shape=(half, half, jax.ShapeDtypeStruct((1, n_lat, rows, cols), jnp.float32)),
        in_specs=[pl.BlockSpec(memory_space=pltpu.HBM)] * INPUTS,
        out_specs=(vmem, vmem, vmem),
        scratch_shapes=[
            pltpu.VMEM((n_lon, n_lat, stats, rows, cols), jnp.float32),
            *[place(x.shape, x.dtype) for place, x in zip(places, arguments)],
            pltpu.SemaphoreType.DMA((INPUTS,)),
        ],
        compiler_params=pltpu.CompilerParams(vmem_limit_bytes=32 * 1024 * 1024),
    )(*[pltpu.with_memory_space_constraint(x, pltpu.HBM) for x in arguments])

    partial = keep + swapped(send, "lon", 1)
    for bit in bits(n_lon)[1:]:
        partial = partial[0::2] + swapped(partial[1::2], "lon", bit)
    strip = jnp.concatenate([partial[0], planes], axis=0)
    for bit in bits(n_lat):
        strip = strip + swapped(strip, "lat", bit)

    near, offsets = strip[None], [(0, 0)]
    for bit in bits(n_tm):
        near = jnp.concatenate([near, swapped(near, "tm", bit)], axis=0)
        offsets = offsets + [(j, t + bit) for j, t in offsets]
    for bit in bits(n_lon)[1:]:
        near = jnp.concatenate([near, swapped(near, "lon", bit)], axis=0)
        offsets = offsets + [(j + bit, t) for j, t in offsets]
    far = swapped(near, "lon", 1)

    height, width = n_lat * rows, n_lon * cols
    field = pltpu.VMEM((n_tm, variables, height, width), jnp.float32)
    plane = pltpu.VMEM((n_tm, height, width), jnp.float32)
    out = jax.ShapeDtypeStruct((1, variables, 1, rows, cols), jnp.float32)
    return pl.pallas_call(
        functools.partial(descent_kernel, offsets),
        out_shape=(out, out),
        in_specs=[smem, smem, vmem, vmem],
        out_specs=(vmem, vmem),
        scratch_shapes=[field, field, field, plane, pltpu.VMEM((5, height, width), jnp.float32), plane],
        compiler_params=pltpu.CompilerParams(vmem_limit_bytes=48 * 1024 * 1024),
    )(cross_cov, time_metric, near, far)


def solution(mesh):
    in_specs = (
        P(None, "lat", "lon"),
        P(),
        P(None, "lat", "lon"),
        P(),
        P(),
        P(ALL, None, None),
        P(ALL, None),
        P(ALL, None),
        P(ALL),
        P(ALL, None),
    )
    out_specs = (P("tm", None, None, "lat", "lon"), P("tm", None, None, "lat", "lon"))
    return jax.shard_map(per_device, mesh=mesh, in_specs=in_specs, out_specs=out_specs, check_vma=False)
```

time: 46.4 us -> 35.4 us (0.76)
  blocking collectives: 37.7 us -> 0 us
  waiting for transfers between devices: 0 us -> 16 us
  starting transfers between devices: 0 us -> 12.3 us
  local copies, waits for them, and re-layouts: 1.68 us -> 0.02 us
    all_to_all x2 -> x0, blocking collectives: 37.7 us -> none  [the longest x1 20.5 us: per_device(): lax.all_to_all(spread, ALL, split_axis=0, concat_axis=0, tiled=True)]
    ppermute x0 -> x7, waiting for transfers between devices: none -> 16 us  [swapped(): lax.ppermute(x, axis, [(i, i ^ bit) for i in range(lax.axis_size(axis))])]
    ppermute x0 -> x7, starting transfers between devices: none -> 12.3 us  [swapped(): lax.ppermute(x, axis, [(i, i ^ bit) for i in range(lax.axis_size(axis))])]
    unnamed x19 -> x4, local copies, waits for them, and re-layouts: 1.64 us -> 0.01 us
  transfers between devices with their start and end apart: 0 -> 7, of which waited for: 0 -> 7; matrix products, arithmetic and copies ran while one was open for 0% -> 0% of each run, Pallas kernels for 0% -> 0%
where the time goes in v2:
time: 35.4 us; the launch traced here: 35.3 us
  waiting for transfers between devices  16 us (45%)
  starting transfers between devices  12.3 us (35%)
  Pallas kernels  6.09 us (17%)
  between operations  0.71 us (2%)
    ppermute x7, waiting for transfers between devices, swapped(): lax.ppermute(x, axis, [(i, i ^ bit) for i in range(lax.axis_size(axis))])  16 us
    ppermute x7, starting transfers between devices, swapped(): lax.ppermute(x, axis, [(i, i ^ bit) for i in range(lax.axis_size(axis))])  12.3 us
    pallas_call x1, Pallas kernels, per_device(): pl.pallas_call(tile_kernel, out_shape=(half, half, jax.ShapeDtypeStruct((...  3.4 us
    pallas_call x1, Pallas kernels, per_device(): pl.pallas_call(functools.partial(descent_kernel, offsets), out_shape=(out...  2.69 us
  transfers between devices with their start and end apart: 7, of which 7 were waited for; matrix products, arithmetic and copies ran while one was open for 0% of the time, Pallas kernels for 0%

profile of v2, /device:TPU:0, one launch (start us, length us, event | category | flops | bytes accessed | tf_op | source)
XLA Modules:
  0.0 35.3 jit_solution(15171793257898277390)
XLA Ops:
  0.6 3.4 %shard_map.113 = (f32[2,4,4,8,128]{4,3,2,1,0:T(8,128)S(1)}, f32[2,4,4,8,128]{4,3,2,1,0:T(8,128)S(1)}, f32[1,4,8,128]{3,2,1,0:T(8,128)S(1)}) custom-call(s32[64]{0:T(128)} %bitcast.7, s32[64]{0:T(128)} %refs_1_.1, f32[8]{0:T(128)} %refs_2_.1, f32[3,64,128]{2,1,0:T(8,128)} %bitcast.6, f32[64,128]{1,0:T(8,128)} %refs_4_.1, s32[64,128]{1,0:T(8,128)} %refs_5_.1, ...), custom_call_target="tpu_custom_call" | custom-call | tf_op jit(solution)/shard_map/pallas_call | solution.py:189
  4.0 0.5 %collective-permute-start = (f32[2,4,4,8,128]{4,3,2,1,0:T(8,128)S(1)}, f32[2,4,4,8,128]{4,3,2,1,0:T(8,128)S(1)}, u32[]{:S(2)}, u32[]{:S(2)}) collective-permute-start(f32[2,4,4,8,128]{4,3,2,1,0:T(8,128)S(1)} %get-tuple-element.6), channel_id=1, source_target_pairs={{0,2},{2,0},{4,6},{6,4},{1,3},{3,1},{5,7},{7,5},{8,10},{10,8},{12,... | collective-permute-start | bytes 393224 | tf_op jit(solution)/shard_map/ppermute | solution.py:176
  4.5 1.0 %collective-permute-done = f32[2,4,4,8,128]{4,3,2,1,0:T(8,128)S(1)} collective-permute-done((f32[2,4,4,8,128]{4,3,2,1,0:T(8,128)S(1)}, f32[2,4,4,8,128]{4,3,2,1,0:T(8,128)S(1)}, u32[]{:S(2)}, u32[]{:S(2)}) %collective-permute-start) | collective-permute-done | bytes 131104 | tf_op jit(solution)/shard_map/ppermute | solution.py:176
  5.6 2.9 %collective-permute-start.1 = (f32[1,4,4,8,128]{4,3,2,1,0:T(8,128)S(1)}, f32[1,4,4,8,128]{4,3,2,1,0:T(8,128)S(1)}, u32[]{:S(2)}, u32[]{:S(2)}) collective-permute-start(f32[1,4,4,8,128]{4,3,2,1,0:T(8,128)S(1)} %slice.11), channel_id=1, source_target_pairs={{0,4},{2,6},{4,0},{6,2},{1,5},{3,7},{5,1},{7,3},{8,12},{10,14},{12... | collective-permute-start | bytes 196616 | tf_op jit(solution)/shard_map/ppermute | solution.py:176
  8.5 2.4 %collective-permute-done.1 = f32[1,4,4,8,128]{4,3,2,1,0:T(8,128)S(1)} collective-permute-done((f32[1,4,4,8,128]{4,3,2,1,0:T(8,128)S(1)}, f32[1,4,4,8,128]{4,3,2,1,0:T(8,128)S(1)}, u32[]{:S(2)}, u32[]{:S(2)}) %collective-permute-start.1) | collective-permute-done | bytes 65568 | tf_op jit(solution)/shard_map/ppermute | solution.py:176
  11.0 2.0 %collective-permute-start.2 = (f32[5,4,8,128]{3,2,1,0:T(8,128)S(1)}, f32[5,4,8,128]{3,2,1,0:T(8,128)S(1)}, u32[]{:S(2)}, u32[]{:S(2)}) collective-permute-start(f32[5,4,8,128]{3,2,1,0:T(8,128)S(1)} %pad_maximum_fusion.2), channel_id=1, source_target_pairs={{0,8},{8,0},{16,24},{24,16},{1,9},{9,1},{17,25},{25,17},{2,10},{10... | collective-permute-start | bytes 245768 | tf_op jit(solution)/shard_map/ppermute | solution.py:176
  12.9 2.5 %collective-permute-done.2 = f32[5,4,8,128]{3,2,1,0:T(8,128)S(1)} collective-permute-done((f32[5,4,8,128]{3,2,1,0:T(8,128)S(1)}, f32[5,4,8,128]{3,2,1,0:T(8,128)S(1)}, u32[]{:S(2)}, u32[]{:S(2)}) %collective-permute-start.2) | collective-permute-done | bytes 81952 | tf_op jit(solution)/shard_map/ppermute | solution.py:176
  15.5 3.0 %collective-permute-start.3 = (f32[5,4,8,128]{3,2,1,0:T(8,128)S(1)}, f32[5,4,8,128]{3,2,1,0:T(8,128)S(1)}, u32[]{:S(2)}, u32[]{:S(2)}) collective-permute-start(f32[5,4,8,128]{3,2,1,0:T(8,128)S(1)} %fusion.1), channel_id=1, source_target_pairs={{0,16},{8,24},{16,0},{24,8},{1,17},{9,25},{17,1},{25,9},{2,18},{10... | collective-permute-start | bytes 245768 | tf_op jit(solution)/shard_map/ppermute | solution.py:176
  18.5 2.4 %collective-permute-done.3 = f32[5,4,8,128]{3,2,1,0:T(8,128)S(1)} collective-permute-done((f32[5,4,8,128]{3,2,1,0:T(8,128)S(1)}, f32[5,4,8,128]{3,2,1,0:T(8,128)S(1)}, u32[]{:S(2)}, u32[]{:S(2)}) %collective-permute-start.3) | collective-permute-done | bytes 81952 | tf_op jit(solution)/shard_map/ppermute | solution.py:176
  20.9 1.9 %collective-permute-start.4 = (f32[1,5,4,8,128]{4,3,2,1,0:T(8,128)S(1)}, f32[1,5,4,8,128]{4,3,2,1,0:T(8,128)S(1)}, u32[]{:S(2)}, u32[]{:S(2)}) collective-permute-start(f32[1,5,4,8,128]{4,3,2,1,0:T(8,128)S(1)} %add_bitcast_fusion), channel_id=1, source_target_pairs={{0,1},{1,0},{2,3},{3,2},{4,5},{5,4},{6,7},{7,6},{8,9},{9,8},{10,11... | collective-permute-start | bytes 245768 | tf_op jit(solution)/shard_map/ppermute | solution.py:176
  22.8 2.6 %collective-permute-done.4 = f32[1,5,4,8,128]{4,3,2,1,0:T(8,128)S(1)} collective-permute-done((f32[1,5,4,8,128]{4,3,2,1,0:T(8,128)S(1)}, f32[1,5,4,8,128]{4,3,2,1,0:T(8,128)S(1)}, u32[]{:S(2)}, u32[]{:S(2)}) %collective-permute-start.4) | collective-permute-done | bytes 81952 | tf_op jit(solution)/shard_map/ppermute | solution.py:176
  25.4 0.0 copy-start
  25.4 0.0 copy-start.1
  25.5 1.9 %collective-permute-start.5 = (f32[2,5,4,8,128]{4,3,2,1,0:T(8,128)S(1)}, f32[2,5,4,8,128]{4,3,2,1,0:T(8,128)S(1)}, u32[]{:S(2)}, u32[]{:S(2)}) collective-permute-start(f32[2,5,4,8,128]{4,3,2,1,0:T(8,128)S(1)} %pad_maximum_fusion.1), channel_id=1, source_target_pairs={{0,4},{2,6},{4,0},{6,2},{1,5},{3,7},{5,1},{7,3},{8,12},{10,14},{12... | collective-permute-start | bytes 491528 | tf_op jit(solution)/shard_map/ppermute | solution.py:176
  27.4 3.5 %collective-permute-done.5 = f32[2,5,4,8,128]{4,3,2,1,0:T(8,128)S(1)} collective-permute-done((f32[2,5,4,8,128]{4,3,2,1,0:T(8,128)S(1)}, f32[2,5,4,8,128]{4,3,2,1,0:T(8,128)S(1)}, u32[]{:S(2)}, u32[]{:S(2)}) %collective-permute-start.5) | collective-permute-done | bytes 163872 | tf_op jit(solution)/shard_map/ppermute | solution.py:176
  30.9 0.1 collective-permute-start.6
  30.9 1.6 %collective-permute-done.6.far_ref = f32[4,5,4,8,128]{4,3,2,1,0:T(8,128)S(1)} collective-permute-done((f32[4,5,4,8,128]{4,3,2,1,0:T(8,128)S(1)}, f32[4,5,4,8,128]{4,3,2,1,0:T(8,128)S(1)}, u32[]{:S(2)}, u32[]{:S(2)}) %collective-permute-start.6) | collective-permute-done | bytes 327712 | tf_op jit(solution)/shard_map/ppermute | solution.py:176
  32.6 0.0 copy-done
  32.6 0.0 copy-done.1
  32.6 2.7 %shard_map.114 = (f32[1,3,1,8,128]{4,3,2,1,0:T(8,128)}, f32[1,3,1,8,128]{4,3,2,1,0:T(8,128)}) custom-call(f32[3,3]{1,0:T(4,128)S(1)} %copy-done, f32[2,2]{1,0:T(2,128)S(1)} %copy-done.1, f32[4,5,4,8,128]{4,3,2,1,0:T(8,128)S(1)} %pad_maximum_fusion.near_ref, f32[4,5,4,8,128]{4,3,2,1,0:T(8,128)S(1)} %collective-permute-done.6.far_ref), custom_call_target="tpu_custom_call" | custom-call | tf_op jit(solution)/shard_map/pallas_call | solution.py:222
  (8 shorter events, 0.1 us)
Async XLA Ops:
  4.0 1.5 %collective-permute-start = (f32[2,4,4,8,128]{4,3,2,1,0:T(8,128)S(1)}, f32[2,4,4,8,128]{4,3,2,1,0:T(8,128)S(1)}, u32[]{:S(2)}, u32[]{:S(2)}) collective-permute-start(f32[2,4,4,8,128]{4,3,2,1,0:T(8,128)S(1)} %get-tuple-element.6), channel_id=1, source_target_pairs={{0,2},{2,0},{4,6},{6,4},{1,3},{3,1},{5,7},{7,5},{8,10},{10,8},{12,... | collective-permute-start | bytes 393224 | tf_op jit(solution)/shard_map/ppermute | solution.py:176
  5.6 5.3 %collective-permute-start.1 = (f32[1,4,4,8,128]{4,3,2,1,0:T(8,128)S(1)}, f32[1,4,4,8,128]{4,3,2,1,0:T(8,128)S(1)}, u32[]{:S(2)}, u32[]{:S(2)}) collective-permute-start(f32[1,4,4,8,128]{4,3,2,1,0:T(8,128)S(1)} %slice.11), channel_id=1, source_target_pairs={{0,4},{2,6},{4,0},{6,2},{1,5},{3,7},{5,1},{7,3},{8,12},{10,14},{12... | collective-permute-start | bytes 196616 | tf_op jit(solution)/shard_map/ppermute | solution.py:176
  11.0 4.5 %collective-permute-start.2 = (f32[5,4,8,128]{3,2,1,0:T(8,128)S(1)}, f32[5,4,8,128]{3,2,1,0:T(8,128)S(1)}, u32[]{:S(2)}, u32[]{:S(2)}) collective-permute-start(f32[5,4,8,128]{3,2,1,0:T(8,128)S(1)} %pad_maximum_fusion.2), channel_id=1, source_target_pairs={{0,8},{8,0},{16,24},{24,16},{1,9},{9,1},{17,25},{25,17},{2,10},{10... | collective-permute-start | bytes 245768 | tf_op jit(solution)/shard_map/ppermute | solution.py:176
  15.5 5.4 %collective-permute-start.3 = (f32[5,4,8,128]{3,2,1,0:T(8,128)S(1)}, f32[5,4,8,128]{3,2,1,0:T(8,128)S(1)}, u32[]{:S(2)}, u32[]{:S(2)}) collective-permute-start(f32[5,4,8,128]{3,2,1,0:T(8,128)S(1)} %fusion.1), channel_id=1, source_target_pairs={{0,16},{8,24},{16,0},{24,8},{1,17},{9,25},{17,1},{25,9},{2,18},{10... | collective-permute-start | bytes 245768 | tf_op jit(solution)/shard_map/ppermute | solution.py:176
  20.9 4.5 %collective-permute-start.4 = (f32[1,5,4,8,128]{4,3,2,1,0:T(8,128)S(1)}, f32[1,5,4,8,128]{4,3,2,1,0:T(8,128)S(1)}, u32[]{:S(2)}, u32[]{:S(2)}) collective-permute-start(f32[1,5,4,8,128]{4,3,2,1,0:T(8,128)S(1)} %add_bitcast_fusion), channel_id=1, source_target_pairs={{0,1},{1,0},{2,3},{3,2},{4,5},{5,4},{6,7},{7,6},{8,9},{9,8},{10,11... | collective-permute-start | bytes 245768 | tf_op jit(solution)/shard_map/ppermute | solution.py:176
  25.4 7.1 %copy-start = (f32[3,3]{1,0:T(4,128)S(1)}, f32[3,3]{1,0:T(4,128)}, u32[]{:S(2)}) copy-start(f32[3,3]{1,0:T(4,128)} %cov_ref.1) | copy-start | bytes 112
  25.4 7.1 %copy-start.1 = (f32[2,2]{1,0:T(2,128)S(1)}, f32[2,2]{1,0:T(2,128)}, u32[]{:S(2)}) copy-start(f32[2,2]{1,0:T(2,128)} %metric_ref.1) | copy-start | bytes 52
  25.5 5.4 %collective-permute-start.5 = (f32[2,5,4,8,128]{4,3,2,1,0:T(8,128)S(1)}, f32[2,5,4,8,128]{4,3,2,1,0:T(8,128)S(1)}, u32[]{:S(2)}, u32[]{:S(2)}) collective-permute-start(f32[2,5,4,8,128]{4,3,2,1,0:T(8,128)S(1)} %pad_maximum_fusion.1), channel_id=1, source_target_pairs={{0,4},{2,6},{4,0},{6,2},{1,5},{3,7},{5,1},{7,3},{8,12},{10,14},{12... | collective-permute-start | bytes 491528 | tf_op jit(solution)/shard_map/ppermute | solution.py:176
  30.9 1.7 %collective-permute-start.6 = (f32[4,5,4,8,128]{4,3,2,1,0:T(8,128)S(1)}, f32[4,5,4,8,128]{4,3,2,1,0:T(8,128)S(1)}, u32[]{:S(2)}, u32[]{:S(2)}) collective-permute-start(f32[4,5,4,8,128]{4,3,2,1,0:T(8,128)S(1)} %pad_maximum_fusion.near_ref), channel_id=1, source_target_pairs={{0,2},{2,0},{4,6},{6,4},{1,3},{3,1},{5,7},{7,5},{8,10},{10,8},{12,... | collective-permute-start | bytes 983048 | tf_op jit(solution)/shard_map/ppermute | solution.py:176

commit v3 on v2

v3 whole, which is shorter than its diff:
```python
import functools

import jax
import jax.numpy as jnp
from jax import lax
from jax.experimental import pallas as pl
from jax.experimental.pallas import tpu as pltpu
from jax.sharding import PartitionSpec as P

GROUP = 8
SIDES = 4
INPUTS = 8
ALL = ("lat", "lon", "tm")


def exact_dot(x, ones):
    high = x.astype(jnp.bfloat16)
    rest = x - high.astype(jnp.float32)
    middle = rest.astype(jnp.bfloat16)
    low = (rest - middle.astype(jnp.float32)).astype(jnp.bfloat16)
    parts = jnp.dot(jnp.concatenate([high, middle, low], axis=0), ones, preferred_element_type=jnp.float32)
    count = x.shape[0]
    return parts[:count] + (parts[count : 2 * count] + parts[2 * count :])


def side_column(side, cols):
    return jnp.where(side < 2, side, side + cols - SIDES)


def edge_columns(height, cols):
    column = lax.broadcasted_iota(jnp.int32, (cols, SIDES * height), 0)
    side = lax.broadcasted_iota(jnp.int32, (cols, SIDES * height), 1) // height
    return jnp.where(column == side_column(side, cols), 1.0, 0.0).astype(jnp.bfloat16)


def tile_kernel(*refs):
    arguments, (keep_ref, send_ref, planes_ref, tiles) = refs[:INPUTS], refs[INPUTS : INPUTS + 4]
    local, arrived = refs[INPUTS + 4 : -1], refs[-1]
    owner_ref, count_ref, table_ref, values_ref, weight_ref, cells_ref, class_ref, land_ref = local
    copies = [pltpu.make_async_copy(a, b, arrived.at[k]) for k, (a, b) in enumerate(zip(arguments, local))]
    for copy in copies:
        copy.start()
    tiles[...] = jnp.zeros_like(tiles)
    planes_ref[...] = jnp.zeros_like(planes_ref)
    variables, block_total, slots = values_ref.shape
    n_lon, n_lat, stats, rows, cols = tiles.shape
    lat, lon, tm = lax.axis_index("lat"), lax.axis_index("lon"), lax.axis_index("tm")
    for copy in copies:
        copy.wait()

    diffusivity = jnp.zeros((rows, cols), jnp.float32)
    for index in range(table_ref.shape[0]):
        diffusivity = jnp.where(class_ref[0] == index, table_ref[index], diffusivity)
    sea = land_ref[0].astype(jnp.float32)
    plane = jnp.where(tm == 0, diffusivity, sea)
    planes_ref[lat] = plane

    lane = lax.broadcasted_iota(jnp.int32, (1, slots), 1)
    row_ids = lax.broadcasted_iota(jnp.int32, (rows, slots), 0)
    col_ids = lax.broadcasted_iota(jnp.int32, (cols, slots), 0)

    def block_sum(block):
        live = jnp.where(lane < count_ref[block], weight_ref[pl.ds(block, 1), :], 0.0)
        cells = cells_ref[pl.ds(block, 1), :]
        row_hit = row_ids == cells // cols
        terms = [live] + [live * values_ref[v, pl.ds(block, 1), :] for v in range(variables)]
        spread = jnp.concatenate([jnp.where(row_hit, term, 0.0) for term in terms], axis=0)
        high = spread.astype(jnp.bfloat16)
        low = (spread - high.astype(jnp.float32)).astype(jnp.bfloat16)
        col_hot = jnp.where(col_ids == cells % cols, 1.0, 0.0).astype(jnp.bfloat16)
        both = lax.dot_general(
            jnp.concatenate([high, low], axis=0),
            col_hot,
            (((1,), (1,)), ((), ())),
            preferred_element_type=jnp.float32,
        )
        return (both[: stats * rows] + both[stats * rows :]).reshape(stats, rows, cols)

    def step(group, carry):
        sums = [block_sum(group * GROUP + k) for k in range(GROUP)]
        for k in range(GROUP):
            owner = owner_ref[group * GROUP + k]
            tiles[jnp.bitwise_xor(owner % n_lon, lon), owner // n_lon] += sums[k]
        return carry

    lax.fori_loop(0, block_total // GROUP, step, 0)
    for m in range(n_lon // 2):
        for i in range(n_lat):
            for s in range(stats):
                spot = (m * stats + s) * n_lat + i
                keep_ref[spot] = tiles[2 * m, i, s]
                send_ref[spot] = tiles[2 * m + 1, i, s]

    height = n_lat * rows
    lanes = SIDES * height
    edges = edge_columns(height, cols)
    row = lax.broadcasted_iota(jnp.int32, (height, lanes), 0)
    at_row = lax.broadcasted_iota(jnp.int32, (height, lanes), 1) % height == row
    own_row = lax.broadcasted_iota(jnp.int32, (rows, lanes), 1) % height == lax.broadcasted_iota(jnp.int32, (rows, lanes), 0) + lat * rows
    first = n_lon // 2 * stats * n_lat
    chunks = lanes // cols
    for offset in range(n_lon):
        picked = exact_dot(jnp.concatenate([tiles[offset, i, s] for s in range(stats) for i in range(n_lat)], axis=0), edges)
        packed = [
            jnp.sum(jnp.where(at_row, picked[s * height : (s + 1) * height], 0.0), axis=0, keepdims=True) for s in range(stats)
        ]
        blank = jnp.zeros((1, lanes), jnp.float32)
        shared = jnp.sum(jnp.where(own_row, exact_dot(plane, edges), 0.0), axis=0, keepdims=True) if offset == 0 else blank
        packed = jnp.concatenate(packed + [shared] + [blank] * (rows - stats - 1), axis=0)
        for c in range(chunks):
            spot = first + jnp.bitwise_xor(lon, offset) * chunks + c
            keep_ref[spot] = packed[:, c * cols : (c + 1) * cols]
            send_ref[spot] = packed[:, c * cols : (c + 1) * cols]


def strip_kernel(offsets, cov_ref, metric_ref, near_ref, far_ref, own_ref, sums_ref, right, image, change, diag, coef, shared):
    rows, cols = near_ref.shape[2:]
    n_tm, variables, height, width = right.shape
    stats, n_lat, lanes = variables + 1, height // rows, SIDES * height
    lat, lon, tm = lax.axis_index("lat"), lax.axis_index("lon"), lax.axis_index("tm")
    n_lon = lax.axis_size("lon")
    chunks = lanes // cols
    first = (stats + 1) * n_lat
    after, before = lax.rem(lon + 1, n_lon), lax.rem(lon + n_lon - 1, n_lon)
    lane = lax.broadcasted_iota(jnp.int32, (height, lanes), 1)
    at_row = lane % height == lax.broadcasted_iota(jnp.int32, (height, lanes), 0)
    from_after = lax.broadcasted_iota(jnp.int32, (rows, lanes), 1) < 2 * height
    side = lax.broadcasted_iota(jnp.int32, (lanes, cols), 0) // height
    column = lax.broadcasted_iota(jnp.int32, (lanes, cols), 1)
    targets = jnp.where(column == side_column(side, cols), 1.0, 0.0).astype(jnp.bfloat16)

    def place(part_ref, part, tm_offset):
        t = jnp.bitwise_xor(tm, tm_offset)
        for i in range(n_lat):
            down = slice(i * rows, (i + 1) * rows)
            diag[t, down, :cols] = part_ref[part, i]
            for v in range(variables):
                right[t, v, down, :cols] = part_ref[part, (v + 1) * n_lat + i]
            shared[t, down, :cols] = part_ref[part, stats * n_lat + i]

        def packed(j):
            return jnp.concatenate([part_ref[part, first + j * chunks + c] for c in range(chunks)], axis=1)

        beside = jnp.where(from_after, packed(after), packed(before))
        spread = jnp.concatenate([jnp.where(at_row, beside[s : s + 1], 0.0) for s in range(stats + 1)], axis=0)
        columns = exact_dot(spread, targets)
        diag[t, :, cols:] = columns[:height]
        for v in range(variables):
            right[t, v, :, cols:] = columns[(v + 1) * height : (v + 2) * height]
        shared[t, :, cols:] = columns[stats * height :]

    for part, tm_offset in enumerate(offsets):
        place(near_ref, part, tm_offset)
        place(far_ref, part, tm_offset + 1)

    def moved(x, dim, forward):
        return pltpu.roll(x, 1 if forward else x.shape[dim] - 1, dim)

    diffusivity, sea = shared[0], shared[1]
    row_ids = lax.broadcasted_iota(jnp.int32, (height, width), 0)
    north_open, south_open = row_ids > 0, row_ids < height - 1
    north = 0.5 * (jnp.where(north_open, moved(diffusivity, 0, True), 0.0) + diffusivity)
    south = 0.5 * (diffusivity + jnp.where(south_open, moved(diffusivity, 0, False), 0.0))
    west = 0.5 * (moved(diffusivity, 1, True) + diffusivity)
    east = 0.5 * (diffusivity + moved(diffusivity, 1, False))
    coef[0] = jnp.where(north_open, north, 0.0)
    coef[1] = jnp.where(south_open, south, 0.0)
    coef[2] = west
    coef[3] = east
    coef[4] = north + south + west + east

    def operate(field, span, use):
        sea = shared[1]
        for t in range(n_tm):
            masked = [[field[s, v] * sea for v in range(variables)] for s in range(n_tm)]
            centre = (diag[t] + coef[4])[:, :span]
            for v in range(variables):
                here = masked[t][v]
                mixed = centre * here[:, :span]
                for w in range(variables):
                    mixed = mixed + cov_ref[v, w] * masked[t][w][:, :span]
                for s in range(n_tm):
                    mixed = mixed + metric_ref[t, s] * masked[s][v][:, :span]
                spread = (
                    coef[0, :, :span] * moved(here[:, :span], 0, True)
                    + coef[1, :, :span] * moved(here[:, :span], 0, False)
                    + coef[2, :, :span] * moved(here, 1, True)[:, :span]
                    + coef[3, :, :span] * moved(here, 1, False)[:, :span]
                )
                use(t, v, sea[:, :span] * (mixed - spread) + (1.0 - sea[:, :span]) * field[t, v, :, :span])

    def sum_of(products):
        return jnp.sum(jnp.sum(products, axis=1, keepdims=True), axis=0, keepdims=True)

    fields = [(t, v) for t in range(n_tm) for v in range(variables)]
    none = jnp.zeros((height, cols), jnp.float32)
    bb, bw, ww, uu, ub, us, cross = [none] * 7
    for t, v in fields:
        start = sea * right[t, v]
        right[t, v] = start
        bb = bb + start[:, :cols] * start[:, :cols]

    def first_image(t, v, result):
        nonlocal bw, ww
        image[t, v] = result
        here = result[:, :cols]
        bw = bw + right[t, v, :, :cols] * here
        ww = ww + here * here

    operate(right, width, first_image)
    bb, ww = sum_of(bb), sum_of(ww)
    usable = (bb > 0.0) & (ww > 0.0)
    alpha = jnp.where(usable, jnp.sqrt(bb / jnp.where(usable, ww, 1.0)), 1.0)
    for t, v in fields:
        start = right[t, v]
        left = start - alpha * image[t, v]
        change[t, v] = left
        left, start = left[:, :cols], start[:, :cols]
        uu = uu + left * left
        ub = ub + left * start

    def second_image(t, v, result):
        nonlocal us, cross
        left, start = change[t, v, :, :cols], right[t, v, :, :cols]
        us = us + left * result
        cross = cross + (left * image[t, v, :, :cols] + start * result)
        image[t, v, :, cols:] = result

    operate(change, cols, second_image)
    own_rows = pl.ds(pl.multiple_of(lat * rows, rows), rows)
    for v in range(variables):
        own_ref[0, v] = right[tm, v, own_rows, :cols]
        own_ref[1, v] = image[tm, v, own_rows, :cols]
        own_ref[2, v] = change[tm, v, own_rows, :cols]
        own_ref[3, v] = image[tm, v, own_rows, cols:]
    for k, value in enumerate((alpha, bb, sum_of(bw), sum_of(uu), sum_of(ub), sum_of(us), sum_of(cross))):
        sums_ref[0, k : k + 1] = jnp.broadcast_to(value, (1, cols))
    sums_ref[0, 7:8] = jnp.zeros((1, cols), jnp.float32)


def update_kernel(own_ref, mine_ref, near_ref, far_ref, solution_ref, residual_ref):
    devices = [near_ref[k] for k in range(near_ref.shape[0])] + [far_ref[k] for k in range(far_ref.shape[0])]

    def over(values):
        return functools.reduce(jnp.add, values)

    def sums(device):
        return [device[k : k + 1] for k in range(7)]

    norm_start = over([sums(d)[1] for d in devices])
    step_first = norm_start / over([sums(d)[2] for d in devices])
    squares = []
    for d in devices:
        alpha, bb, bw, uu, ub, us, cross = sums(d)
        rho = step_first / alpha
        squares.append(rho * rho * uu + 2.0 * rho * (1.0 - rho) * ub + (1.0 - rho) * (1.0 - rho) * bb)
    norm_next = over(squares)
    share = norm_next / norm_start
    products = []
    for d in devices:
        alpha, bb, bw, uu, ub, us, cross = sums(d)
        rho = step_first / alpha
        kappa = 1.0 - rho + share
        products.append(rho * rho * us + rho * kappa * cross + kappa * kappa * bw)
    step_second = norm_next / over(products)
    rho = step_first / mine_ref[0, 0:1]
    kappa = 1.0 - rho + share
    for v in range(own_ref.shape[1]):
        start, image, left, left_image = (own_ref[k, v] for k in range(4))
        solution_ref[0, v, 0] = step_first * start + step_second * (rho * left + kappa * start)
        residual_ref[0, v, 0] = rho * left + (1.0 - rho) * start - step_second * (rho * left_image + kappa * image)


def bits(count):
    return [1 << k for k in range(count.bit_length() - 1)]


def swapped(x, axis, bit):
    return lax.ppermute(x, axis, [(i, i ^ bit) for i in range(lax.axis_size(axis))])


def gathered(x, axis):
    near, offsets = x[None], [0]
    for bit in reversed(bits(lax.axis_size(axis))[1:]):
        near = jnp.concatenate([near, swapped(near, axis, bit)], axis=0)
        offsets = offsets + [j + bit for j in offsets]
    return near, swapped(near, axis, 1), offsets


def per_device(class_ids, coef_table, land_mask, cross_cov, time_metric, obs_values, obs_weight, obs_cells, obs_count, block_owner):
    n_lat, n_lon, n_tm = (lax.axis_size(axis) for axis in ("lat", "lon", "tm"))
    rows, cols = class_ids.shape[1:]
    variables = obs_values.shape[1]
    stats = variables + 1
    vmem, smem = pl.BlockSpec(memory_space=pltpu.VMEM), pl.BlockSpec(memory_space=pltpu.SMEM)
    height = n_lat * rows
    halo = n_lon * SIDES * height // cols
    half = jax.ShapeDtypeStruct((n_lon // 2 * stats * n_lat + halo, rows, cols), jnp.float32)
    values = obs_values.transpose(1, 0, 2)
    arguments = (block_owner[:, 0], obs_count, coef_table, values, obs_weight, obs_cells, class_ids, land_mask)
    places = [pltpu.SMEM] * 3 + [pltpu.VMEM] * 5
    keep, send, planes = pl.pallas_call(
        tile_kernel,
        out_shape=(half, half, jax.ShapeDtypeStruct((n_lat, rows, cols), jnp.float32)),
        in_specs=[pl.BlockSpec(memory_space=pltpu.HBM)] * INPUTS,
        out_specs=(vmem, vmem, vmem),
        scratch_shapes=[
            pltpu.VMEM((n_lon, n_lat, stats, rows, cols), jnp.float32),
            *[place(x.shape, x.dtype) for place, x in zip(places, arguments)],
            pltpu.SemaphoreType.DMA((INPUTS,)),
        ],
        compiler_params=pltpu.CompilerParams(vmem_limit_bytes=32 * 1024 * 1024),
    )(*[pltpu.with_memory_space_constraint(x, pltpu.HBM) for x in arguments])

    partial = keep + swapped(send, "lon", 1)
    body, sides = partial[:-halo].reshape(n_lon // 2, stats * n_lat, rows, cols), partial[-halo:]
    for bit in bits(n_lon)[1:]:
        count = body.shape[0] // 2
        given = swapped(jnp.concatenate([body[1::2].reshape(-1, rows, cols), sides], axis=0), "lon", bit)
        body = body[0::2] + given[:-halo].reshape(count, stats * n_lat, rows, cols)
        sides = sides + given[-halo:]
    strip = jnp.concatenate([body[0], planes, sides], axis=0)
    for bit in bits(n_lat):
        strip = strip + swapped(strip, "lat", bit)

    near, far, offsets = gathered(strip, "tm")
    field = pltpu.VMEM((n_tm, variables, height, 2 * cols), jnp.float32)
    plane = pltpu.VMEM((n_tm, height, 2 * cols), jnp.float32)
    own, sums = pl.pallas_call(
        functools.partial(strip_kernel, offsets),
        out_shape=(
            jax.ShapeDtypeStruct((4, variables, rows, cols), jnp.float32),
            jax.ShapeDtypeStruct((1, rows, cols), jnp.float32),
        ),
        in_specs=[smem, smem, vmem, vmem],
        out_specs=(vmem, vmem),
        scratch_shapes=[field, field, field, plane, pltpu.VMEM((5, height, 2 * cols), jnp.float32), plane],
        compiler_params=pltpu.CompilerParams(vmem_limit_bytes=24 * 1024 * 1024),
    )(cross_cov, time_metric, near, far)

    near, far, _ = gathered(sums[0], "lon")
    out = jax.ShapeDtypeStruct((1, variables, 1, rows, cols), jnp.float32)
    return pl.pallas_call(
        update_kernel,
        out_shape=(out, out),
        in_specs=[vmem] * 4,
        out_specs=(vmem, vmem),
        compiler_params=pltpu.CompilerParams(vmem_limit_bytes=8 * 1024 * 1024),
    )(own, sums, near, far)


def solution(mesh):
    in_specs = (
        P(None, "lat", "lon"),
        P(),
        P(None, "lat", "lon"),
        P(),
        P(),
        P(ALL, None, None),
        P(ALL, None),
        P(ALL, None),
        P(ALL),
        P(ALL, None),
    )
    out_specs = (P("tm", None, None, "lat", "lon"), P("tm", None, None, "lat", "lon"))
    return jax.shard_map(per_device, mesh=mesh, in_specs=in_specs, out_specs=out_specs, check_vma=False)
```

time: 35.4 us -> 33.8 us (0.955)
  waiting for transfers between devices: 16 us -> 15.2 us
  starting transfers between devices: 12.3 us -> 11.8 us
    ppermute x7, waiting for transfers between devices: 16 us -> 15.2 us  [swapped(): lax.ppermute(x, axis, [(i, i ^ bit) for i in range(lax.axis_size(axis))])]
    pallas_call x1 -> x2, Pallas kernels: 2.69 us -> 2.14 us  [the longest x1 1.49 us: per_device(): pl.pallas_call(functools.partial(strip_kernel, offsets), out_shape=(jax.S...]
    ppermute x7, starting transfers between devices: 12.3 us -> 11.8 us  [swapped(): lax.ppermute(x, axis, [(i, i ^ bit) for i in range(lax.axis_size(axis))])]
where the time goes in v3:
time: 33.8 us; the launch traced here: 33.6 us
  waiting for transfers between devices  15.2 us (45%)
  starting transfers between devices  11.8 us (35%)
  Pallas kernels  5.77 us (17%)
  between operations  0.69 us (2%)
    ppermute x7, waiting for transfers between devices, swapped(): lax.ppermute(x, axis, [(i, i ^ bit) for i in range(lax.axis_size(axis))])  15.2 us
    ppermute x7, starting transfers between devices, swapped(): lax.ppermute(x, axis, [(i, i ^ bit) for i in range(lax.axis_size(axis))])  11.8 us
    pallas_call x1, Pallas kernels, per_device(): pl.pallas_call(tile_kernel, out_shape=(half, half, jax.ShapeDtypeStruct((...  3.63 us
    pallas_call x1, Pallas kernels, per_device(): pl.pallas_call(functools.partial(strip_kernel, offsets), out_shape=(jax.S...  1.49 us
  transfers between devices with their start and end apart: 7, of which 7 were waited for; matrix products, arithmetic and copies ran while one was open for 0% of the time, Pallas kernels for 0%

profile of v3, /device:TPU:0, one launch (start us, length us, event | category | flops | bytes accessed | tf_op | source)
XLA Modules:
  0.0 33.6 jit_solution(2214566022807986242)
XLA Ops:
  0.6 3.6 %shard_map.113 = (f32[36,8,128]{2,1,0:T(8,128)S(1)}, f32[36,8,128]{2,1,0:T(8,128)S(1)}, f32[4,8,128]{2,1,0:T(8,128)S(1)}) custom-call(s32[64]{0:T(128)} %bitcast.5, s32[64]{0:T(128)} %refs_1_.1, f32[8]{0:T(128)} %refs_2_.1, f32[3,64,128]{2,1,0:T(8,128)} %bitcast.4, f32[64,128]{1,0:T(8,128)} %refs_4_.1, s32[64,128]{1,0:T(8,128)} %refs_5_.1, ...), custom_call_target="tpu_custom_call" | custom-call | tf_op jit(solution)/shard_map/pallas_call | solution.py:302
  4.3 0.5 %collective-permute-start = (f32[36,8,128]{2,1,0:T(8,128)S(1)}, f32[36,8,128]{2,1,0:T(8,128)S(1)}, u32[]{:S(2)}, u32[]{:S(2)}) collective-permute-start(f32[36,8,128]{2,1,0:T(8,128)S(1)} %get-tuple-element.8), channel_id=1, source_target_pairs={{0,2},{2,0},{4,6},{6,4},{1,3},{3,1},{5,7},{7,5},{8,10},{10,8},{12,... | collective-permute-start | bytes 442376 | tf_op jit(solution)/shard_map/ppermute | solution.py:279
  4.8 1.0 %collective-permute-done = f32[36,8,128]{2,1,0:T(8,128)S(1)} collective-permute-done((f32[36,8,128]{2,1,0:T(8,128)S(1)}, f32[36,8,128]{2,1,0:T(8,128)S(1)}, u32[]{:S(2)}, u32[]{:S(2)}) %collective-permute-start) | collective-permute-done | bytes 147488 | tf_op jit(solution)/shard_map/ppermute | solution.py:279
  5.8 2.9 %collective-permute-start.1 = (f32[20,8,128]{2,1,0:T(8,128)S(1)}, f32[20,8,128]{2,1,0:T(8,128)S(1)}, u32[]{:S(2)}, u32[]{:S(2)}) collective-permute-start(f32[20,8,128]{2,1,0:T(8,128)S(1)} %concatenate.12), channel_id=1, source_target_pairs={{0,4},{2,6},{4,0},{6,2},{1,5},{3,7},{5,1},{7,3},{8,12},{10,14},{12... | collective-permute-start | bytes 245768 | tf_op jit(solution)/shard_map/ppermute | solution.py:279
  8.8 2.8 %collective-permute-done.1 = f32[20,8,128]{2,1,0:T(8,128)S(1)} collective-permute-done((f32[20,8,128]{2,1,0:T(8,128)S(1)}, f32[20,8,128]{2,1,0:T(8,128)S(1)}, u32[]{:S(2)}, u32[]{:S(2)}) %collective-permute-start.1) | collective-permute-done | bytes 81952 | tf_op jit(solution)/shard_map/ppermute | solution.py:279
  11.6 1.9 %collective-permute-start.2 = (f32[24,8,128]{2,1,0:T(8,128)S(1)}, f32[24,8,128]{2,1,0:T(8,128)S(1)}, u32[]{:S(2)}, u32[]{:S(2)}) collective-permute-start(f32[24,8,128]{2,1,0:T(8,128)S(1)} %pad_maximum_fusion), channel_id=1, source_target_pairs={{0,8},{8,0},{16,24},{24,16},{1,9},{9,1},{17,25},{25,17},{2,10},{10... | collective-permute-start | bytes 294920 | tf_op jit(solution)/shard_map/ppermute | solution.py:279
  13.4 2.8 %collective-permute-done.2 = f32[24,8,128]{2,1,0:T(8,128)S(1)} collective-permute-done((f32[24,8,128]{2,1,0:T(8,128)S(1)}, f32[24,8,128]{2,1,0:T(8,128)S(1)}, u32[]{:S(2)}, u32[]{:S(2)}) %collective-permute-start.2) | collective-permute-done | bytes 98336 | tf_op jit(solution)/shard_map/ppermute | solution.py:279
  16.3 0.0 copy-start
  16.3 0.0 copy-start.1
  16.3 2.9 %collective-permute-start.3 = (f32[24,8,128]{2,1,0:T(8,128)S(1)}, f32[24,8,128]{2,1,0:T(8,128)S(1)}, u32[]{:S(2)}, u32[]{:S(2)}) collective-permute-start(f32[24,8,128]{2,1,0:T(8,128)S(1)} %fusion), channel_id=1, source_target_pairs={{0,16},{8,24},{16,0},{24,8},{1,17},{9,25},{17,1},{25,9},{2,18},{10... | collective-permute-start | bytes 294920 | tf_op jit(solution)/shard_map/ppermute | solution.py:279
  19.2 2.7 %collective-permute-done.3 = f32[24,8,128]{2,1,0:T(8,128)S(1)} collective-permute-done((f32[24,8,128]{2,1,0:T(8,128)S(1)}, f32[24,8,128]{2,1,0:T(8,128)S(1)}, u32[]{:S(2)}, u32[]{:S(2)}) %collective-permute-start.3) | collective-permute-done | bytes 98336 | tf_op jit(solution)/shard_map/ppermute | solution.py:279
  21.9 1.8 %collective-permute-start.4 = (f32[1,24,8,128]{3,2,1,0:T(8,128)S(1)}, f32[1,24,8,128]{3,2,1,0:T(8,128)S(1)}, u32[]{:S(2)}, u32[]{:S(2)}) collective-permute-start(f32[1,24,8,128]{3,2,1,0:T(8,128)S(1)} %add_bitcast_fusion.near_ref), channel_id=1, source_target_pairs={{0,1},{1,0},{2,3},{3,2},{4,5},{5,4},{6,7},{7,6},{8,9},{9,8},{10,11... | collective-permute-start | bytes 294920 | tf_op jit(solution)/shard_map/ppermute | solution.py:279
  23.7 2.9 %collective-permute-done.4.far_ref = f32[1,24,8,128]{3,2,1,0:T(8,128)S(1)} collective-permute-done((f32[1,24,8,128]{3,2,1,0:T(8,128)S(1)}, f32[1,24,8,128]{3,2,1,0:T(8,128)S(1)}, u32[]{:S(2)}, u32[]{:S(2)}) %collective-permute-start.4) | collective-permute-done | bytes 98336 | tf_op jit(solution)/shard_map/ppermute | solution.py:279
  26.6 0.0 copy-done
  26.6 0.0 copy-done.1
  26.6 1.5 %shard_map.114 = (f32[4,3,8,128]{3,2,1,0:T(8,128)S(1)}, f32[1,8,128]{2,1,0:T(8,128)S(1)}) custom-call(f32[3,3]{1,0:T(4,128)S(1)} %copy-done, f32[2,2]{1,0:T(2,128)S(1)} %copy-done.1, f32[1,24,8,128]{3,2,1,0:T(8,128)S(1)} %add_bitcast_fusion.near_ref, f32[1,24,8,128]{3,2,1,0:T(8,128)S(1)} %collective-permute-done.4.far_ref), custom_call_target="tpu_custom_call" | custom-call | tf_op jit(solution)/shard_map/pallas_call | solution.py:329
  28.1 1.8 %collective-permute-start.5 = (f32[1,8,128]{2,1,0:T(8,128)S(1)}, f32[1,8,128]{2,1,0:T(8,128)S(1)}, u32[]{:S(2)}, u32[]{:S(2)}) collective-permute-start(f32[1,8,128]{2,1,0:T(8,128)S(1)} %get-tuple-element.11.mine_ref), channel_id=1, source_target_pairs={{0,4},{2,6},{4,0},{6,2},{1,5},{3,7},{5,1},{7,3},{8,12},{10,14},{12... | collective-permute-start | bytes 12296 | tf_op jit(solution)/shard_map/ppermute | solution.py:279
  29.9 1.9 %collective-permute-done.5 = f32[1,8,128]{2,1,0:T(8,128)S(1)} collective-permute-done((f32[1,8,128]{2,1,0:T(8,128)S(1)}, f32[1,8,128]{2,1,0:T(8,128)S(1)}, u32[]{:S(2)}, u32[]{:S(2)}) %collective-permute-start.5) | collective-permute-done | bytes 4128 | tf_op jit(solution)/shard_map/ppermute | solution.py:279
  31.7 0.0 collective-permute-start.6
  31.7 1.2 %collective-permute-done.6.far_ref = f32[2,8,128]{2,1,0:T(8,128)S(1)} collective-permute-done((f32[2,8,128]{2,1,0:T(8,128)S(1)}, f32[2,8,128]{2,1,0:T(8,128)S(1)}, u32[]{:S(2)}, u32[]{:S(2)}) %collective-permute-start.6) | collective-permute-done | bytes 8224 | tf_op jit(solution)/shard_map/ppermute | solution.py:279
  32.9 0.6 %shard_map.115 = (f32[1,3,1,8,128]{4,3,2,1,0:T(8,128)}, f32[1,3,1,8,128]{4,3,2,1,0:T(8,128)}) custom-call(f32[4,3,8,128]{3,2,1,0:T(8,128)S(1)} %get-tuple-element.10.own_ref, f32[1,8,128]{2,1,0:T(8,128)S(1)} %get-tuple-element.11.mine_ref, f32[2,8,128]{2,1,0:T(8,128)S(1)} %constant_dynamic-update-slice_fusion.near_ref, ...), custom_call_target="tpu_custom_call" | custom-call | tf_op jit(solution)/shard_map/pallas_call | solution.py:343
  (9 shorter events, 0.1 us)
Async XLA Ops:
  4.3 1.5 %collective-permute-start = (f32[36,8,128]{2,1,0:T(8,128)S(1)}, f32[36,8,128]{2,1,0:T(8,128)S(1)}, u32[]{:S(2)}, u32[]{:S(2)}) collective-permute-start(f32[36,8,128]{2,1,0:T(8,128)S(1)} %get-tuple-element.8), channel_id=1, source_target_pairs={{0,2},{2,0},{4,6},{6,4},{1,3},{3,1},{5,7},{7,5},{8,10},{10,8},{12,... | collective-permute-start | bytes 442376 | tf_op jit(solution)/shard_map/ppermute | solution.py:279
  5.8 5.7 %collective-permute-start.1 = (f32[20,8,128]{2,1,0:T(8,128)S(1)}, f32[20,8,128]{2,1,0:T(8,128)S(1)}, u32[]{:S(2)}, u32[]{:S(2)}) collective-permute-start(f32[20,8,128]{2,1,0:T(8,128)S(1)} %concatenate.12), channel_id=1, source_target_pairs={{0,4},{2,6},{4,0},{6,2},{1,5},{3,7},{5,1},{7,3},{8,12},{10,14},{12... | collective-permute-start | bytes 245768 | tf_op jit(solution)/shard_map/ppermute | solution.py:279
  11.6 4.7 %collective-permute-start.2 = (f32[24,8,128]{2,1,0:T(8,128)S(1)}, f32[24,8,128]{2,1,0:T(8,128)S(1)}, u32[]{:S(2)}, u32[]{:S(2)}) collective-permute-start(f32[24,8,128]{2,1,0:T(8,128)S(1)} %pad_maximum_fusion), channel_id=1, source_target_pairs={{0,8},{8,0},{16,24},{24,16},{1,9},{9,1},{17,25},{25,17},{2,10},{10... | collective-permute-start | bytes 294920 | tf_op jit(solution)/shard_map/ppermute | solution.py:279
  16.3 10.3 %copy-start = (f32[3,3]{1,0:T(4,128)S(1)}, f32[3,3]{1,0:T(4,128)}, u32[]{:S(2)}) copy-start(f32[3,3]{1,0:T(4,128)} %cov_ref.1) | copy-start | bytes 112
  16.3 10.3 %copy-start.1 = (f32[2,2]{1,0:T(2,128)S(1)}, f32[2,2]{1,0:T(2,128)}, u32[]{:S(2)}) copy-start(f32[2,2]{1,0:T(2,128)} %metric_ref.1) | copy-start | bytes 52
  16.3 5.6 %collective-permute-start.3 = (f32[24,8,128]{2,1,0:T(8,128)S(1)}, f32[24,8,128]{2,1,0:T(8,128)S(1)}, u32[]{:S(2)}, u32[]{:S(2)}) collective-permute-start(f32[24,8,128]{2,1,0:T(8,128)S(1)} %fusion), channel_id=1, source_target_pairs={{0,16},{8,24},{16,0},{24,8},{1,17},{9,25},{17,1},{25,9},{2,18},{10... | collective-permute-start | bytes 294920 | tf_op jit(solution)/shard_map/ppermute | solution.py:279
  21.9 4.7 %collective-permute-start.4 = (f32[1,24,8,128]{3,2,1,0:T(8,128)S(1)}, f32[1,24,8,128]{3,2,1,0:T(8,128)S(1)}, u32[]{:S(2)}, u32[]{:S(2)}) collective-permute-start(f32[1,24,8,128]{3,2,1,0:T(8,128)S(1)} %add_bitcast_fusion.near_ref), channel_id=1, source_target_pairs={{0,1},{1,0},{2,3},{3,2},{4,5},{5,4},{6,7},{7,6},{8,9},{9,8},{10,11... | collective-permute-start | bytes 294920 | tf_op jit(solution)/shard_map/ppermute | solution.py:279
  28.1 3.7 %collective-permute-start.5 = (f32[1,8,128]{2,1,0:T(8,128)S(1)}, f32[1,8,128]{2,1,0:T(8,128)S(1)}, u32[]{:S(2)}, u32[]{:S(2)}) collective-permute-start(f32[1,8,128]{2,1,0:T(8,128)S(1)} %get-tuple-element.11.mine_ref), channel_id=1, source_target_pairs={{0,4},{2,6},{4,0},{6,2},{1,5},{3,7},{5,1},{7,3},{8,12},{10,14},{12... | collective-permute-start | bytes 12296 | tf_op jit(solution)/shard_map/ppermute | solution.py:279
  31.7 1.2 %collective-permute-start.6 = (f32[2,8,128]{2,1,0:T(8,128)S(1)}, f32[2,8,128]{2,1,0:T(8,128)S(1)}, u32[]{:S(2)}, u32[]{:S(2)}) collective-permute-start(f32[2,8,128]{2,1,0:T(8,128)S(1)} %constant_dynamic-update-slice_fusion.near_ref), channel_id=1, source_target_pairs={{0,2},{2,0},{4,6},{6,4},{1,3},{3,1},{5,7},{7,5},{8,10},{10,8},{12,... | collective-permute-start | bytes 24584 | tf_op jit(solution)/shard_map/ppermute | solution.py:279

commit v4 on v3

--- a/solution.py
+++ b/solution.py
@@ -7,7 +7,7 @@
 from jax.experimental.pallas import tpu as pltpu
 from jax.sharding import PartitionSpec as P
 
-GROUP = 8
+GROUP = 64
 SIDES = 4
 INPUTS = 8
 ALL = ("lat", "lon", "tm")
@@ -34,8 +34,8 @@
 
 
 def tile_kernel(*refs):
-    arguments, (keep_ref, send_ref, planes_ref, tiles) = refs[:INPUTS], refs[INPUTS : INPUTS + 4]
-    local, arrived = refs[INPUTS + 4 : -1], refs[-1]
+    arguments, (keep_ref, send_ref, planes_ref, tiles, packed) = refs[:INPUTS], refs[INPUTS : INPUTS + 5]
+    local, arrived = refs[INPUTS + 5 : -1], refs[-1]
     owner_ref, count_ref, table_ref, values_ref, weight_ref, cells_ref, class_ref, land_ref = local
     copies = [pltpu.make_async_copy(a, b, arrived.at[k]) for k, (a, b) in enumerate(zip(arguments, local))]
     for copy in copies:
@@ -59,37 +59,44 @@
     row_ids = lax.broadcasted_iota(jnp.int32, (rows, slots), 0)
     col_ids = lax.broadcasted_iota(jnp.int32, (cols, slots), 0)
 
-    def block_sum(block):
+    nothing = jnp.zeros((2 * stats * rows, slots), jnp.bfloat16)
+
+    def operands(block):
         live = jnp.where(lane < count_ref[block], weight_ref[pl.ds(block, 1), :], 0.0)
         cells = cells_ref[pl.ds(block, 1), :]
         row_hit = row_ids == cells // cols
         terms = [live] + [live * values_ref[v, pl.ds(block, 1), :] for v in range(variables)]
-        spread = jnp.concatenate([jnp.where(row_hit, term, 0.0) for term in terms], axis=0)
-        high = spread.astype(jnp.bfloat16)
-        low = (spread - high.astype(jnp.float32)).astype(jnp.bfloat16)
-        col_hot = jnp.where(col_ids == cells % cols, 1.0, 0.0).astype(jnp.bfloat16)
+        high = [term.astype(jnp.bfloat16).astype(jnp.float32) for term in terms]
+        low = [term - part for term, part in zip(terms, high)]
+        spread = jnp.concatenate([jnp.where(row_hit, part, 0.0) for part in high + low], axis=0)
+        return spread.astype(jnp.bfloat16), jnp.where(col_ids == cells % cols, 1.0, 0.0).astype(jnp.bfloat16)
+
+    def pair_sums(block):
+        (first, first_hot), (second, second_hot) = operands(block), operands(block + 1)
         both = lax.dot_general(
-            jnp.concatenate([high, low], axis=0),
-            col_hot,
+            jnp.concatenate([jnp.concatenate([first, nothing], axis=1), jnp.concatenate([nothing, second], axis=1)], axis=0),
+            jnp.concatenate([first_hot, second_hot], axis=1),
             (((1,), (1,)), ((), ())),
             preferred_element_type=jnp.float32,
-        )
-        return (both[: stats * rows] + both[stats * rows :]).reshape(stats, rows, cols)
+        ).reshape(2, 2, stats, rows, cols)
+        return [both[0, 0] + both[0, 1], both[1, 0] + both[1, 1]]
 
     def step(group, carry):
-        sums = [block_sum(group * GROUP + k) for k in range(GROUP)]
+        sums = []
+        for k in range(0, GROUP, 2):
+            sums += pair_sums(group * GROUP + k)
         for k in range(GROUP):
             owner = owner_ref[group * GROUP + k]
             tiles[jnp.bitwise_xor(owner % n_lon, lon), owner // n_lon] += sums[k]
         return carry
 
     lax.fori_loop(0, block_total // GROUP, step, 0)
+    own_tiles = stats * n_lat
     for m in range(n_lon // 2):
         for i in range(n_lat):
             for s in range(stats):
-                spot = (m * stats + s) * n_lat + i
-                keep_ref[spot] = tiles[2 * m, i, s]
-                send_ref[spot] = tiles[2 * m + 1, i, s]
+                keep_ref[m, s * n_lat + i] = tiles[2 * m, i, s]
+                send_ref[m, s * n_lat + i] = tiles[2 * m + 1, i, s]
 
     height = n_lat * rows
     lanes = SIDES * height
@@ -97,34 +104,33 @@
     row = lax.broadcasted_iota(jnp.int32, (height, lanes), 0)
     at_row = lax.broadcasted_iota(jnp.int32, (height, lanes), 1) % height == row
     own_row = lax.broadcasted_iota(jnp.int32, (rows, lanes), 1) % height == lax.broadcasted_iota(jnp.int32, (rows, lanes), 0) + lat * rows
-    first = n_lon // 2 * stats * n_lat
-    chunks = lanes // cols
+    blank = jnp.zeros((1, lanes), jnp.float32)
     for offset in range(n_lon):
         picked = exact_dot(jnp.concatenate([tiles[offset, i, s] for s in range(stats) for i in range(n_lat)], axis=0), edges)
-        packed = [
-            jnp.sum(jnp.where(at_row, picked[s * height : (s + 1) * height], 0.0), axis=0, keepdims=True) for s in range(stats)
-        ]
-        blank = jnp.zeros((1, lanes), jnp.float32)
-        shared = jnp.sum(jnp.where(own_row, exact_dot(plane, edges), 0.0), axis=0, keepdims=True) if offset == 0 else blank
-        packed = jnp.concatenate(packed + [shared] + [blank] * (rows - stats - 1), axis=0)
-        for c in range(chunks):
-            spot = first + jnp.bitwise_xor(lon, offset) * chunks + c
-            keep_ref[spot] = packed[:, c * cols : (c + 1) * cols]
-            send_ref[spot] = packed[:, c * cols : (c + 1) * cols]
+        rows_of = [jnp.where(at_row, picked[s * height : (s + 1) * height], 0.0) for s in range(stats)]
+        rows_of.append(jnp.where(own_row, exact_dot(plane, edges), 0.0) if offset == 0 else blank)
+        sums = [jnp.sum(x, axis=0, keepdims=True) for x in rows_of]
+        packed[offset] = jnp.concatenate(sums + [blank] * (rows - stats - 1), axis=0)
+    from_after = lax.broadcasted_iota(jnp.int32, (rows, lanes), 1) < 2 * height
+    for offset in range(n_lon):
+        target = jnp.bitwise_xor(lon, offset)
+        after = jnp.bitwise_xor(lon, lax.rem(target + 1, n_lon))
+        before = jnp.bitwise_xor(lon, lax.rem(target + n_lon - 1, n_lon))
+        beside = jnp.where(from_after, packed[after], packed[before])
+        out_ref = send_ref if offset % 2 else keep_ref
+        for c in range(lanes // cols):
+            out_ref[offset // 2, own_tiles + c] = beside[:, c * cols : (c + 1) * cols]
 
 
 def strip_kernel(offsets, cov_ref, metric_ref, near_ref, far_ref, own_ref, sums_ref, right, image, change, diag, coef, shared):
     rows, cols = near_ref.shape[2:]
     n_tm, variables, height, width = right.shape
     stats, n_lat, lanes = variables + 1, height // rows, SIDES * height
-    lat, lon, tm = lax.axis_index("lat"), lax.axis_index("lon"), lax.axis_index("tm")
-    n_lon = lax.axis_size("lon")
+    lat, tm = lax.axis_index("lat"), lax.axis_index("tm")
     chunks = lanes // cols
-    first = (stats + 1) * n_lat
-    after, before = lax.rem(lon + 1, n_lon), lax.rem(lon + n_lon - 1, n_lon)
+    first = stats * n_lat
     lane = lax.broadcasted_iota(jnp.int32, (height, lanes), 1)
     at_row = lane % height == lax.broadcasted_iota(jnp.int32, (height, lanes), 0)
-    from_after = lax.broadcasted_iota(jnp.int32, (rows, lanes), 1) < 2 * height
     side = lax.broadcasted_iota(jnp.int32, (lanes, cols), 0) // height
     column = lax.broadcasted_iota(jnp.int32, (lanes, cols), 1)
     targets = jnp.where(column == side_column(side, cols), 1.0, 0.0).astype(jnp.bfloat16)
@@ -136,12 +142,9 @@
             diag[t, down, :cols] = part_ref[part, i]
             for v in range(variables):
                 right[t, v, down, :cols] = part_ref[part, (v + 1) * n_lat + i]
-            shared[t, down, :cols] = part_ref[part, stats * n_lat + i]
-
-        def packed(j):
-            return jnp.concatenate([part_ref[part, first + j * chunks + c] for c in range(chunks)], axis=1)
-
-        beside = jnp.where(from_after, packed(after), packed(before))
+            shared[t, down, :cols] = part_ref[part, first + chunks + i]
+
+        beside = jnp.concatenate([part_ref[part, first + c] for c in range(chunks)], axis=1)
         spread = jnp.concatenate([jnp.where(at_row, beside[s : s + 1], 0.0) for s in range(stats + 1)], axis=0)
         columns = exact_dot(spread, targets)
         diag[t, :, cols:] = columns[:height]
@@ -294,8 +297,7 @@
     stats = variables + 1
     vmem, smem = pl.BlockSpec(memory_space=pltpu.VMEM), pl.BlockSpec(memory_space=pltpu.SMEM)
     height = n_lat * rows
-    halo = n_lon * SIDES * height // cols
-    half = jax.ShapeDtypeStruct((n_lon // 2 * stats * n_lat + halo, rows, cols), jnp.float32)
+    half = jax.ShapeDtypeStruct((n_lon // 2, stats * n_lat + SIDES * height // cols, rows, cols), jnp.float32)
     values = obs_values.transpose(1, 0, 2)
     arguments = (block_owner[:, 0], obs_count, coef_table, values, obs_weight, obs_cells, class_ids, land_mask)
     places = [pltpu.SMEM] * 3 + [pltpu.VMEM] * 5
@@ -306,6 +308,7 @@
         out_specs=(vmem, vmem, vmem),
         scratch_shapes=[
             pltpu.VMEM((n_lon, n_lat, stats, rows, cols), jnp.float32),
+            pltpu.VMEM((n_lon, rows, SIDES * height), jnp.float32),
             *[place(x.shape, x.dtype) for place, x in zip(places, arguments)],
             pltpu.SemaphoreType.DMA((INPUTS,)),
         ],
@@ -313,13 +316,9 @@
     )(*[pltpu.with_memory_space_constraint(x, pltpu.HBM) for x in arguments])
 
     partial = keep + swapped(send, "lon", 1)
-    body, sides = partial[:-halo].reshape(n_lon // 2, stats * n_lat, rows, cols), partial[-halo:]
     for bit in bits(n_lon)[1:]:
-        count = body.shape[0] // 2
-        given = swapped(jnp.concatenate([body[1::2].reshape(-1, rows, cols), sides], axis=0), "lon", bit)
-        body = body[0::2] + given[:-halo].reshape(count, stats * n_lat, rows, cols)
-        sides = sides + given[-halo:]
-    strip = jnp.concatenate([body[0], planes, sides], axis=0)
+        partial = partial[0::2] + swapped(partial[1::2], "lon", bit)
+    strip = jnp.concatenate([partial[0], planes], axis=0)
     for bit in bits(n_lat):
         strip = strip + swapped(strip, "lat", bit)
 

time: 33.8 us -> 31.8 us (0.941)
  Pallas kernels: 5.77 us -> 4.49 us
  waiting for transfers between devices: 15.2 us -> 14.3 us
    pallas_call x1, Pallas kernels: 3.63 us -> 2.36 us  [per_device(): pl.pallas_call(tile_kernel, out_shape=(half, half, jax.ShapeDtypeStruct((...]
    ppermute x7, waiting for transfers between devices: 15.2 us -> 14.3 us  [swapped(): lax.ppermute(x, axis, [(i, i ^ bit) for i in range(lax.axis_size(axis))])]
where the time goes in v4:
time: 31.8 us; the launch traced here: 31.6 us
  waiting for transfers between devices  14.3 us (45%)
  starting transfers between devices  12 us (38%)
  Pallas kernels  4.49 us (14%)
  between operations  0.69 us (2%)
    ppermute x7, waiting for transfers between devices, swapped(): lax.ppermute(x, axis, [(i, i ^ bit) for i in range(lax.axis_size(axis))])  14.3 us
    ppermute x7, starting transfers between devices, swapped(): lax.ppermute(x, axis, [(i, i ^ bit) for i in range(lax.axis_size(axis))])  12 us
    pallas_call x1, Pallas kernels, per_device(): pl.pallas_call(tile_kernel, out_shape=(half, half, jax.ShapeDtypeStruct((...  2.36 us
    pallas_call x1, Pallas kernels, per_device(): pl.pallas_call(functools.partial(strip_kernel, offsets), out_shape=(jax.S...  1.49 us
    pallas_call x1, Pallas kernels, per_device(): pl.pallas_call(update_kernel, out_shape=(out, out), in_specs=[vmem] * 4,...  0.65 us
  transfers between devices with their start and end apart: 7, of which 7 were waited for; matrix products, arithmetic and copies ran while one was open for 0% of the time, Pallas kernels for 0%

profile of v4, /device:TPU:0, one launch (start us, length us, event | category | flops | bytes accessed | tf_op | source)
XLA Modules:
  0.0 31.6 jit_solution(7611365776642508336)
XLA Ops:
  0.6 2.4 %shard_map.113 = (f32[2,17,8,128]{3,2,1,0:T(8,128)S(1)}, f32[2,17,8,128]{3,2,1,0:T(8,128)S(1)}, f32[4,8,128]{2,1,0:T(8,128)S(1)}) custom-call(s32[64]{0:T(128)} %bitcast.7, s32[64]{0:T(128)} %refs_1_.1, f32[8]{0:T(128)} %refs_2_.1, f32[3,64,128]{2,1,0:T(8,128)} %bitcast.6, f32[64,128]{1,0:T(8,128)} %refs_4_.1, s32[64,128]{1,0:T(8,128)} %refs_5_.1, ...), custom_call_target="tpu_custom_call" | custom-call | tf_op jit(solution)/shard_map/pallas_call | solution.py:304
  3.0 0.5 %collective-permute-start = (f32[2,17,8,128]{3,2,1,0:T(8,128)S(1)}, f32[2,17,8,128]{3,2,1,0:T(8,128)S(1)}, u32[]{:S(2)}, u32[]{:S(2)}) collective-permute-start(f32[2,17,8,128]{3,2,1,0:T(8,128)S(1)} %get-tuple-element.8), channel_id=1, source_target_pairs={{0,2},{2,0},{4,6},{6,4},{1,3},{3,1},{5,7},{7,5},{8,10},{10,8},{12,... | collective-permute-start | bytes 417800 | tf_op jit(solution)/shard_map/ppermute | solution.py:282
  3.5 1.0 %collective-permute-done = f32[2,17,8,128]{3,2,1,0:T(8,128)S(1)} collective-permute-done((f32[2,17,8,128]{3,2,1,0:T(8,128)S(1)}, f32[2,17,8,128]{3,2,1,0:T(8,128)S(1)}, u32[]{:S(2)}, u32[]{:S(2)}) %collective-permute-start) | collective-permute-done | bytes 139296 | tf_op jit(solution)/shard_map/ppermute | solution.py:282
  4.5 3.0 %collective-permute-start.1 = (f32[1,17,8,128]{3,2,1,0:T(8,128)S(1)}, f32[1,17,8,128]{3,2,1,0:T(8,128)S(1)}, u32[]{:S(2)}, u32[]{:S(2)}) collective-permute-start(f32[1,17,8,128]{3,2,1,0:T(8,128)S(1)} %slice.11), channel_id=1, source_target_pairs={{0,4},{2,6},{4,0},{6,2},{1,5},{3,7},{5,1},{7,3},{8,12},{10,14},{12... | collective-permute-start | bytes 208904 | tf_op jit(solution)/shard_map/ppermute | solution.py:282
  7.5 2.5 %collective-permute-done.1 = f32[1,17,8,128]{3,2,1,0:T(8,128)S(1)} collective-permute-done((f32[1,17,8,128]{3,2,1,0:T(8,128)S(1)}, f32[1,17,8,128]{3,2,1,0:T(8,128)S(1)}, u32[]{:S(2)}, u32[]{:S(2)}) %collective-permute-start.1) | collective-permute-done | bytes 69664 | tf_op jit(solution)/shard_map/ppermute | solution.py:282
  10.0 1.9 %collective-permute-start.2 = (f32[21,8,128]{2,1,0:T(8,128)S(1)}, f32[21,8,128]{2,1,0:T(8,128)S(1)}, u32[]{:S(2)}, u32[]{:S(2)}) collective-permute-start(f32[21,8,128]{2,1,0:T(8,128)S(1)} %pad_maximum_fusion), channel_id=1, source_target_pairs={{0,8},{8,0},{16,24},{24,16},{1,9},{9,1},{17,25},{25,17},{2,10},{10... | collective-permute-start | bytes 258056 | tf_op jit(solution)/shard_map/ppermute | solution.py:282
  11.9 2.6 %collective-permute-done.2 = f32[21,8,128]{2,1,0:T(8,128)S(1)} collective-permute-done((f32[21,8,128]{2,1,0:T(8,128)S(1)}, f32[21,8,128]{2,1,0:T(8,128)S(1)}, u32[]{:S(2)}, u32[]{:S(2)}) %collective-permute-start.2) | collective-permute-done | bytes 86048 | tf_op jit(solution)/shard_map/ppermute | solution.py:282
  14.6 0.0 copy-start
  14.6 0.0 copy-start.1
  14.6 2.9 %collective-permute-start.3 = (f32[21,8,128]{2,1,0:T(8,128)S(1)}, f32[21,8,128]{2,1,0:T(8,128)S(1)}, u32[]{:S(2)}, u32[]{:S(2)}) collective-permute-start(f32[21,8,128]{2,1,0:T(8,128)S(1)} %fusion.1), channel_id=1, source_target_pairs={{0,16},{8,24},{16,0},{24,8},{1,17},{9,25},{17,1},{25,9},{2,18},{10... | collective-permute-start | bytes 258056 | tf_op jit(solution)/shard_map/ppermute | solution.py:282
  17.5 2.5 %collective-permute-done.3 = f32[21,8,128]{2,1,0:T(8,128)S(1)} collective-permute-done((f32[21,8,128]{2,1,0:T(8,128)S(1)}, f32[21,8,128]{2,1,0:T(8,128)S(1)}, u32[]{:S(2)}, u32[]{:S(2)}) %collective-permute-start.3) | collective-permute-done | bytes 86048 | tf_op jit(solution)/shard_map/ppermute | solution.py:282
  20.1 1.9 %collective-permute-start.4 = (f32[1,21,8,128]{3,2,1,0:T(8,128)S(1)}, f32[1,21,8,128]{3,2,1,0:T(8,128)S(1)}, u32[]{:S(2)}, u32[]{:S(2)}) collective-permute-start(f32[1,21,8,128]{3,2,1,0:T(8,128)S(1)} %add_bitcast_fusion.near_ref), channel_id=1, source_target_pairs={{0,1},{1,0},{2,3},{3,2},{4,5},{5,4},{6,7},{7,6},{8,9},{9,8},{10,11... | collective-permute-start | bytes 258056 | tf_op jit(solution)/shard_map/ppermute | solution.py:282
  21.9 2.7 %collective-permute-done.4.far_ref = f32[1,21,8,128]{3,2,1,0:T(8,128)S(1)} collective-permute-done((f32[1,21,8,128]{3,2,1,0:T(8,128)S(1)}, f32[1,21,8,128]{3,2,1,0:T(8,128)S(1)}, u32[]{:S(2)}, u32[]{:S(2)}) %collective-permute-start.4) | collective-permute-done | bytes 86048 | tf_op jit(solution)/shard_map/ppermute | solution.py:282
  24.6 0.0 copy-done
  24.6 0.0 copy-done.1
  24.6 1.5 %shard_map.114 = (f32[4,3,8,128]{3,2,1,0:T(8,128)S(1)}, f32[1,8,128]{2,1,0:T(8,128)S(1)}) custom-call(f32[3,3]{1,0:T(4,128)S(1)} %copy-done, f32[2,2]{1,0:T(2,128)S(1)} %copy-done.1, f32[1,21,8,128]{3,2,1,0:T(8,128)S(1)} %add_bitcast_fusion.near_ref, f32[1,21,8,128]{3,2,1,0:T(8,128)S(1)} %collective-permute-done.4.far_ref), custom_call_target="tpu_custom_call" | custom-call | tf_op jit(solution)/shard_map/pallas_call | solution.py:328
  26.1 1.9 %collective-permute-start.5 = (f32[1,8,128]{2,1,0:T(8,128)S(1)}, f32[1,8,128]{2,1,0:T(8,128)S(1)}, u32[]{:S(2)}, u32[]{:S(2)}) collective-permute-start(f32[1,8,128]{2,1,0:T(8,128)S(1)} %get-tuple-element.11.mine_ref), channel_id=1, source_target_pairs={{0,4},{2,6},{4,0},{6,2},{1,5},{3,7},{5,1},{7,3},{8,12},{10,14},{12... | collective-permute-start | bytes 12296 | tf_op jit(solution)/shard_map/ppermute | solution.py:282
  28.0 1.8 %collective-permute-done.5 = f32[1,8,128]{2,1,0:T(8,128)S(1)} collective-permute-done((f32[1,8,128]{2,1,0:T(8,128)S(1)}, f32[1,8,128]{2,1,0:T(8,128)S(1)}, u32[]{:S(2)}, u32[]{:S(2)}) %collective-permute-start.5) | collective-permute-done | bytes 4128 | tf_op jit(solution)/shard_map/ppermute | solution.py:282
  29.8 0.0 collective-permute-start.6
  29.8 1.2 %collective-permute-done.6.far_ref = f32[2,8,128]{2,1,0:T(8,128)S(1)} collective-permute-done((f32[2,8,128]{2,1,0:T(8,128)S(1)}, f32[2,8,128]{2,1,0:T(8,128)S(1)}, u32[]{:S(2)}, u32[]{:S(2)}) %collective-permute-start.6) | collective-permute-done | bytes 8224 | tf_op jit(solution)/shard_map/ppermute | solution.py:282
  31.0 0.6 %shard_map.115 = (f32[1,3,1,8,128]{4,3,2,1,0:T(8,128)}, f32[1,3,1,8,128]{4,3,2,1,0:T(8,128)}) custom-call(f32[4,3,8,128]{3,2,1,0:T(8,128)S(1)} %get-tuple-element.10.own_ref, f32[1,8,128]{2,1,0:T(8,128)S(1)} %get-tuple-element.11.mine_ref, f32[2,8,128]{2,1,0:T(8,128)S(1)} %constant_dynamic-update-slice_fusion.near_ref, ...), custom_call_target="tpu_custom_call" | custom-call | tf_op jit(solution)/shard_map/pallas_call | solution.py:342
  (8 shorter events, 0.1 us)
Async XLA Ops:
  3.0 1.5 %collective-permute-start = (f32[2,17,8,128]{3,2,1,0:T(8,128)S(1)}, f32[2,17,8,128]{3,2,1,0:T(8,128)S(1)}, u32[]{:S(2)}, u32[]{:S(2)}) collective-permute-start(f32[2,17,8,128]{3,2,1,0:T(8,128)S(1)} %get-tuple-element.8), channel_id=1, source_target_pairs={{0,2},{2,0},{4,6},{6,4},{1,3},{3,1},{5,7},{7,5},{8,10},{10,8},{12,... | collective-permute-start | bytes 417800 | tf_op jit(solution)/shard_map/ppermute | solution.py:282
  4.5 5.5 %collective-permute-start.1 = (f32[1,17,8,128]{3,2,1,0:T(8,128)S(1)}, f32[1,17,8,128]{3,2,1,0:T(8,128)S(1)}, u32[]{:S(2)}, u32[]{:S(2)}) collective-permute-start(f32[1,17,8,128]{3,2,1,0:T(8,128)S(1)} %slice.11), channel_id=1, source_target_pairs={{0,4},{2,6},{4,0},{6,2},{1,5},{3,7},{5,1},{7,3},{8,12},{10,14},{12... | collective-permute-start | bytes 208904 | tf_op jit(solution)/shard_map/ppermute | solution.py:282
  10.0 4.6 %collective-permute-start.2 = (f32[21,8,128]{2,1,0:T(8,128)S(1)}, f32[21,8,128]{2,1,0:T(8,128)S(1)}, u32[]{:S(2)}, u32[]{:S(2)}) collective-permute-start(f32[21,8,128]{2,1,0:T(8,128)S(1)} %pad_maximum_fusion), channel_id=1, source_target_pairs={{0,8},{8,0},{16,24},{24,16},{1,9},{9,1},{17,25},{25,17},{2,10},{10... | collective-permute-start | bytes 258056 | tf_op jit(solution)/shard_map/ppermute | solution.py:282
  14.6 10.0 %copy-start = (f32[3,3]{1,0:T(4,128)S(1)}, f32[3,3]{1,0:T(4,128)}, u32[]{:S(2)}) copy-start(f32[3,3]{1,0:T(4,128)} %cov_ref.1) | copy-start | bytes 112
  14.6 10.0 %copy-start.1 = (f32[2,2]{1,0:T(2,128)S(1)}, f32[2,2]{1,0:T(2,128)}, u32[]{:S(2)}) copy-start(f32[2,2]{1,0:T(2,128)} %metric_ref.1) | copy-start | bytes 52
  14.6 5.4 %collective-permute-start.3 = (f32[21,8,128]{2,1,0:T(8,128)S(1)}, f32[21,8,128]{2,1,0:T(8,128)S(1)}, u32[]{:S(2)}, u32[]{:S(2)}) collective-permute-start(f32[21,8,128]{2,1,0:T(8,128)S(1)} %fusion.1), channel_id=1, source_target_pairs={{0,16},{8,24},{16,0},{24,8},{1,17},{9,25},{17,1},{25,9},{2,18},{10... | collective-permute-start | bytes 258056 | tf_op jit(solution)/shard_map/ppermute | solution.py:282
  20.1 4.6 %collective-permute-start.4 = (f32[1,21,8,128]{3,2,1,0:T(8,128)S(1)}, f32[1,21,8,128]{3,2,1,0:T(8,128)S(1)}, u32[]{:S(2)}, u32[]{:S(2)}) collective-permute-start(f32[1,21,8,128]{3,2,1,0:T(8,128)S(1)} %add_bitcast_fusion.near_ref), channel_id=1, source_target_pairs={{0,1},{1,0},{2,3},{3,2},{4,5},{5,4},{6,7},{7,6},{8,9},{9,8},{10,11... | collective-permute-start | bytes 258056 | tf_op jit(solution)/shard_map/ppermute | solution.py:282
  26.1 3.7 %collective-permute-start.5 = (f32[1,8,128]{2,1,0:T(8,128)S(1)}, f32[1,8,128]{2,1,0:T(8,128)S(1)}, u32[]{:S(2)}, u32[]{:S(2)}) collective-permute-start(f32[1,8,128]{2,1,0:T(8,128)S(1)} %get-tuple-element.11.mine_ref), channel_id=1, source_target_pairs={{0,4},{2,6},{4,0},{6,2},{1,5},{3,7},{5,1},{7,3},{8,12},{10,14},{12... | collective-permute-start | bytes 12296 | tf_op jit(solution)/shard_map/ppermute | solution.py:282
  29.8 1.2 %collective-permute-start.6 = (f32[2,8,128]{2,1,0:T(8,128)S(1)}, f32[2,8,128]{2,1,0:T(8,128)S(1)}, u32[]{:S(2)}, u32[]{:S(2)}) collective-permute-start(f32[2,8,128]{2,1,0:T(8,128)S(1)} %constant_dynamic-update-slice_fusion.near_ref), channel_id=1, source_target_pairs={{0,2},{2,0},{4,6},{6,4},{1,3},{3,1},{5,7},{7,5},{8,10},{10,8},{12,... | collective-permute-start | bytes 24584 | tf_op jit(solution)/shard_map/ppermute | solution.py:282

commit v5 on v4

--- a/solution.py
+++ b/solution.py
@@ -9,7 +9,7 @@
 
 GROUP = 64
 SIDES = 4
-INPUTS = 8
+INPUTS = 10
 ALL = ("lat", "lon", "tm")
 
 
@@ -34,14 +34,13 @@
 
 
 def tile_kernel(*refs):
-    arguments, (keep_ref, send_ref, planes_ref, tiles, packed) = refs[:INPUTS], refs[INPUTS : INPUTS + 5]
-    local, arrived = refs[INPUTS + 5 : -1], refs[-1]
-    owner_ref, count_ref, table_ref, values_ref, weight_ref, cells_ref, class_ref, land_ref = local
+    arguments, (keep_ref, send_ref, plane_ref, factors_ref, tiles, packed) = refs[:INPUTS], refs[INPUTS : INPUTS + 6]
+    local, arrived = refs[INPUTS + 6 : -1], refs[-1]
+    owner_ref, count_ref, table_ref, cov_ref, metric_ref, values_ref, weight_ref, cells_ref, class_ref, land_ref = local
     copies = [pltpu.make_async_copy(a, b, arrived.at[k]) for k, (a, b) in enumerate(zip(arguments, local))]
     for copy in copies:
         copy.start()
     tiles[...] = jnp.zeros_like(tiles)
-    planes_ref[...] = jnp.zeros_like(planes_ref)
     variables, block_total, slots = values_ref.shape
     n_lon, n_lat, stats, rows, cols = tiles.shape
     lat, lon, tm = lax.axis_index("lat"), lax.axis_index("lon"), lax.axis_index("tm")
@@ -53,7 +52,14 @@
         diffusivity = jnp.where(class_ref[0] == index, table_ref[index], diffusivity)
     sea = land_ref[0].astype(jnp.float32)
     plane = jnp.where(tm == 0, diffusivity, sea)
-    planes_ref[lat] = plane
+    plane_ref[0] = plane
+    months = metric_ref.shape[0]
+    for v in range(variables):
+        for w in range(variables):
+            factors_ref[v * variables + w] = jnp.full(factors_ref.shape[1:], cov_ref[v, w])
+    for t in range(months):
+        for u in range(months):
+            factors_ref[variables * variables + t * months + u] = jnp.full(factors_ref.shape[1:], metric_ref[t, u])
 
     lane = lax.broadcasted_iota(jnp.int32, (1, slots), 1)
     row_ids = lax.broadcasted_iota(jnp.int32, (rows, slots), 0)
@@ -122,7 +128,7 @@
             out_ref[offset // 2, own_tiles + c] = beside[:, c * cols : (c + 1) * cols]
 
 
-def strip_kernel(offsets, cov_ref, metric_ref, near_ref, far_ref, own_ref, sums_ref, right, image, change, diag, coef, shared):
+def strip_kernel(offsets, lat_offsets, factors_ref, near_ref, far_ref, own_ref, sums_ref, right, image, change, diag, coef, shared):
     rows, cols = near_ref.shape[2:]
     n_tm, variables, height, width = right.shape
     stats, n_lat, lanes = variables + 1, height // rows, SIDES * height
@@ -142,7 +148,10 @@
             diag[t, down, :cols] = part_ref[part, i]
             for v in range(variables):
                 right[t, v, down, :cols] = part_ref[part, (v + 1) * n_lat + i]
-            shared[t, down, :cols] = part_ref[part, first + chunks + i]
+
+        for k, offset in enumerate(lat_offsets):
+            down = pl.ds(pl.multiple_of(jnp.bitwise_xor(lat, offset) * rows, rows), rows)
+            shared[t, down, :cols] = part_ref[part, first + chunks + k]
 
         beside = jnp.concatenate([part_ref[part, first + c] for c in range(chunks)], axis=1)
         spread = jnp.concatenate([jnp.where(at_row, beside[s : s + 1], 0.0) for s in range(stats + 1)], axis=0)
@@ -181,9 +190,9 @@
                 here = masked[t][v]
                 mixed = centre * here[:, :span]
                 for w in range(variables):
-                    mixed = mixed + cov_ref[v, w] * masked[t][w][:, :span]
+                    mixed = mixed + factors_ref[v * variables + w, :, :span] * masked[t][w][:, :span]
                 for s in range(n_tm):
-                    mixed = mixed + metric_ref[t, s] * masked[s][v][:, :span]
+                    mixed = mixed + factors_ref[variables * variables + t * n_tm + s, :, :span] * masked[s][v][:, :span]
                 spread = (
                     coef[0, :, :span] * moved(here[:, :span], 0, True)
                     + coef[1, :, :span] * moved(here[:, :span], 0, False)
@@ -295,17 +304,22 @@
     rows, cols = class_ids.shape[1:]
     variables = obs_values.shape[1]
     stats = variables + 1
-    vmem, smem = pl.BlockSpec(memory_space=pltpu.VMEM), pl.BlockSpec(memory_space=pltpu.SMEM)
+    vmem = pl.BlockSpec(memory_space=pltpu.VMEM)
     height = n_lat * rows
     half = jax.ShapeDtypeStruct((n_lon // 2, stats * n_lat + SIDES * height // cols, rows, cols), jnp.float32)
     values = obs_values.transpose(1, 0, 2)
-    arguments = (block_owner[:, 0], obs_count, coef_table, values, obs_weight, obs_cells, class_ids, land_mask)
-    places = [pltpu.SMEM] * 3 + [pltpu.VMEM] * 5
-    keep, send, planes = pl.pallas_call(
+    arguments = (block_owner[:, 0], obs_count, coef_table, cross_cov, time_metric, values, obs_weight, obs_cells, class_ids, land_mask)
+    places = [pltpu.SMEM] * 5 + [pltpu.VMEM] * 5
+    keep, send, planes, factors = pl.pallas_call(
         tile_kernel,
-        out_shape=(half, half, jax.ShapeDtypeStruct((n_lat, rows, cols), jnp.float32)),
+        out_shape=(
+            half,
+            half,
+            jax.ShapeDtypeStruct((1, rows, cols), jnp.float32),
+            jax.ShapeDtypeStruct((variables * variables + n_tm * n_tm, 1, 2 * cols), jnp.float32),
+        ),
         in_specs=[pl.BlockSpec(memory_space=pltpu.HBM)] * INPUTS,
-        out_specs=(vmem, vmem, vmem),
+        out_specs=(vmem,) * 4,
         scratch_shapes=[
             pltpu.VMEM((n_lon, n_lat, stats, rows, cols), jnp.float32),
             pltpu.VMEM((n_lon, rows, SIDES * height), jnp.float32),
@@ -318,24 +332,29 @@
     partial = keep + swapped(send, "lon", 1)
     for bit in bits(n_lon)[1:]:
         partial = partial[0::2] + swapped(partial[1::2], "lon", bit)
-    strip = jnp.concatenate([partial[0], planes], axis=0)
+    summed, lat_offsets = partial[0], [0]
+    count = summed.shape[0]
     for bit in bits(n_lat):
-        strip = strip + swapped(strip, "lat", bit)
+        given = swapped(jnp.concatenate([summed, planes], axis=0), "lat", bit)
+        summed = summed + given[:count]
+        planes = jnp.concatenate([planes, given[count:]], axis=0)
+        lat_offsets = lat_offsets + [i + bit for i in lat_offsets]
+    strip = jnp.concatenate([summed, planes], axis=0)
 
     near, far, offsets = gathered(strip, "tm")
     field = pltpu.VMEM((n_tm, variables, height, 2 * cols), jnp.float32)
     plane = pltpu.VMEM((n_tm, height, 2 * cols), jnp.float32)
     own, sums = pl.pallas_call(
-        functools.partial(strip_kernel, offsets),
+        functools.partial(strip_kernel, offsets, lat_offsets),
         out_shape=(
             jax.ShapeDtypeStruct((4, variables, rows, cols), jnp.float32),
             jax.ShapeDtypeStruct((1, rows, cols), jnp.float32),
         ),
-        in_specs=[smem, smem, vmem, vmem],
+        in_specs=[vmem] * 3,
         out_specs=(vmem, vmem),
         scratch_shapes=[field, field, field, plane, pltpu.VMEM((5, height, 2 * cols), jnp.float32), plane],
         compiler_params=pltpu.CompilerParams(vmem_limit_bytes=24 * 1024 * 1024),
-    )(cross_cov, time_metric, near, far)
+    )(factors, near, far)
 
     near, far, _ = gathered(sums[0], "lon")
     out = jax.ShapeDtypeStruct((1, variables, 1, rows, cols), jnp.float32)

time: 31.8 us -> 30.9 us (0.972)
  Pallas kernels: 4.49 us -> 3.86 us
    pallas_call x1, Pallas kernels: 1.49 us -> 0.92 us  [per_device(): pl.pallas_call(functools.partial(strip_kernel, offsets, lat_offsets), out...]
where the time goes in v5:
time: 30.9 us; the launch traced here: 30.8 us
  waiting for transfers between devices  14 us (45%)
  starting transfers between devices  12.1 us (39%)
  Pallas kernels  3.86 us (12%)
  between operations  0.71 us (2%)
    ppermute x7, waiting for transfers between devices, swapped(): lax.ppermute(x, axis, [(i, i ^ bit) for i in range(lax.axis_size(axis))])  14 us
    ppermute x7, starting transfers between devices, swapped(): lax.ppermute(x, axis, [(i, i ^ bit) for i in range(lax.axis_size(axis))])  12.1 us
    pallas_call x1, Pallas kernels, per_device(): pl.pallas_call(tile_kernel, out_shape=(half, half, jax.ShapeDtypeStruct((...  2.3 us
    pallas_call x1, Pallas kernels, per_device(): pl.pallas_call(functools.partial(strip_kernel, offsets, lat_offsets), out...  0.92 us
    pallas_call x1, Pallas kernels, per_device(): pl.pallas_call(update_kernel, out_shape=(out, out), in_specs=[vmem] * 4,...  0.65 us
  transfers between devices with their start and end apart: 7, of which 7 were waited for; matrix products, arithmetic and copies ran while one was open for 0% of the time, Pallas kernels for 0%

profile of v5, /device:TPU:0, one launch (start us, length us, event | category | flops | bytes accessed | tf_op | source)
XLA Modules:
  0.0 30.8 jit_solution(748732124944837048)
XLA Ops:
  0.6 2.3 %shard_map.113 = (f32[2,17,8,128]{3,2,1,0:T(8,128)S(1)}, f32[2,17,8,128]{3,2,1,0:T(8,128)S(1)}, f32[1,8,128]{2,1,0:T(8,128)S(1)}, f32[13,1,256]{2,1,0:T(1,128)S(1)}) custom-call(s32[64]{0:T(128)} %bitcast.7, s32[64]{0:T(128)} %refs_1_.1, f32[8]{0:T(128)} %refs_2_.1, f32[3,3]{1,0:T(4,128)} %refs_3_.1, f32[2,2]{1,0:T(2,128)} %refs_4_.1, ...), custom_call_target="tpu_custom_call" | custom-call | tf_op jit(solution)/shard_map/pallas_call | solution.py:313
  2.9 0.5 %collective-permute-start = (f32[2,17,8,128]{3,2,1,0:T(8,128)S(1)}, f32[2,17,8,128]{3,2,1,0:T(8,128)S(1)}, u32[]{:S(2)}, u32[]{:S(2)}) collective-permute-start(f32[2,17,8,128]{3,2,1,0:T(8,128)S(1)} %get-tuple-element.10), channel_id=1, source_target_pairs={{0,2},{2,0},{4,6},{6,4},{1,3},{3,1},{5,7},{7,5},{8,10},{10,8},{12,... | collective-permute-start | bytes 417800 | tf_op jit(solution)/shard_map/ppermute | solution.py:291
  3.5 1.0 %collective-permute-done = f32[2,17,8,128]{3,2,1,0:T(8,128)S(1)} collective-permute-done((f32[2,17,8,128]{3,2,1,0:T(8,128)S(1)}, f32[2,17,8,128]{3,2,1,0:T(8,128)S(1)}, u32[]{:S(2)}, u32[]{:S(2)}) %collective-permute-start) | collective-permute-done | bytes 139296 | tf_op jit(solution)/shard_map/ppermute | solution.py:291
  4.5 2.9 %collective-permute-start.1 = (f32[1,17,8,128]{3,2,1,0:T(8,128)S(1)}, f32[1,17,8,128]{3,2,1,0:T(8,128)S(1)}, u32[]{:S(2)}, u32[]{:S(2)}) collective-permute-start(f32[1,17,8,128]{3,2,1,0:T(8,128)S(1)} %slice.27), channel_id=1, source_target_pairs={{0,4},{2,6},{4,0},{6,2},{1,5},{3,7},{5,1},{7,3},{8,12},{10,14},{12... | collective-permute-start | bytes 208904 | tf_op jit(solution)/shard_map/ppermute | solution.py:291
  7.4 2.5 %collective-permute-done.1 = f32[1,17,8,128]{3,2,1,0:T(8,128)S(1)} collective-permute-done((f32[1,17,8,128]{3,2,1,0:T(8,128)S(1)}, f32[1,17,8,128]{3,2,1,0:T(8,128)S(1)}, u32[]{:S(2)}, u32[]{:S(2)}) %collective-permute-start.1) | collective-permute-done | bytes 69664 | tf_op jit(solution)/shard_map/ppermute | solution.py:291
  10.0 1.9 %collective-permute-start.2 = (f32[18,8,128]{2,1,0:T(8,128)S(1)}, f32[18,8,128]{2,1,0:T(8,128)S(1)}, u32[]{:S(2)}, u32[]{:S(2)}) collective-permute-start(f32[18,8,128]{2,1,0:T(8,128)S(1)} %pad_maximum_fusion.1), channel_id=1, source_target_pairs={{0,8},{8,0},{16,24},{24,16},{1,9},{9,1},{17,25},{25,17},{2,10},{10... | collective-permute-start | bytes 221192 | tf_op jit(solution)/shard_map/ppermute | solution.py:291
  11.9 2.5 %collective-permute-done.2 = f32[18,8,128]{2,1,0:T(8,128)S(1)} collective-permute-done((f32[18,8,128]{2,1,0:T(8,128)S(1)}, f32[18,8,128]{2,1,0:T(8,128)S(1)}, u32[]{:S(2)}, u32[]{:S(2)}) %collective-permute-start.2) | collective-permute-done | bytes 73760 | tf_op jit(solution)/shard_map/ppermute | solution.py:291
  14.4 2.9 %collective-permute-start.3 = (f32[19,8,128]{2,1,0:T(8,128)S(1)}, f32[19,8,128]{2,1,0:T(8,128)S(1)}, u32[]{:S(2)}, u32[]{:S(2)}) collective-permute-start(f32[19,8,128]{2,1,0:T(8,128)S(1)} %pad_maximum_fusion), channel_id=1, source_target_pairs={{0,16},{8,24},{16,0},{24,8},{1,17},{9,25},{17,1},{25,9},{2,18},{10... | collective-permute-start | bytes 233480 | tf_op jit(solution)/shard_map/ppermute | solution.py:291
  17.4 2.4 %collective-permute-done.3 = f32[19,8,128]{2,1,0:T(8,128)S(1)} collective-permute-done((f32[19,8,128]{2,1,0:T(8,128)S(1)}, f32[19,8,128]{2,1,0:T(8,128)S(1)}, u32[]{:S(2)}, u32[]{:S(2)}) %collective-permute-start.3) | collective-permute-done | bytes 77856 | tf_op jit(solution)/shard_map/ppermute | solution.py:291
  19.8 1.8 %collective-permute-start.4 = (f32[1,21,8,128]{3,2,1,0:T(8,128)S(1)}, f32[1,21,8,128]{3,2,1,0:T(8,128)S(1)}, u32[]{:S(2)}, u32[]{:S(2)}) collective-permute-start(f32[1,21,8,128]{3,2,1,0:T(8,128)S(1)} %maximum_bitcast_fusion.near_ref), channel_id=1, source_target_pairs={{0,1},{1,0},{2,3},{3,2},{4,5},{5,4},{6,7},{7,6},{8,9},{9,8},{10,11... | collective-permute-start | bytes 258056 | tf_op jit(solution)/shard_map/ppermute | solution.py:291
  21.7 2.7 %collective-permute-done.4.far_ref = f32[1,21,8,128]{3,2,1,0:T(8,128)S(1)} collective-permute-done((f32[1,21,8,128]{3,2,1,0:T(8,128)S(1)}, f32[1,21,8,128]{3,2,1,0:T(8,128)S(1)}, u32[]{:S(2)}, u32[]{:S(2)}) %collective-permute-start.4) | collective-permute-done | bytes 86048 | tf_op jit(solution)/shard_map/ppermute | solution.py:291
  24.4 0.9 %shard_map.114 = (f32[4,3,8,128]{3,2,1,0:T(8,128)S(1)}, f32[1,8,128]{2,1,0:T(8,128)S(1)}) custom-call(f32[13,1,256]{2,1,0:T(1,128)S(1)} %get-tuple-element.8.factors_ref, f32[1,21,8,128]{3,2,1,0:T(8,128)S(1)} %maximum_bitcast_fusion.near_ref, f32[1,21,8,128]{3,2,1,0:T(8,128)S(1)} %collective-permute-done.4.far_ref), custom_call_target="tpu_custom_call" | custom-call | tf_op jit(solution)/shard_map/pallas_call | solution.py:347
  25.3 1.9 %collective-permute-start.5 = (f32[1,8,128]{2,1,0:T(8,128)S(1)}, f32[1,8,128]{2,1,0:T(8,128)S(1)}, u32[]{:S(2)}, u32[]{:S(2)}) collective-permute-start(f32[1,8,128]{2,1,0:T(8,128)S(1)} %get-tuple-element.13.mine_ref), channel_id=1, source_target_pairs={{0,4},{2,6},{4,0},{6,2},{1,5},{3,7},{5,1},{7,3},{8,12},{10,14},{12... | collective-permute-start | bytes 12296 | tf_op jit(solution)/shard_map/ppermute | solution.py:291
  27.2 1.8 %collective-permute-done.5 = f32[1,8,128]{2,1,0:T(8,128)S(1)} collective-permute-done((f32[1,8,128]{2,1,0:T(8,128)S(1)}, f32[1,8,128]{2,1,0:T(8,128)S(1)}, u32[]{:S(2)}, u32[]{:S(2)}) %collective-permute-start.5) | collective-permute-done | bytes 4128 | tf_op jit(solution)/shard_map/ppermute | solution.py:291
  29.0 0.0 collective-permute-start.6
  29.0 1.2 %collective-permute-done.6.far_ref = f32[2,8,128]{2,1,0:T(8,128)S(1)} collective-permute-done((f32[2,8,128]{2,1,0:T(8,128)S(1)}, f32[2,8,128]{2,1,0:T(8,128)S(1)}, u32[]{:S(2)}, u32[]{:S(2)}) %collective-permute-start.6) | collective-permute-done | bytes 8224 | tf_op jit(solution)/shard_map/ppermute | solution.py:291
  30.1 0.6 %shard_map.115 = (f32[1,3,1,8,128]{4,3,2,1,0:T(8,128)}, f32[1,3,1,8,128]{4,3,2,1,0:T(8,128)}) custom-call(f32[4,3,8,128]{3,2,1,0:T(8,128)S(1)} %get-tuple-element.12.own_ref, f32[1,8,128]{2,1,0:T(8,128)S(1)} %get-tuple-element.13.mine_ref, f32[2,8,128]{2,1,0:T(8,128)S(1)} %constant_dynamic-update-slice_fusion.near_ref, ...), custom_call_target="tpu_custom_call" | custom-call | tf_op jit(solution)/shard_map/pallas_call | solution.py:361
  (12 shorter events, 0.1 us)
Async XLA Ops:
  2.9 1.5 %collective-permute-start = (f32[2,17,8,128]{3,2,1,0:T(8,128)S(1)}, f32[2,17,8,128]{3,2,1,0:T(8,128)S(1)}, u32[]{:S(2)}, u32[]{:S(2)}) collective-permute-start(f32[2,17,8,128]{3,2,1,0:T(8,128)S(1)} %get-tuple-element.10), channel_id=1, source_target_pairs={{0,2},{2,0},{4,6},{6,4},{1,3},{3,1},{5,7},{7,5},{8,10},{10,8},{12,... | collective-permute-start | bytes 417800 | tf_op jit(solution)/shard_map/ppermute | solution.py:291
  4.5 5.4 %collective-permute-start.1 = (f32[1,17,8,128]{3,2,1,0:T(8,128)S(1)}, f32[1,17,8,128]{3,2,1,0:T(8,128)S(1)}, u32[]{:S(2)}, u32[]{:S(2)}) collective-permute-start(f32[1,17,8,128]{3,2,1,0:T(8,128)S(1)} %slice.27), channel_id=1, source_target_pairs={{0,4},{2,6},{4,0},{6,2},{1,5},{3,7},{5,1},{7,3},{8,12},{10,14},{12... | collective-permute-start | bytes 208904 | tf_op jit(solution)/shard_map/ppermute | solution.py:291
  10.0 4.4 %collective-permute-start.2 = (f32[18,8,128]{2,1,0:T(8,128)S(1)}, f32[18,8,128]{2,1,0:T(8,128)S(1)}, u32[]{:S(2)}, u32[]{:S(2)}) collective-permute-start(f32[18,8,128]{2,1,0:T(8,128)S(1)} %pad_maximum_fusion.1), channel_id=1, source_target_pairs={{0,8},{8,0},{16,24},{24,16},{1,9},{9,1},{17,25},{25,17},{2,10},{10... | collective-permute-start | bytes 221192 | tf_op jit(solution)/shard_map/ppermute | solution.py:291
  14.4 5.4 %collective-permute-start.3 = (f32[19,8,128]{2,1,0:T(8,128)S(1)}, f32[19,8,128]{2,1,0:T(8,128)S(1)}, u32[]{:S(2)}, u32[]{:S(2)}) collective-permute-start(f32[19,8,128]{2,1,0:T(8,128)S(1)} %pad_maximum_fusion), channel_id=1, source_target_pairs={{0,16},{8,24},{16,0},{24,8},{1,17},{9,25},{17,1},{25,9},{2,18},{10... | collective-permute-start | bytes 233480 | tf_op jit(solution)/shard_map/ppermute | solution.py:291
  19.8 4.6 %collective-permute-start.4 = (f32[1,21,8,128]{3,2,1,0:T(8,128)S(1)}, f32[1,21,8,128]{3,2,1,0:T(8,128)S(1)}, u32[]{:S(2)}, u32[]{:S(2)}) collective-permute-start(f32[1,21,8,128]{3,2,1,0:T(8,128)S(1)} %maximum_bitcast_fusion.near_ref), channel_id=1, source_target_pairs={{0,1},{1,0},{2,3},{3,2},{4,5},{5,4},{6,7},{7,6},{8,9},{9,8},{10,11... | collective-permute-start | bytes 258056 | tf_op jit(solution)/shard_map/ppermute | solution.py:291
  25.3 3.7 %collective-permute-start.5 = (f32[1,8,128]{2,1,0:T(8,128)S(1)}, f32[1,8,128]{2,1,0:T(8,128)S(1)}, u32[]{:S(2)}, u32[]{:S(2)}) collective-permute-start(f32[1,8,128]{2,1,0:T(8,128)S(1)} %get-tuple-element.13.mine_ref), channel_id=1, source_target_pairs={{0,4},{2,6},{4,0},{6,2},{1,5},{3,7},{5,1},{7,3},{8,12},{10,14},{12... | collective-permute-start | bytes 12296 | tf_op jit(solution)/shard_map/ppermute | solution.py:291
  29.0 1.2 %collective-permute-start.6 = (f32[2,8,128]{2,1,0:T(8,128)S(1)}, f32[2,8,128]{2,1,0:T(8,128)S(1)}, u32[]{:S(2)}, u32[]{:S(2)}) collective-permute-start(f32[2,8,128]{2,1,0:T(8,128)S(1)} %constant_dynamic-update-slice_fusion.near_ref), channel_id=1, source_target_pairs={{0,2},{2,0},{4,6},{6,4},{1,3},{3,1},{5,7},{7,5},{8,10},{10,8},{12,... | collective-permute-start | bytes 24584 | tf_op jit(solution)/shard_map/ppermute | solution.py:291

commit v6 on v5

--- a/solution.py
+++ b/solution.py
@@ -63,7 +63,8 @@
 
     lane = lax.broadcasted_iota(jnp.int32, (1, slots), 1)
     row_ids = lax.broadcasted_iota(jnp.int32, (rows, slots), 0)
-    col_ids = lax.broadcasted_iota(jnp.int32, (cols, slots), 0)
+    col_ids = lax.broadcasted_iota(jnp.int32, (cols, slots), 0).astype(jnp.int16)
+    one, zero = jnp.ones((cols, slots), jnp.bfloat16), jnp.zeros((cols, slots), jnp.bfloat16)
 
     nothing = jnp.zeros((2 * stats * rows, slots), jnp.bfloat16)
 
@@ -75,7 +76,8 @@
         high = [term.astype(jnp.bfloat16).astype(jnp.float32) for term in terms]
         low = [term - part for term, part in zip(terms, high)]
         spread = jnp.concatenate([jnp.where(row_hit, part, 0.0) for part in high + low], axis=0)
-        return spread.astype(jnp.bfloat16), jnp.where(col_ids == cells % cols, 1.0, 0.0).astype(jnp.bfloat16)
+        at_col = jnp.broadcast_to((cells % cols).astype(jnp.int16), (cols, slots))
+        return spread.astype(jnp.bfloat16), jnp.where(at_col == col_ids, one, zero)
 
     def pair_sums(block):
         (first, first_hot), (second, second_hot) = operands(block), operands(block + 1)

time: 30.9 us -> 30.7 us (level)
  no operation moved by 1% of the time
where the time goes in v6:
time: 30.7 us; the launch traced here: 30.6 us
  waiting for transfers between devices  14 us (46%)
  starting transfers between devices  12.1 us (39%)
  Pallas kernels  3.68 us (12%)
  between operations  0.71 us (2%)
    ppermute x7, waiting for transfers between devices, swapped(): lax.ppermute(x, axis, [(i, i ^ bit) for i in range(lax.axis_size(axis))])  14 us
    ppermute x7, starting transfers between devices, swapped(): lax.ppermute(x, axis, [(i, i ^ bit) for i in range(lax.axis_size(axis))])  12.1 us
    pallas_call x1, Pallas kernels, per_device(): pl.pallas_call(tile_kernel, out_shape=(half, half, jax.ShapeDtypeStruct((...  2.11 us
    pallas_call x1, Pallas kernels, per_device(): pl.pallas_call(functools.partial(strip_kernel, offsets, lat_offsets), out...  0.92 us
    pallas_call x1, Pallas kernels, per_device(): pl.pallas_call(update_kernel, out_shape=(out, out), in_specs=[vmem] * 4,...  0.65 us
  transfers between devices with their start and end apart: 7, of which 7 were waited for; matrix products, arithmetic and copies ran while one was open for 0% of the time, Pallas kernels for 0%

profile of v6, /device:TPU:0, one launch (start us, length us, event | category | flops | bytes accessed | tf_op | source)
XLA Modules:
  0.0 30.6 jit_solution(10512818795022157339)
XLA Ops:
  0.6 2.1 %shard_map.113 = (f32[2,17,8,128]{3,2,1,0:T(8,128)S(1)}, f32[2,17,8,128]{3,2,1,0:T(8,128)S(1)}, f32[1,8,128]{2,1,0:T(8,128)S(1)}, f32[13,1,256]{2,1,0:T(1,128)S(1)}) custom-call(s32[64]{0:T(128)} %bitcast.7, s32[64]{0:T(128)} %refs_1_.1, f32[8]{0:T(128)} %refs_2_.1, f32[3,3]{1,0:T(4,128)} %refs_3_.1, f32[2,2]{1,0:T(2,128)} %refs_4_.1, ...), custom_call_target="tpu_custom_call" | custom-call | tf_op jit(solution)/shard_map/pallas_call | solution.py:315
  2.7 0.5 %collective-permute-start = (f32[2,17,8,128]{3,2,1,0:T(8,128)S(1)}, f32[2,17,8,128]{3,2,1,0:T(8,128)S(1)}, u32[]{:S(2)}, u32[]{:S(2)}) collective-permute-start(f32[2,17,8,128]{3,2,1,0:T(8,128)S(1)} %get-tuple-element.10), channel_id=1, source_target_pairs={{0,2},{2,0},{4,6},{6,4},{1,3},{3,1},{5,7},{7,5},{8,10},{10,8},{12,... | collective-permute-start | bytes 417800 | tf_op jit(solution)/shard_map/ppermute | solution.py:293
  3.3 1.0 %collective-permute-done = f32[2,17,8,128]{3,2,1,0:T(8,128)S(1)} collective-permute-done((f32[2,17,8,128]{3,2,1,0:T(8,128)S(1)}, f32[2,17,8,128]{3,2,1,0:T(8,128)S(1)}, u32[]{:S(2)}, u32[]{:S(2)}) %collective-permute-start) | collective-permute-done | bytes 139296 | tf_op jit(solution)/shard_map/ppermute | solution.py:293
  4.3 2.9 %collective-permute-start.1 = (f32[1,17,8,128]{3,2,1,0:T(8,128)S(1)}, f32[1,17,8,128]{3,2,1,0:T(8,128)S(1)}, u32[]{:S(2)}, u32[]{:S(2)}) collective-permute-start(f32[1,17,8,128]{3,2,1,0:T(8,128)S(1)} %slice.27), channel_id=1, source_target_pairs={{0,4},{2,6},{4,0},{6,2},{1,5},{3,7},{5,1},{7,3},{8,12},{10,14},{12... | collective-permute-start | bytes 208904 | tf_op jit(solution)/shard_map/ppermute | solution.py:293
  7.2 2.5 %collective-permute-done.1 = f32[1,17,8,128]{3,2,1,0:T(8,128)S(1)} collective-permute-done((f32[1,17,8,128]{3,2,1,0:T(8,128)S(1)}, f32[1,17,8,128]{3,2,1,0:T(8,128)S(1)}, u32[]{:S(2)}, u32[]{:S(2)}) %collective-permute-start.1) | collective-permute-done | bytes 69664 | tf_op jit(solution)/shard_map/ppermute | solution.py:293
  9.8 1.9 %collective-permute-start.2 = (f32[18,8,128]{2,1,0:T(8,128)S(1)}, f32[18,8,128]{2,1,0:T(8,128)S(1)}, u32[]{:S(2)}, u32[]{:S(2)}) collective-permute-start(f32[18,8,128]{2,1,0:T(8,128)S(1)} %pad_maximum_fusion.1), channel_id=1, source_target_pairs={{0,8},{8,0},{16,24},{24,16},{1,9},{9,1},{17,25},{25,17},{2,10},{10... | collective-permute-start | bytes 221192 | tf_op jit(solution)/shard_map/ppermute | solution.py:293
  11.7 2.5 %collective-permute-done.2 = f32[18,8,128]{2,1,0:T(8,128)S(1)} collective-permute-done((f32[18,8,128]{2,1,0:T(8,128)S(1)}, f32[18,8,128]{2,1,0:T(8,128)S(1)}, u32[]{:S(2)}, u32[]{:S(2)}) %collective-permute-start.2) | collective-permute-done | bytes 73760 | tf_op jit(solution)/shard_map/ppermute | solution.py:293
  14.2 2.9 %collective-permute-start.3 = (f32[19,8,128]{2,1,0:T(8,128)S(1)}, f32[19,8,128]{2,1,0:T(8,128)S(1)}, u32[]{:S(2)}, u32[]{:S(2)}) collective-permute-start(f32[19,8,128]{2,1,0:T(8,128)S(1)} %pad_maximum_fusion), channel_id=1, source_target_pairs={{0,16},{8,24},{16,0},{24,8},{1,17},{9,25},{17,1},{25,9},{2,18},{10... | collective-permute-start | bytes 233480 | tf_op jit(solution)/shard_map/ppermute | solution.py:293
  17.2 2.4 %collective-permute-done.3 = f32[19,8,128]{2,1,0:T(8,128)S(1)} collective-permute-done((f32[19,8,128]{2,1,0:T(8,128)S(1)}, f32[19,8,128]{2,1,0:T(8,128)S(1)}, u32[]{:S(2)}, u32[]{:S(2)}) %collective-permute-start.3) | collective-permute-done | bytes 77856 | tf_op jit(solution)/shard_map/ppermute | solution.py:293
  19.6 1.9 %collective-permute-start.4 = (f32[1,21,8,128]{3,2,1,0:T(8,128)S(1)}, f32[1,21,8,128]{3,2,1,0:T(8,128)S(1)}, u32[]{:S(2)}, u32[]{:S(2)}) collective-permute-start(f32[1,21,8,128]{3,2,1,0:T(8,128)S(1)} %maximum_bitcast_fusion.near_ref), channel_id=1, source_target_pairs={{0,1},{1,0},{2,3},{3,2},{4,5},{5,4},{6,7},{7,6},{8,9},{9,8},{10,11... | collective-permute-start | bytes 258056 | tf_op jit(solution)/shard_map/ppermute | solution.py:293
  21.5 2.7 %collective-permute-done.4.far_ref = f32[1,21,8,128]{3,2,1,0:T(8,128)S(1)} collective-permute-done((f32[1,21,8,128]{3,2,1,0:T(8,128)S(1)}, f32[1,21,8,128]{3,2,1,0:T(8,128)S(1)}, u32[]{:S(2)}, u32[]{:S(2)}) %collective-permute-start.4) | collective-permute-done | bytes 86048 | tf_op jit(solution)/shard_map/ppermute | solution.py:293
  24.2 0.9 %shard_map.114 = (f32[4,3,8,128]{3,2,1,0:T(8,128)S(1)}, f32[1,8,128]{2,1,0:T(8,128)S(1)}) custom-call(f32[13,1,256]{2,1,0:T(1,128)S(1)} %get-tuple-element.8.factors_ref, f32[1,21,8,128]{3,2,1,0:T(8,128)S(1)} %maximum_bitcast_fusion.near_ref, f32[1,21,8,128]{3,2,1,0:T(8,128)S(1)} %collective-permute-done.4.far_ref), custom_call_target="tpu_custom_call" | custom-call | tf_op jit(solution)/shard_map/pallas_call | solution.py:349
  25.1 1.9 %collective-permute-start.5 = (f32[1,8,128]{2,1,0:T(8,128)S(1)}, f32[1,8,128]{2,1,0:T(8,128)S(1)}, u32[]{:S(2)}, u32[]{:S(2)}) collective-permute-start(f32[1,8,128]{2,1,0:T(8,128)S(1)} %get-tuple-element.13.mine_ref), channel_id=1, source_target_pairs={{0,4},{2,6},{4,0},{6,2},{1,5},{3,7},{5,1},{7,3},{8,12},{10,14},{12... | collective-permute-start | bytes 12296 | tf_op jit(solution)/shard_map/ppermute | solution.py:293
  27.0 1.8 %collective-permute-done.5 = f32[1,8,128]{2,1,0:T(8,128)S(1)} collective-permute-done((f32[1,8,128]{2,1,0:T(8,128)S(1)}, f32[1,8,128]{2,1,0:T(8,128)S(1)}, u32[]{:S(2)}, u32[]{:S(2)}) %collective-permute-start.5) | collective-permute-done | bytes 4128 | tf_op jit(solution)/shard_map/ppermute | solution.py:293
  28.8 0.0 collective-permute-start.6
  28.8 1.2 %collective-permute-done.6.far_ref = f32[2,8,128]{2,1,0:T(8,128)S(1)} collective-permute-done((f32[2,8,128]{2,1,0:T(8,128)S(1)}, f32[2,8,128]{2,1,0:T(8,128)S(1)}, u32[]{:S(2)}, u32[]{:S(2)}) %collective-permute-start.6) | collective-permute-done | bytes 8224 | tf_op jit(solution)/shard_map/ppermute | solution.py:293
  29.9 0.6 %shard_map.115 = (f32[1,3,1,8,128]{4,3,2,1,0:T(8,128)}, f32[1,3,1,8,128]{4,3,2,1,0:T(8,128)}) custom-call(f32[4,3,8,128]{3,2,1,0:T(8,128)S(1)} %get-tuple-element.12.own_ref, f32[1,8,128]{2,1,0:T(8,128)S(1)} %get-tuple-element.13.mine_ref, f32[2,8,128]{2,1,0:T(8,128)S(1)} %constant_dynamic-update-slice_fusion.near_ref, ...), custom_call_target="tpu_custom_call" | custom-call | tf_op jit(solution)/shard_map/pallas_call | solution.py:363
  (12 shorter events, 0.1 us)
Async XLA Ops:
  2.7 1.5 %collective-permute-start = (f32[2,17,8,128]{3,2,1,0:T(8,128)S(1)}, f32[2,17,8,128]{3,2,1,0:T(8,128)S(1)}, u32[]{:S(2)}, u32[]{:S(2)}) collective-permute-start(f32[2,17,8,128]{3,2,1,0:T(8,128)S(1)} %get-tuple-element.10), channel_id=1, source_target_pairs={{0,2},{2,0},{4,6},{6,4},{1,3},{3,1},{5,7},{7,5},{8,10},{10,8},{12,... | collective-permute-start | bytes 417800 | tf_op jit(solution)/shard_map/ppermute | solution.py:293
  4.3 5.4 %collective-permute-start.1 = (f32[1,17,8,128]{3,2,1,0:T(8,128)S(1)}, f32[1,17,8,128]{3,2,1,0:T(8,128)S(1)}, u32[]{:S(2)}, u32[]{:S(2)}) collective-permute-start(f32[1,17,8,128]{3,2,1,0:T(8,128)S(1)} %slice.27), channel_id=1, source_target_pairs={{0,4},{2,6},{4,0},{6,2},{1,5},{3,7},{5,1},{7,3},{8,12},{10,14},{12... | collective-permute-start | bytes 208904 | tf_op jit(solution)/shard_map/ppermute | solution.py:293
  9.8 4.4 %collective-permute-start.2 = (f32[18,8,128]{2,1,0:T(8,128)S(1)}, f32[18,8,128]{2,1,0:T(8,128)S(1)}, u32[]{:S(2)}, u32[]{:S(2)}) collective-permute-start(f32[18,8,128]{2,1,0:T(8,128)S(1)} %pad_maximum_fusion.1), channel_id=1, source_target_pairs={{0,8},{8,0},{16,24},{24,16},{1,9},{9,1},{17,25},{25,17},{2,10},{10... | collective-permute-start | bytes 221192 | tf_op jit(solution)/shard_map/ppermute | solution.py:293
  14.2 5.4 %collective-permute-start.3 = (f32[19,8,128]{2,1,0:T(8,128)S(1)}, f32[19,8,128]{2,1,0:T(8,128)S(1)}, u32[]{:S(2)}, u32[]{:S(2)}) collective-permute-start(f32[19,8,128]{2,1,0:T(8,128)S(1)} %pad_maximum_fusion), channel_id=1, source_target_pairs={{0,16},{8,24},{16,0},{24,8},{1,17},{9,25},{17,1},{25,9},{2,18},{10... | collective-permute-start | bytes 233480 | tf_op jit(solution)/shard_map/ppermute | solution.py:293
  19.6 4.6 %collective-permute-start.4 = (f32[1,21,8,128]{3,2,1,0:T(8,128)S(1)}, f32[1,21,8,128]{3,2,1,0:T(8,128)S(1)}, u32[]{:S(2)}, u32[]{:S(2)}) collective-permute-start(f32[1,21,8,128]{3,2,1,0:T(8,128)S(1)} %maximum_bitcast_fusion.near_ref), channel_id=1, source_target_pairs={{0,1},{1,0},{2,3},{3,2},{4,5},{5,4},{6,7},{7,6},{8,9},{9,8},{10,11... | collective-permute-start | bytes 258056 | tf_op jit(solution)/shard_map/ppermute | solution.py:293
  25.1 3.7 %collective-permute-start.5 = (f32[1,8,128]{2,1,0:T(8,128)S(1)}, f32[1,8,128]{2,1,0:T(8,128)S(1)}, u32[]{:S(2)}, u32[]{:S(2)}) collective-permute-start(f32[1,8,128]{2,1,0:T(8,128)S(1)} %get-tuple-element.13.mine_ref), channel_id=1, source_target_pairs={{0,4},{2,6},{4,0},{6,2},{1,5},{3,7},{5,1},{7,3},{8,12},{10,14},{12... | collective-permute-start | bytes 12296 | tf_op jit(solution)/shard_map/ppermute | solution.py:293
  28.8 1.2 %collective-permute-start.6 = (f32[2,8,128]{2,1,0:T(8,128)S(1)}, f32[2,8,128]{2,1,0:T(8,128)S(1)}, u32[]{:S(2)}, u32[]{:S(2)}) collective-permute-start(f32[2,8,128]{2,1,0:T(8,128)S(1)} %constant_dynamic-update-slice_fusion.near_ref), channel_id=1, source_target_pairs={{0,2},{2,0},{4,6},{6,4},{1,3},{3,1},{5,7},{7,5},{8,10},{10,8},{12,... | collective-permute-start | bytes 24584 | tf_op jit(solution)/shard_map/ppermute | solution.py:293

commit v7 on v6

--- a/solution.py
+++ b/solution.py
@@ -7,7 +7,7 @@
 from jax.experimental.pallas import tpu as pltpu
 from jax.sharding import PartitionSpec as P
 
-GROUP = 64
+GROUP = 8
 SIDES = 4
 INPUTS = 10
 ALL = ("lat", "lon", "tm")
@@ -38,7 +38,7 @@
     local, arrived = refs[INPUTS + 6 : -1], refs[-1]
     owner_ref, count_ref, table_ref, cov_ref, metric_ref, values_ref, weight_ref, cells_ref, class_ref, land_ref = local
     copies = [pltpu.make_async_copy(a, b, arrived.at[k]) for k, (a, b) in enumerate(zip(arguments, local))]
-    for copy in copies:
+    for copy in copies[5:8] + copies[:5] + copies[8:]:
         copy.start()
     tiles[...] = jnp.zeros_like(tiles)
     variables, block_total, slots = values_ref.shape
@@ -61,44 +61,43 @@
         for u in range(months):
             factors_ref[variables * variables + t * months + u] = jnp.full(factors_ref.shape[1:], metric_ref[t, u])
 
-    lane = lax.broadcasted_iota(jnp.int32, (1, slots), 1)
+    lane = lax.broadcasted_iota(jnp.int32, (GROUP, slots), 1)
+    turn = lax.broadcasted_iota(jnp.int32, (GROUP, slots), 0)
     row_ids = lax.broadcasted_iota(jnp.int32, (rows, slots), 0)
     col_ids = lax.broadcasted_iota(jnp.int32, (cols, slots), 0).astype(jnp.int16)
     one, zero = jnp.ones((cols, slots), jnp.bfloat16), jnp.zeros((cols, slots), jnp.bfloat16)
-
     nothing = jnp.zeros((2 * stats * rows, slots), jnp.bfloat16)
 
-    def operands(block):
-        live = jnp.where(lane < count_ref[block], weight_ref[pl.ds(block, 1), :], 0.0)
-        cells = cells_ref[pl.ds(block, 1), :]
-        row_hit = row_ids == cells // cols
-        terms = [live] + [live * values_ref[v, pl.ds(block, 1), :] for v in range(variables)]
-        high = [term.astype(jnp.bfloat16).astype(jnp.float32) for term in terms]
-        low = [term - part for term, part in zip(terms, high)]
-        spread = jnp.concatenate([jnp.where(row_hit, part, 0.0) for part in high + low], axis=0)
-        at_col = jnp.broadcast_to((cells % cols).astype(jnp.int16), (cols, slots))
-        return spread.astype(jnp.bfloat16), jnp.where(at_col == col_ids, one, zero)
-
-    def pair_sums(block):
-        (first, first_hot), (second, second_hot) = operands(block), operands(block + 1)
+    def pair_sums(parts, row_of, col_of, k):
+        spread, hot = [], []
+        for at in (slice(k, k + 1), slice(k + 1, k + 2)):
+            row_hit = row_ids == row_of[at]
+            spread.append(jnp.concatenate([jnp.where(row_hit, part[at], 0.0) for part in parts], axis=0).astype(jnp.bfloat16))
+            hot.append(jnp.where(jnp.broadcast_to(col_of[at].astype(jnp.int16), (cols, slots)) == col_ids, one, zero))
         both = lax.dot_general(
-            jnp.concatenate([jnp.concatenate([first, nothing], axis=1), jnp.concatenate([nothing, second], axis=1)], axis=0),
-            jnp.concatenate([first_hot, second_hot], axis=1),
+            jnp.concatenate([jnp.concatenate([spread[0], nothing], axis=1), jnp.concatenate([nothing, spread[1]], axis=1)], axis=0),
+            jnp.concatenate(hot, axis=1),
             (((1,), (1,)), ((), ())),
             preferred_element_type=jnp.float32,
         ).reshape(2, 2, stats, rows, cols)
         return [both[0, 0] + both[0, 1], both[1, 0] + both[1, 1]]
 
-    def step(group, carry):
-        sums = []
+    sums = []
+    for first in range(0, block_total, GROUP):
+        blocks = slice(first, first + GROUP)
+        counts = jnp.zeros((GROUP, slots), jnp.int32)
+        for k in range(GROUP):
+            counts = jnp.where(turn == k, count_ref[first + k], counts)
+        live = jnp.where(lane < counts, weight_ref[blocks], 0.0)
+        terms = [live] + [live * values_ref[v, blocks] for v in range(variables)]
+        high = [term.astype(jnp.bfloat16).astype(jnp.float32) for term in terms]
+        low = [term - part for term, part in zip(terms, high)]
+        row_of, col_of = cells_ref[blocks] // cols, cells_ref[blocks] % cols
         for k in range(0, GROUP, 2):
-            sums += pair_sums(group * GROUP + k)
-        for k in range(GROUP):
-            owner = owner_ref[group * GROUP + k]
-            tiles[jnp.bitwise_xor(owner % n_lon, lon), owner // n_lon] += sums[k]
-        return carry
-
-    lax.fori_loop(0, block_total // GROUP, step, 0)
+            sums += pair_sums(high + low, row_of, col_of, k)
+    for block in range(block_total):
+        owner = owner_ref[block]
+        tiles[jnp.bitwise_xor(owner % n_lon, lon), owner // n_lon] += sums[block]
     own_tiles = stats * n_lat
     for m in range(n_lon // 2):
         for i in range(n_lat):
@@ -113,10 +112,12 @@
     at_row = lax.broadcasted_iota(jnp.int32, (height, lanes), 1) % height == row
     own_row = lax.broadcasted_iota(jnp.int32, (rows, lanes), 1) % height == lax.broadcasted_iota(jnp.int32, (rows, lanes), 0) + lat * rows
     blank = jnp.zeros((1, lanes), jnp.float32)
+    stacked = [tiles[offset, i, s] for offset in range(n_lon) for s in range(stats) for i in range(n_lat)]
+    picked = exact_dot(jnp.concatenate(stacked + [plane], axis=0), edges)
+    tall = stats * height
     for offset in range(n_lon):
-        picked = exact_dot(jnp.concatenate([tiles[offset, i, s] for s in range(stats) for i in range(n_lat)], axis=0), edges)
-        rows_of = [jnp.where(at_row, picked[s * height : (s + 1) * height], 0.0) for s in range(stats)]
-        rows_of.append(jnp.where(own_row, exact_dot(plane, edges), 0.0) if offset == 0 else blank)
+        rows_of = [jnp.where(at_row, picked[offset * tall + s * height : offset * tall + (s + 1) * height], 0.0) for s in range(stats)]
+        rows_of.append(jnp.where(own_row, picked[n_lon * tall :], 0.0) if offset == 0 else blank)
         sums = [jnp.sum(x, axis=0, keepdims=True) for x in rows_of]
         packed[offset] = jnp.concatenate(sums + [blank] * (rows - stats - 1), axis=0)
     from_after = lax.broadcasted_iota(jnp.int32, (rows, lanes), 1) < 2 * height

time: 30.7 us -> 30.6 us (level)
  no operation moved by 1% of the time
where the time goes in v7:
time: 30.6 us; the launch traced here: 30.5 us
  waiting for transfers between devices  14 us (46%)
  starting transfers between devices  12.1 us (40%)
  Pallas kernels  3.58 us (12%)
  between operations  0.71 us (2%)
    ppermute x7, waiting for transfers between devices, swapped(): lax.ppermute(x, axis, [(i, i ^ bit) for i in range(lax.axis_size(axis))])  14 us
    ppermute x7, starting transfers between devices, swapped(): lax.ppermute(x, axis, [(i, i ^ bit) for i in range(lax.axis_size(axis))])  12.1 us
    pallas_call x1, Pallas kernels, per_device(): pl.pallas_call(tile_kernel, out_shape=(half, half, jax.ShapeDtypeStruct((...  2 us
    pallas_call x1, Pallas kernels, per_device(): pl.pallas_call(functools.partial(strip_kernel, offsets, lat_offsets), out...  0.93 us
    pallas_call x1, Pallas kernels, per_device(): pl.pallas_call(update_kernel, out_shape=(out, out), in_specs=[vmem] * 4,...  0.65 us
  transfers between devices with their start and end apart: 7, of which 7 were waited for; matrix products, arithmetic and copies ran while one was open for 0% of the time, Pallas kernels for 0%

profile of v7, /device:TPU:0, one launch (start us, length us, event | category | flops | bytes accessed | tf_op | source)
XLA Modules:
  0.0 30.5 jit_solution(13006591012400851685)
XLA Ops:
  0.6 2.0 %shard_map.113 = (f32[2,17,8,128]{3,2,1,0:T(8,128)S(1)}, f32[2,17,8,128]{3,2,1,0:T(8,128)S(1)}, f32[1,8,128]{2,1,0:T(8,128)S(1)}, f32[13,1,256]{2,1,0:T(1,128)S(1)}) custom-call(s32[64]{0:T(128)} %bitcast.7, s32[64]{0:T(128)} %refs_1_.1, f32[8]{0:T(128)} %refs_2_.1, f32[3,3]{1,0:T(4,128)} %refs_3_.1, f32[2,2]{1,0:T(2,128)} %refs_4_.1, ...), custom_call_target="tpu_custom_call" | custom-call | tf_op jit(solution)/shard_map/pallas_call | solution.py:316
  2.6 0.5 %collective-permute-start = (f32[2,17,8,128]{3,2,1,0:T(8,128)S(1)}, f32[2,17,8,128]{3,2,1,0:T(8,128)S(1)}, u32[]{:S(2)}, u32[]{:S(2)}) collective-permute-start(f32[2,17,8,128]{3,2,1,0:T(8,128)S(1)} %get-tuple-element.10), channel_id=1, source_target_pairs={{0,2},{2,0},{4,6},{6,4},{1,3},{3,1},{5,7},{7,5},{8,10},{10,8},{12,... | collective-permute-start | bytes 417800 | tf_op jit(solution)/shard_map/ppermute | solution.py:294
  3.2 1.0 %collective-permute-done = f32[2,17,8,128]{3,2,1,0:T(8,128)S(1)} collective-permute-done((f32[2,17,8,128]{3,2,1,0:T(8,128)S(1)}, f32[2,17,8,128]{3,2,1,0:T(8,128)S(1)}, u32[]{:S(2)}, u32[]{:S(2)}) %collective-permute-start) | collective-permute-done | bytes 139296 | tf_op jit(solution)/shard_map/ppermute | solution.py:294
  4.2 2.9 %collective-permute-start.1 = (f32[1,17,8,128]{3,2,1,0:T(8,128)S(1)}, f32[1,17,8,128]{3,2,1,0:T(8,128)S(1)}, u32[]{:S(2)}, u32[]{:S(2)}) collective-permute-start(f32[1,17,8,128]{3,2,1,0:T(8,128)S(1)} %slice.27), channel_id=1, source_target_pairs={{0,4},{2,6},{4,0},{6,2},{1,5},{3,7},{5,1},{7,3},{8,12},{10,14},{12... | collective-permute-start | bytes 208904 | tf_op jit(solution)/shard_map/ppermute | solution.py:294
  7.1 2.5 %collective-permute-done.1 = f32[1,17,8,128]{3,2,1,0:T(8,128)S(1)} collective-permute-done((f32[1,17,8,128]{3,2,1,0:T(8,128)S(1)}, f32[1,17,8,128]{3,2,1,0:T(8,128)S(1)}, u32[]{:S(2)}, u32[]{:S(2)}) %collective-permute-start.1) | collective-permute-done | bytes 69664 | tf_op jit(solution)/shard_map/ppermute | solution.py:294
  9.7 1.9 %collective-permute-start.2 = (f32[18,8,128]{2,1,0:T(8,128)S(1)}, f32[18,8,128]{2,1,0:T(8,128)S(1)}, u32[]{:S(2)}, u32[]{:S(2)}) collective-permute-start(f32[18,8,128]{2,1,0:T(8,128)S(1)} %pad_maximum_fusion.1), channel_id=1, source_target_pairs={{0,8},{8,0},{16,24},{24,16},{1,9},{9,1},{17,25},{25,17},{2,10},{10... | collective-permute-start | bytes 221192 | tf_op jit(solution)/shard_map/ppermute | solution.py:294
  11.6 2.5 %collective-permute-done.2 = f32[18,8,128]{2,1,0:T(8,128)S(1)} collective-permute-done((f32[18,8,128]{2,1,0:T(8,128)S(1)}, f32[18,8,128]{2,1,0:T(8,128)S(1)}, u32[]{:S(2)}, u32[]{:S(2)}) %collective-permute-start.2) | collective-permute-done | bytes 73760 | tf_op jit(solution)/shard_map/ppermute | solution.py:294
  14.1 3.0 %collective-permute-start.3 = (f32[19,8,128]{2,1,0:T(8,128)S(1)}, f32[19,8,128]{2,1,0:T(8,128)S(1)}, u32[]{:S(2)}, u32[]{:S(2)}) collective-permute-start(f32[19,8,128]{2,1,0:T(8,128)S(1)} %pad_maximum_fusion), channel_id=1, source_target_pairs={{0,16},{8,24},{16,0},{24,8},{1,17},{9,25},{17,1},{25,9},{2,18},{10... | collective-permute-start | bytes 233480 | tf_op jit(solution)/shard_map/ppermute | solution.py:294
  17.1 2.4 %collective-permute-done.3 = f32[19,8,128]{2,1,0:T(8,128)S(1)} collective-permute-done((f32[19,8,128]{2,1,0:T(8,128)S(1)}, f32[19,8,128]{2,1,0:T(8,128)S(1)}, u32[]{:S(2)}, u32[]{:S(2)}) %collective-permute-start.3) | collective-permute-done | bytes 77856 | tf_op jit(solution)/shard_map/ppermute | solution.py:294
  19.5 1.9 %collective-permute-start.4 = (f32[1,21,8,128]{3,2,1,0:T(8,128)S(1)}, f32[1,21,8,128]{3,2,1,0:T(8,128)S(1)}, u32[]{:S(2)}, u32[]{:S(2)}) collective-permute-start(f32[1,21,8,128]{3,2,1,0:T(8,128)S(1)} %maximum_bitcast_fusion.near_ref), channel_id=1, source_target_pairs={{0,1},{1,0},{2,3},{3,2},{4,5},{5,4},{6,7},{7,6},{8,9},{9,8},{10,11... | collective-permute-start | bytes 258056 | tf_op jit(solution)/shard_map/ppermute | solution.py:294
  21.4 2.7 %collective-permute-done.4.far_ref = f32[1,21,8,128]{3,2,1,0:T(8,128)S(1)} collective-permute-done((f32[1,21,8,128]{3,2,1,0:T(8,128)S(1)}, f32[1,21,8,128]{3,2,1,0:T(8,128)S(1)}, u32[]{:S(2)}, u32[]{:S(2)}) %collective-permute-start.4) | collective-permute-done | bytes 86048 | tf_op jit(solution)/shard_map/ppermute | solution.py:294
  24.1 0.9 %shard_map.114 = (f32[4,3,8,128]{3,2,1,0:T(8,128)S(1)}, f32[1,8,128]{2,1,0:T(8,128)S(1)}) custom-call(f32[13,1,256]{2,1,0:T(1,128)S(1)} %get-tuple-element.8.factors_ref, f32[1,21,8,128]{3,2,1,0:T(8,128)S(1)} %maximum_bitcast_fusion.near_ref, f32[1,21,8,128]{3,2,1,0:T(8,128)S(1)} %collective-permute-done.4.far_ref), custom_call_target="tpu_custom_call" | custom-call | tf_op jit(solution)/shard_map/pallas_call | solution.py:350
  25.0 1.9 %collective-permute-start.5 = (f32[1,8,128]{2,1,0:T(8,128)S(1)}, f32[1,8,128]{2,1,0:T(8,128)S(1)}, u32[]{:S(2)}, u32[]{:S(2)}) collective-permute-start(f32[1,8,128]{2,1,0:T(8,128)S(1)} %get-tuple-element.13.mine_ref), channel_id=1, source_target_pairs={{0,4},{2,6},{4,0},{6,2},{1,5},{3,7},{5,1},{7,3},{8,12},{10,14},{12... | collective-permute-start | bytes 12296 | tf_op jit(solution)/shard_map/ppermute | solution.py:294
  26.9 1.8 %collective-permute-done.5 = f32[1,8,128]{2,1,0:T(8,128)S(1)} collective-permute-done((f32[1,8,128]{2,1,0:T(8,128)S(1)}, f32[1,8,128]{2,1,0:T(8,128)S(1)}, u32[]{:S(2)}, u32[]{:S(2)}) %collective-permute-start.5) | collective-permute-done | bytes 4128 | tf_op jit(solution)/shard_map/ppermute | solution.py:294
  28.7 0.0 collective-permute-start.6
  28.7 1.2 %collective-permute-done.6.far_ref = f32[2,8,128]{2,1,0:T(8,128)S(1)} collective-permute-done((f32[2,8,128]{2,1,0:T(8,128)S(1)}, f32[2,8,128]{2,1,0:T(8,128)S(1)}, u32[]{:S(2)}, u32[]{:S(2)}) %collective-permute-start.6) | collective-permute-done | bytes 8224 | tf_op jit(solution)/shard_map/ppermute | solution.py:294
  29.8 0.6 %shard_map.115 = (f32[1,3,1,8,128]{4,3,2,1,0:T(8,128)}, f32[1,3,1,8,128]{4,3,2,1,0:T(8,128)}) custom-call(f32[4,3,8,128]{3,2,1,0:T(8,128)S(1)} %get-tuple-element.12.own_ref, f32[1,8,128]{2,1,0:T(8,128)S(1)} %get-tuple-element.13.mine_ref, f32[2,8,128]{2,1,0:T(8,128)S(1)} %constant_dynamic-update-slice_fusion.near_ref, ...), custom_call_target="tpu_custom_call" | custom-call | tf_op jit(solution)/shard_map/pallas_call | solution.py:364
  (12 shorter events, 0.1 us)
Async XLA Ops:
  2.6 1.5 %collective-permute-start = (f32[2,17,8,128]{3,2,1,0:T(8,128)S(1)}, f32[2,17,8,128]{3,2,1,0:T(8,128)S(1)}, u32[]{:S(2)}, u32[]{:S(2)}) collective-permute-start(f32[2,17,8,128]{3,2,1,0:T(8,128)S(1)} %get-tuple-element.10), channel_id=1, source_target_pairs={{0,2},{2,0},{4,6},{6,4},{1,3},{3,1},{5,7},{7,5},{8,10},{10,8},{12,... | collective-permute-start | bytes 417800 | tf_op jit(solution)/shard_map/ppermute | solution.py:294
  4.2 5.4 %collective-permute-start.1 = (f32[1,17,8,128]{3,2,1,0:T(8,128)S(1)}, f32[1,17,8,128]{3,2,1,0:T(8,128)S(1)}, u32[]{:S(2)}, u32[]{:S(2)}) collective-permute-start(f32[1,17,8,128]{3,2,1,0:T(8,128)S(1)} %slice.27), channel_id=1, source_target_pairs={{0,4},{2,6},{4,0},{6,2},{1,5},{3,7},{5,1},{7,3},{8,12},{10,14},{12... | collective-permute-start | bytes 208904 | tf_op jit(solution)/shard_map/ppermute | solution.py:294
  9.7 4.4 %collective-permute-start.2 = (f32[18,8,128]{2,1,0:T(8,128)S(1)}, f32[18,8,128]{2,1,0:T(8,128)S(1)}, u32[]{:S(2)}, u32[]{:S(2)}) collective-permute-start(f32[18,8,128]{2,1,0:T(8,128)S(1)} %pad_maximum_fusion.1), channel_id=1, source_target_pairs={{0,8},{8,0},{16,24},{24,16},{1,9},{9,1},{17,25},{25,17},{2,10},{10... | collective-permute-start | bytes 221192 | tf_op jit(solution)/shard_map/ppermute | solution.py:294
  14.1 5.4 %collective-permute-start.3 = (f32[19,8,128]{2,1,0:T(8,128)S(1)}, f32[19,8,128]{2,1,0:T(8,128)S(1)}, u32[]{:S(2)}, u32[]{:S(2)}) collective-permute-start(f32[19,8,128]{2,1,0:T(8,128)S(1)} %pad_maximum_fusion), channel_id=1, source_target_pairs={{0,16},{8,24},{16,0},{24,8},{1,17},{9,25},{17,1},{25,9},{2,18},{10... | collective-permute-start | bytes 233480 | tf_op jit(solution)/shard_map/ppermute | solution.py:294
  19.5 4.6 %collective-permute-start.4 = (f32[1,21,8,128]{3,2,1,0:T(8,128)S(1)}, f32[1,21,8,128]{3,2,1,0:T(8,128)S(1)}, u32[]{:S(2)}, u32[]{:S(2)}) collective-permute-start(f32[1,21,8,128]{3,2,1,0:T(8,128)S(1)} %maximum_bitcast_fusion.near_ref), channel_id=1, source_target_pairs={{0,1},{1,0},{2,3},{3,2},{4,5},{5,4},{6,7},{7,6},{8,9},{9,8},{10,11... | collective-permute-start | bytes 258056 | tf_op jit(solution)/shard_map/ppermute | solution.py:294
  25.0 3.7 %collective-permute-start.5 = (f32[1,8,128]{2,1,0:T(8,128)S(1)}, f32[1,8,128]{2,1,0:T(8,128)S(1)}, u32[]{:S(2)}, u32[]{:S(2)}) collective-permute-start(f32[1,8,128]{2,1,0:T(8,128)S(1)} %get-tuple-element.13.mine_ref), channel_id=1, source_target_pairs={{0,4},{2,6},{4,0},{6,2},{1,5},{3,7},{5,1},{7,3},{8,12},{10,14},{12... | collective-permute-start | bytes 12296 | tf_op jit(solution)/shard_map/ppermute | solution.py:294
  28.7 1.2 %collective-permute-start.6 = (f32[2,8,128]{2,1,0:T(8,128)S(1)}, f32[2,8,128]{2,1,0:T(8,128)S(1)}, u32[]{:S(2)}, u32[]{:S(2)}) collective-permute-start(f32[2,8,128]{2,1,0:T(8,128)S(1)} %constant_dynamic-update-slice_fusion.near_ref), channel_id=1, source_target_pairs={{0,2},{2,0},{4,6},{6,4},{1,3},{3,1},{5,7},{7,5},{8,10},{10,8},{12,... | collective-permute-start | bytes 24584 | tf_op jit(solution)/shard_map/ppermute | solution.py:294

commit v8 on v7

--- a/solution.py
+++ b/solution.py
@@ -294,10 +294,10 @@
     return lax.ppermute(x, axis, [(i, i ^ bit) for i in range(lax.axis_size(axis))])
 
 
-def gathered(x, axis):
+def gathered(x, axis, crossed=0):
     near, offsets = x[None], [0]
     for bit in reversed(bits(lax.axis_size(axis))[1:]):
-        near = jnp.concatenate([near, swapped(near, axis, bit)], axis=0)
+        near = jnp.concatenate([near, swapped(near, axis, bit | crossed)], axis=0)
         offsets = offsets + [j + bit for j in offsets]
     return near, swapped(near, axis, 1), offsets
 
@@ -359,7 +359,7 @@
         compiler_params=pltpu.CompilerParams(vmem_limit_bytes=24 * 1024 * 1024),
     )(factors, near, far)
 
-    near, far, _ = gathered(sums[0], "lon")
+    near, far, _ = gathered(sums[0], "lon", 1)
     out = jax.ShapeDtypeStruct((1, variables, 1, rows, cols), jnp.float32)
     return pl.pallas_call(
         update_kernel,

time: 30.6 us -> 30.1 us (0.984)
  starting transfers between devices: 12.1 us -> 10.5 us
  waiting for transfers between devices: 14 us -> 15 us
    ppermute x7, starting transfers between devices: 12.1 us -> 10.5 us  [swapped(): lax.ppermute(x, axis, [(i, i ^ bit) for i in range(lax.axis_size(axis))])]
    ppermute x7, waiting for transfers between devices: 14 us -> 15 us  [swapped(): lax.ppermute(x, axis, [(i, i ^ bit) for i in range(lax.axis_size(axis))])]
where the time goes in v8:
time: 30.1 us; the launch traced here: 29.9 us
  waiting for transfers between devices  15 us (50%)
  starting transfers between devices  10.5 us (35%)
  Pallas kernels  3.57 us (12%)
  between operations  0.72 us (2%)
    ppermute x7, waiting for transfers between devices, swapped(): lax.ppermute(x, axis, [(i, i ^ bit) for i in range(lax.axis_size(axis))])  15 us
    ppermute x7, starting transfers between devices, swapped(): lax.ppermute(x, axis, [(i, i ^ bit) for i in range(lax.axis_size(axis))])  10.5 us
    pallas_call x1, Pallas kernels, per_device(): pl.pallas_call(tile_kernel, out_shape=(half, half, jax.ShapeDtypeStruct((...  2 us
    pallas_call x1, Pallas kernels, per_device(): pl.pallas_call(functools.partial(strip_kernel, offsets, lat_offsets), out...  0.92 us
    pallas_call x1, Pallas kernels, per_device(): pl.pallas_call(update_kernel, out_shape=(out, out), in_specs=[vmem] * 4,...  0.65 us
  transfers between devices with their start and end apart: 7, of which 7 were waited for; matrix products, arithmetic and copies ran while one was open for 0% of the time, Pallas kernels for 0%

profile of v8, /device:TPU:0, one launch (start us, length us, event | category | flops | bytes accessed | tf_op | source)
XLA Modules:
  0.0 29.9 jit_solution(14262393385488060729)
XLA Ops:
  0.6 2.0 %shard_map.113 = (f32[2,17,8,128]{3,2,1,0:T(8,128)S(1)}, f32[2,17,8,128]{3,2,1,0:T(8,128)S(1)}, f32[1,8,128]{2,1,0:T(8,128)S(1)}, f32[13,1,256]{2,1,0:T(1,128)S(1)}) custom-call(s32[64]{0:T(128)} %bitcast.7, s32[64]{0:T(128)} %refs_1_.1, f32[8]{0:T(128)} %refs_2_.1, f32[3,3]{1,0:T(4,128)} %refs_3_.1, f32[2,2]{1,0:T(2,128)} %refs_4_.1, ...), custom_call_target="tpu_custom_call" | custom-call | tf_op jit(solution)/shard_map/pallas_call | solution.py:316
  2.6 0.5 %collective-permute-start = (f32[2,17,8,128]{3,2,1,0:T(8,128)S(1)}, f32[2,17,8,128]{3,2,1,0:T(8,128)S(1)}, u32[]{:S(2)}, u32[]{:S(2)}) collective-permute-start(f32[2,17,8,128]{3,2,1,0:T(8,128)S(1)} %get-tuple-element.10), channel_id=1, source_target_pairs={{0,2},{2,0},{4,6},{6,4},{1,3},{3,1},{5,7},{7,5},{8,10},{10,8},{12,... | collective-permute-start | bytes 417800 | tf_op jit(solution)/shard_map/ppermute | solution.py:294
  3.2 1.0 %collective-permute-done = f32[2,17,8,128]{3,2,1,0:T(8,128)S(1)} collective-permute-done((f32[2,17,8,128]{3,2,1,0:T(8,128)S(1)}, f32[2,17,8,128]{3,2,1,0:T(8,128)S(1)}, u32[]{:S(2)}, u32[]{:S(2)}) %collective-permute-start) | collective-permute-done | bytes 139296 | tf_op jit(solution)/shard_map/ppermute | solution.py:294
  4.2 2.9 %collective-permute-start.1 = (f32[1,17,8,128]{3,2,1,0:T(8,128)S(1)}, f32[1,17,8,128]{3,2,1,0:T(8,128)S(1)}, u32[]{:S(2)}, u32[]{:S(2)}) collective-permute-start(f32[1,17,8,128]{3,2,1,0:T(8,128)S(1)} %slice.27), channel_id=1, source_target_pairs={{0,4},{2,6},{4,0},{6,2},{1,5},{3,7},{5,1},{7,3},{8,12},{10,14},{12... | collective-permute-start | bytes 208904 | tf_op jit(solution)/shard_map/ppermute | solution.py:294
  7.1 2.5 %collective-permute-done.1 = f32[1,17,8,128]{3,2,1,0:T(8,128)S(1)} collective-permute-done((f32[1,17,8,128]{3,2,1,0:T(8,128)S(1)}, f32[1,17,8,128]{3,2,1,0:T(8,128)S(1)}, u32[]{:S(2)}, u32[]{:S(2)}) %collective-permute-start.1) | collective-permute-done | bytes 69664 | tf_op jit(solution)/shard_map/ppermute | solution.py:294
  9.6 1.9 %collective-permute-start.2 = (f32[18,8,128]{2,1,0:T(8,128)S(1)}, f32[18,8,128]{2,1,0:T(8,128)S(1)}, u32[]{:S(2)}, u32[]{:S(2)}) collective-permute-start(f32[18,8,128]{2,1,0:T(8,128)S(1)} %pad_maximum_fusion.1), channel_id=1, source_target_pairs={{0,8},{8,0},{16,24},{24,16},{1,9},{9,1},{17,25},{25,17},{2,10},{10... | collective-permute-start | bytes 221192 | tf_op jit(solution)/shard_map/ppermute | solution.py:294
  11.6 2.5 %collective-permute-done.2 = f32[18,8,128]{2,1,0:T(8,128)S(1)} collective-permute-done((f32[18,8,128]{2,1,0:T(8,128)S(1)}, f32[18,8,128]{2,1,0:T(8,128)S(1)}, u32[]{:S(2)}, u32[]{:S(2)}) %collective-permute-start.2) | collective-permute-done | bytes 73760 | tf_op jit(solution)/shard_map/ppermute | solution.py:294
  14.1 3.0 %collective-permute-start.3 = (f32[19,8,128]{2,1,0:T(8,128)S(1)}, f32[19,8,128]{2,1,0:T(8,128)S(1)}, u32[]{:S(2)}, u32[]{:S(2)}) collective-permute-start(f32[19,8,128]{2,1,0:T(8,128)S(1)} %pad_maximum_fusion), channel_id=1, source_target_pairs={{0,16},{8,24},{16,0},{24,8},{1,17},{9,25},{17,1},{25,9},{2,18},{10... | collective-permute-start | bytes 233480 | tf_op jit(solution)/shard_map/ppermute | solution.py:294
  17.1 2.4 %collective-permute-done.3 = f32[19,8,128]{2,1,0:T(8,128)S(1)} collective-permute-done((f32[19,8,128]{2,1,0:T(8,128)S(1)}, f32[19,8,128]{2,1,0:T(8,128)S(1)}, u32[]{:S(2)}, u32[]{:S(2)}) %collective-permute-start.3) | collective-permute-done | bytes 77856 | tf_op jit(solution)/shard_map/ppermute | solution.py:294
  19.5 1.9 %collective-permute-start.4 = (f32[1,21,8,128]{3,2,1,0:T(8,128)S(1)}, f32[1,21,8,128]{3,2,1,0:T(8,128)S(1)}, u32[]{:S(2)}, u32[]{:S(2)}) collective-permute-start(f32[1,21,8,128]{3,2,1,0:T(8,128)S(1)} %maximum_bitcast_fusion.near_ref), channel_id=1, source_target_pairs={{0,1},{1,0},{2,3},{3,2},{4,5},{5,4},{6,7},{7,6},{8,9},{9,8},{10,11... | collective-permute-start | bytes 258056 | tf_op jit(solution)/shard_map/ppermute | solution.py:294
  21.4 2.7 %collective-permute-done.4.far_ref = f32[1,21,8,128]{3,2,1,0:T(8,128)S(1)} collective-permute-done((f32[1,21,8,128]{3,2,1,0:T(8,128)S(1)}, f32[1,21,8,128]{3,2,1,0:T(8,128)S(1)}, u32[]{:S(2)}, u32[]{:S(2)}) %collective-permute-start.4) | collective-permute-done | bytes 86048 | tf_op jit(solution)/shard_map/ppermute | solution.py:294
  24.1 0.9 %shard_map.114 = (f32[4,3,8,128]{3,2,1,0:T(8,128)S(1)}, f32[1,8,128]{2,1,0:T(8,128)S(1)}) custom-call(f32[13,1,256]{2,1,0:T(1,128)S(1)} %get-tuple-element.8.factors_ref, f32[1,21,8,128]{3,2,1,0:T(8,128)S(1)} %maximum_bitcast_fusion.near_ref, f32[1,21,8,128]{3,2,1,0:T(8,128)S(1)} %collective-permute-done.4.far_ref), custom_call_target="tpu_custom_call" | custom-call | tf_op jit(solution)/shard_map/pallas_call | solution.py:350
  25.0 0.1 collective-permute-start.5
  25.1 3.0 %collective-permute-done.5 = f32[1,8,128]{2,1,0:T(8,128)S(1)} collective-permute-done((f32[1,8,128]{2,1,0:T(8,128)S(1)}, f32[1,8,128]{2,1,0:T(8,128)S(1)}, u32[]{:S(2)}, u32[]{:S(2)}) %collective-permute-start.5) | collective-permute-done | bytes 4128 | tf_op jit(solution)/shard_map/ppermute | solution.py:294
  28.1 0.2 collective-permute-start.6
  28.3 1.0 %collective-permute-done.6.far_ref = f32[2,8,128]{2,1,0:T(8,128)S(1)} collective-permute-done((f32[2,8,128]{2,1,0:T(8,128)S(1)}, f32[2,8,128]{2,1,0:T(8,128)S(1)}, u32[]{:S(2)}, u32[]{:S(2)}) %collective-permute-start.6) | collective-permute-done | bytes 8224 | tf_op jit(solution)/shard_map/ppermute | solution.py:294
  29.3 0.6 %shard_map.115 = (f32[1,3,1,8,128]{4,3,2,1,0:T(8,128)}, f32[1,3,1,8,128]{4,3,2,1,0:T(8,128)}) custom-call(f32[4,3,8,128]{3,2,1,0:T(8,128)S(1)} %get-tuple-element.12.own_ref, f32[1,8,128]{2,1,0:T(8,128)S(1)} %get-tuple-element.13.mine_ref, f32[2,8,128]{2,1,0:T(8,128)S(1)} %constant_dynamic-update-slice_fusion.near_ref, ...), custom_call_target="tpu_custom_call" | custom-call | tf_op jit(solution)/shard_map/pallas_call | solution.py:364
  (12 shorter events, 0.1 us)
Async XLA Ops:
  2.6 1.5 %collective-permute-start = (f32[2,17,8,128]{3,2,1,0:T(8,128)S(1)}, f32[2,17,8,128]{3,2,1,0:T(8,128)S(1)}, u32[]{:S(2)}, u32[]{:S(2)}) collective-permute-start(f32[2,17,8,128]{3,2,1,0:T(8,128)S(1)} %get-tuple-element.10), channel_id=1, source_target_pairs={{0,2},{2,0},{4,6},{6,4},{1,3},{3,1},{5,7},{7,5},{8,10},{10,8},{12,... | collective-permute-start | bytes 417800 | tf_op jit(solution)/shard_map/ppermute | solution.py:294
  4.2 5.4 %collective-permute-start.1 = (f32[1,17,8,128]{3,2,1,0:T(8,128)S(1)}, f32[1,17,8,128]{3,2,1,0:T(8,128)S(1)}, u32[]{:S(2)}, u32[]{:S(2)}) collective-permute-start(f32[1,17,8,128]{3,2,1,0:T(8,128)S(1)} %slice.27), channel_id=1, source_target_pairs={{0,4},{2,6},{4,0},{6,2},{1,5},{3,7},{5,1},{7,3},{8,12},{10,14},{12... | collective-permute-start | bytes 208904 | tf_op jit(solution)/shard_map/ppermute | solution.py:294
  9.6 4.4 %collective-permute-start.2 = (f32[18,8,128]{2,1,0:T(8,128)S(1)}, f32[18,8,128]{2,1,0:T(8,128)S(1)}, u32[]{:S(2)}, u32[]{:S(2)}) collective-permute-start(f32[18,8,128]{2,1,0:T(8,128)S(1)} %pad_maximum_fusion.1), channel_id=1, source_target_pairs={{0,8},{8,0},{16,24},{24,16},{1,9},{9,1},{17,25},{25,17},{2,10},{10... | collective-permute-start | bytes 221192 | tf_op jit(solution)/shard_map/ppermute | solution.py:294
  14.1 5.4 %collective-permute-start.3 = (f32[19,8,128]{2,1,0:T(8,128)S(1)}, f32[19,8,128]{2,1,0:T(8,128)S(1)}, u32[]{:S(2)}, u32[]{:S(2)}) collective-permute-start(f32[19,8,128]{2,1,0:T(8,128)S(1)} %pad_maximum_fusion), channel_id=1, source_target_pairs={{0,16},{8,24},{16,0},{24,8},{1,17},{9,25},{17,1},{25,9},{2,18},{10... | collective-permute-start | bytes 233480 | tf_op jit(solution)/shard_map/ppermute | solution.py:294
  19.5 4.6 %collective-permute-start.4 = (f32[1,21,8,128]{3,2,1,0:T(8,128)S(1)}, f32[1,21,8,128]{3,2,1,0:T(8,128)S(1)}, u32[]{:S(2)}, u32[]{:S(2)}) collective-permute-start(f32[1,21,8,128]{3,2,1,0:T(8,128)S(1)} %maximum_bitcast_fusion.near_ref), channel_id=1, source_target_pairs={{0,1},{1,0},{2,3},{3,2},{4,5},{5,4},{6,7},{7,6},{8,9},{9,8},{10,11... | collective-permute-start | bytes 258056 | tf_op jit(solution)/shard_map/ppermute | solution.py:294
  25.0 3.1 %collective-permute-start.5 = (f32[1,8,128]{2,1,0:T(8,128)S(1)}, f32[1,8,128]{2,1,0:T(8,128)S(1)}, u32[]{:S(2)}, u32[]{:S(2)}) collective-permute-start(f32[1,8,128]{2,1,0:T(8,128)S(1)} %get-tuple-element.13.mine_ref), channel_id=1, source_target_pairs={{0,6},{2,4},{4,2},{6,0},{1,7},{3,5},{5,3},{7,1},{8,14},{10,12},{12... | collective-permute-start | bytes 12296 | tf_op jit(solution)/shard_map/ppermute | solution.py:294
  28.1 1.2 %collective-permute-start.6 = (f32[2,8,128]{2,1,0:T(8,128)S(1)}, f32[2,8,128]{2,1,0:T(8,128)S(1)}, u32[]{:S(2)}, u32[]{:S(2)}) collective-permute-start(f32[2,8,128]{2,1,0:T(8,128)S(1)} %constant_dynamic-update-slice_fusion.near_ref), channel_id=1, source_target_pairs={{0,2},{2,0},{4,6},{6,4},{1,3},{3,1},{5,7},{7,5},{8,10},{10,8},{12,... | collective-permute-start | bytes 24584 | tf_op jit(solution)/shard_map/ppermute | solution.py:294
